TPU v7x, 32 devices: a whole 2x2x4 slice. The times are simulated.
32 devices in a mesh: dp: 8 (over z, y), section: 4 (over x, core).
Axes of the slice: x: 2, y: 2, z: 4, core: 2. Of those that a mesh axis runs over, the one named last changes fastest.
Arguments:
- inputs: bfloat16 [8192, 768], P('dp'), may hold values from -8 to 8
- cotangent_first: bfloat16 [8192, 768], P('dp'), may hold values from -6 to 6
- cotangent_second: bfloat16 [8192, 768], P('dp'), may hold values from -6 to 6
- segment_ids: int32 [8192], P('dp'), may hold values from -1 to 5, as said below
- joint_projection: bfloat16 [1536, 2304], P('section'), may hold values from -0.21875 to 0.21875
- mixing_weight: bfloat16 [1536, 768], P('section'), may hold values from -0.875 to 0.875
- gated_weight: bfloat16 [1536, 6144], P('section'), may hold values from -0.21875 to 0.21875
- down_weight: bfloat16 [6144, 768], P('section'), may hold values from -0.109375 to 0.109375
- norm_gain: float32 [4, 768], P('section'), may hold values from 0.5 to 1.5
- norm_bias: float32 [4, 768], P('section'), may hold values from -1.75 to 1.75
Outputs:
- first_output: bfloat16 [8192, 768], P(('dp', 'section'))
- second_output: bfloat16 [8192, 768], P(('dp', 'section'))
- input_gradient: bfloat16 [8192, 768], P(('dp', 'section'))
- middle_gradient: bfloat16 [8192, 768], P(('dp', 'section'))
- joint_gradient: float32 [1536, 2304], P('section')
- mixing_gradient: float32 [1536, 768], P('section')
- gated_gradient: float32 [1536, 6144], P('section')
- down_gradient: float32 [6144, 768], P('section')
- gain_gradient: float32 [4, 768], P('section')
- bias_gradient: float32 [4, 768], P('section')
- magnitudes: float32 [2, 4], replicated
Inputs may be any that keep to these rules, and one draw needn't show every extreme that they name: `segment_ids`: within each aligned block of 128 positions the numbers start at 0 and rise by one at each new sequence; every sequence is 20 positions or longer; positions after a block's last sequence hold -1.
All inputs are finite; a program needn't handle non-finite values.
Results may differ from a plain program's by a relative error of at most 0.028.
The roundings to bfloat16 on the way count: a program that leaves them out, or rounds other values in their place, can miss the bound.
Values may be sent and summed in bfloat16 or wider, within the bound.
A program may use at most 256 MiB of HBM per device.

v0:
```python
import jax
import jax.numpy as jnp
from jax import lax
from jax.sharding import PartitionSpec as P

D = 768
HEADS = 12
FF = 3072
BLOCK = 128
MICRO = 8


EPSILON = 1e-05
MASKED = -1e30
ROOT_HALF = 0.7071067811865476
ROOT_TWO_PI = 2.5066282746310002


def shifted(value, axis, by):
    length = lax.axis_size(axis)
    pairs = [(i, i + by) for i in range(length) if 0 <= i + by < length]
    return lax.ppermute(value, axis, pairs)


def for_sending(value):
    return jax.tree.map(lambda a: a.astype(jnp.bfloat16) if a.dtype == jnp.float32 else a, value)


def alibi_slopes(heads_count):
    closest = 1 << heads_count.bit_length() - 1
    first_slope = 2.0 ** (-8.0 / closest)
    slopes = [first_slope ** (power_index + 1) for power_index in range(closest)]
    double_slope = 2.0 ** (-8.0 / (2 * closest))
    extra_slopes = [double_slope ** (power_index + 1) for power_index in range(2 * closest)]
    slopes = slopes + extra_slopes[0::2][: heads_count - closest]
    return jnp.array(slopes, jnp.float32)


def alibi_bias(heads_count):
    positions = jnp.arange(BLOCK)
    distance = jnp.abs(positions[:, None] - positions[None, :]).astype(jnp.float32)
    return -alibi_slopes(heads_count)[:, None, None] * distance


def post_norm(inputs, branch, gain_vector, bias_vector):
    summed_rows = inputs.astype(jnp.float32) + branch
    center = summed_rows - jnp.mean(summed_rows, axis=-1, keepdims=True)
    spread = jnp.mean(center * center, axis=-1, keepdims=True)
    inverse = lax.rsqrt(spread + EPSILON)
    scaled = center * inverse
    return (scaled * gain_vector + bias_vector, scaled, inverse)


def norm_back(upstream, scaled, inverse, gain_vector):
    scaled_grad = upstream * gain_vector
    gain_term = jnp.sum(upstream * scaled, axis=0)
    bias_term = jnp.sum(upstream, axis=0)
    through = inverse * (
        scaled_grad
        - jnp.mean(scaled_grad, axis=-1, keepdims=True)
        - scaled * jnp.mean(scaled_grad * scaled, axis=-1, keepdims=True)
    )
    return (through, gain_term, bias_term)


def attention_core(inputs, segments, joint_weight, score_scale):
    total_rows = inputs.shape[0]
    blocks = total_rows // BLOCK
    head_size = D // HEADS
    joint_rows = jnp.dot(inputs, joint_weight, preferred_element_type=jnp.float32).astype(
        jnp.bfloat16
    )
    split_heads = joint_rows.reshape(blocks, BLOCK, 3, HEADS, head_size)
    queries = split_heads[:, :, 0]
    keys_part = split_heads[:, :, 1]
    values_part = split_heads[:, :, 2]
    raw_scores = jnp.einsum(
        "bqhd,bkhd->bhqk", queries, keys_part, preferred_element_type=jnp.float32
    )
    scores = raw_scores * score_scale + alibi_bias(HEADS)[None]
    segment_rows = segments.reshape(blocks, BLOCK)
    same_segment = segment_rows[:, None, :, None] == segment_rows[:, None, None, :]
    masked_scores = jnp.where(same_segment, scores, MASKED)
    row_peak = jnp.max(masked_scores, axis=-1, keepdims=True)
    exponents = jnp.exp(masked_scores - row_peak)
    weights_soft = exponents / jnp.sum(exponents, axis=-1, keepdims=True)
    weights_low = weights_soft.astype(jnp.bfloat16)
    mixed_rows = jnp.einsum(
        "bhqk,bkhd->bqhd", weights_low, values_part, preferred_element_type=jnp.float32
    )
    mixed_rows = mixed_rows.reshape(total_rows, D).astype(jnp.bfloat16)
    return (queries, keys_part, values_part, weights_soft, weights_low, mixed_rows)


def attention_forward(
    inputs, segments, joint_weight, mixing_matrix, gain_vector, bias_vector, score_scale
):
    core_parts = attention_core(inputs, segments, joint_weight, score_scale)
    branch = jnp.dot(core_parts[5], mixing_matrix, preferred_element_type=jnp.float32)
    normed = post_norm(inputs, branch, gain_vector, bias_vector)[0]
    return (normed.astype(jnp.bfloat16), branch)


def attention_backward(
    inputs, segments, upstream, joint_weight, mixing_matrix, gain_vector, bias_vector, score_scale
):
    total_rows = inputs.shape[0]
    blocks = total_rows // BLOCK
    head_size = D // HEADS
    queries, keys_part, values_part, weights_soft, weights_low, mixed_rows = attention_core(
        inputs, segments, joint_weight, score_scale
    )
    branch = jnp.dot(mixed_rows, mixing_matrix, preferred_element_type=jnp.float32)
    normed, scaled, inverse = post_norm(inputs, branch, gain_vector, bias_vector)
    through, gain_term, bias_term = norm_back(upstream, scaled, inverse, gain_vector)
    branch_low = through.astype(jnp.bfloat16)
    mixing_term = jnp.einsum(
        "nd,ne->de", mixed_rows, branch_low, preferred_element_type=jnp.float32
    )
    mixed_grad = jnp.einsum(
        "ne,de->nd", branch_low, mixing_matrix, preferred_element_type=jnp.float32
    )
    mixed_grad = mixed_grad.astype(jnp.bfloat16).reshape(blocks, BLOCK, HEADS, head_size)
    weights_grad = jnp.einsum(
        "bqhd,bkhd->bhqk", mixed_grad, values_part, preferred_element_type=jnp.float32
    )
    values_grad = jnp.einsum(
        "bhqk,bqhd->bkhd", weights_low, mixed_grad, preferred_element_type=jnp.float32
    )
    score_grad = weights_soft * (
        weights_grad - jnp.sum(weights_grad * weights_soft, axis=-1, keepdims=True)
    )
    score_low = score_grad.astype(jnp.bfloat16)
    queries_grad = (
        jnp.einsum("bhqk,bkhd->bqhd", score_low, keys_part, preferred_element_type=jnp.float32)
        * score_scale
    )
    keys_grad = (
        jnp.einsum("bhqk,bqhd->bkhd", score_low, queries, preferred_element_type=jnp.float32)
        * score_scale
    )
    joint_grad = jnp.stack([queries_grad, keys_grad, values_grad], axis=2)
    joint_grad = joint_grad.reshape(total_rows, 3 * D).astype(jnp.bfloat16)
    joint_term = jnp.einsum("nd,ne->de", inputs, joint_grad, preferred_element_type=jnp.float32)
    inputs_grad = through + jnp.einsum(
        "ne,de->nd", joint_grad, joint_weight, preferred_element_type=jnp.float32
    )
    return (inputs_grad, joint_term, mixing_term, gain_term, bias_term)


def feedforward_core(inputs, gated_matrix):
    gate_up = jnp.dot(inputs, gated_matrix, preferred_element_type=jnp.float32)
    gate_part = gate_up[:, :FF]
    up_part = gate_up[:, FF:]
    activated = jax.nn.gelu(gate_part, approximate=False)
    hidden = (activated * up_part).astype(jnp.bfloat16)
    return (gate_part, up_part, activated, hidden)


def feedforward_forward(inputs, gated_matrix, down_matrix, gain_vector, bias_vector):
    hidden = feedforward_core(inputs, gated_matrix)[3]
    branch = jnp.dot(hidden, down_matrix, preferred_element_type=jnp.float32)
    normed = post_norm(inputs, branch, gain_vector, bias_vector)[0]
    return (normed.astype(jnp.bfloat16), branch)


def feedforward_backward(inputs, upstream, gated_matrix, down_matrix, gain_vector, bias_vector):
    gate_part, up_part, activated, hidden = feedforward_core(inputs, gated_matrix)
    branch = jnp.dot(hidden, down_matrix, preferred_element_type=jnp.float32)
    normed, scaled, inverse = post_norm(inputs, branch, gain_vector, bias_vector)
    through, gain_term, bias_term = norm_back(upstream, scaled, inverse, gain_vector)
    branch_low = through.astype(jnp.bfloat16)
    down_term = jnp.einsum("nf,nd->fd", hidden, branch_low, preferred_element_type=jnp.float32)
    hidden_grad = jnp.einsum(
        "nd,fd->nf", branch_low, down_matrix, preferred_element_type=jnp.float32
    )
    normal_cdf = 0.5 * (1.0 + lax.erf(gate_part * ROOT_HALF))
    density = jnp.exp(-0.5 * gate_part * gate_part) / ROOT_TWO_PI
    gate_grad = hidden_grad * up_part * (normal_cdf + gate_part * density)
    up_grad = hidden_grad * activated
    both_grad = jnp.concatenate([gate_grad, up_grad], axis=-1).astype(jnp.bfloat16)
    gated_term = jnp.einsum("nd,nf->df", inputs, both_grad, preferred_element_type=jnp.float32)
    inputs_grad = through + jnp.einsum(
        "nf,df->nd", both_grad, gated_matrix, preferred_element_type=jnp.float32
    )
    return (inputs_grad, gated_term, down_term, gain_term, bias_term)


def keep_slot(buffer, new_value, slot_index, active):
    previous = lax.dynamic_index_in_dim(buffer, slot_index, 0, keepdims=False)
    chosen = jnp.where(active, new_value, previous)
    return lax.dynamic_update_index_in_dim(buffer, chosen, slot_index, 0)


def per_device(
    inputs,
    cotangent_first,
    cotangent_second,
    segment_ids,
    joint_projection,
    mixing_weight,
    gated_weight,
    down_weight,
    norm_gain,
    norm_bias,
):
    section_count = lax.axis_size("section")
    section_index = lax.axis_index("section")
    attend_section = section_index % 2 == 0
    token_rows = inputs.shape[0]
    micro_rows = token_rows // MICRO
    half_width = D // 2
    half_hidden = FF // 2
    score_scale = (D // HEADS) ** (-0.5)
    attention_other = shifted((joint_projection, mixing_weight), "section", -1)
    joint_full = jnp.concatenate([joint_projection, attention_other[0]], axis=0)
    mixing_full = jnp.concatenate([mixing_weight, attention_other[1]], axis=0)
    feedforward_other = shifted((gated_weight, down_weight), "section", 1)
    gated_full = jnp.concatenate([feedforward_other[0], gated_weight], axis=0)
    down_full = jnp.concatenate([feedforward_other[1], down_weight], axis=0)
    gain_vector = norm_gain[0]
    bias_vector = norm_bias[0]

    def run_attention(rows_in, segments):
        return attention_forward(
            rows_in, segments, joint_full, mixing_full, gain_vector, bias_vector, score_scale
        )

    def run_feedforward(rows_in, segments):
        return feedforward_forward(rows_in, gated_full, down_full, gain_vector, bias_vector)

    def run_nothing(rows_in, segments):
        return (rows_in, jnp.zeros(rows_in.shape, jnp.float32))

    def back_attention(rows_in, segments, upstream, accumulated):
        inputs_grad, joint_term, mixing_term, gain_term, bias_term = attention_backward(
            rows_in,
            segments,
            upstream,
            joint_full,
            mixing_full,
            gain_vector,
            bias_vector,
            score_scale,
        )
        return (
            inputs_grad,
            (
                accumulated[0] + joint_term,
                accumulated[1] + mixing_term,
                accumulated[2],
                accumulated[3],
                accumulated[4] + gain_term,
                accumulated[5] + bias_term,
            ),
        )

    def back_feedforward(rows_in, segments, upstream, accumulated):
        inputs_grad, gated_term, down_term, gain_term, bias_term = feedforward_backward(
            rows_in, upstream, gated_full, down_full, gain_vector, bias_vector
        )
        return (
            inputs_grad,
            (
                accumulated[0],
                accumulated[1],
                accumulated[2] + gated_term,
                accumulated[3] + down_term,
                accumulated[4] + gain_term,
                accumulated[5] + bias_term,
            ),
        )

    def back_nothing(rows_in, segments, upstream, accumulated):
        return (jnp.zeros_like(upstream), accumulated)

    input_blocks = inputs.reshape(MICRO, micro_rows, D)
    segment_blocks = segment_ids.reshape(MICRO, micro_rows)
    first_cot = cotangent_first.reshape(MICRO, micro_rows, D)
    second_cot = cotangent_second.reshape(MICRO, micro_rows, D)
    kept_inputs = jnp.zeros((MICRO, micro_rows, D), jnp.bfloat16)
    kept_outputs = jnp.zeros((MICRO, micro_rows, D), jnp.bfloat16)
    kept_back = jnp.zeros((MICRO, micro_rows, D), jnp.bfloat16)
    incoming = jnp.zeros((micro_rows, D), jnp.bfloat16)
    residual_square = jnp.zeros((), jnp.float32)
    branch_square = jnp.zeros((), jnp.float32)
    tick_count = MICRO + section_count - 1
    for step_index in range(tick_count):
        micro_index = step_index - section_index
        active = (micro_index >= 0) & (micro_index < MICRO)
        safe_index = jnp.clip(micro_index, 0, MICRO - 1)
        fresh_rows = lax.dynamic_index_in_dim(input_blocks, safe_index, 0, keepdims=False)
        rows_in = jnp.where(section_index == 0, fresh_rows, incoming)
        segments = lax.dynamic_index_in_dim(segment_blocks, safe_index, 0, keepdims=False)
        selector = jnp.where(active, jnp.where(attend_section, 0, 1), 2)
        rows_out, branch = lax.switch(
            selector, [run_attention, run_feedforward, run_nothing], rows_in, segments
        )
        valid_rows = (segments >= 0).astype(jnp.float32)
        active_weight = active.astype(jnp.float32)
        rows_float = rows_in.astype(jnp.float32)
        residual_square = residual_square + active_weight * jnp.sum(
            valid_rows * jnp.sum(rows_float * rows_float, axis=-1)
        )
        branch_square = branch_square + active_weight * jnp.sum(
            valid_rows * jnp.sum(branch * branch, axis=-1)
        )
        kept_inputs = keep_slot(kept_inputs, rows_in, safe_index, active)
        kept_outputs = keep_slot(kept_outputs, rows_out, safe_index, active)
        if step_index + 1 < tick_count:
            incoming = jax.tree.map(
                lambda part, own: part.astype(own.dtype),
                shifted(for_sending(rows_out), "section", 1),
                rows_out,
            )
    accumulated = (
        jnp.zeros((D, 3 * D), jnp.float32),
        jnp.zeros((D, D), jnp.float32),
        jnp.zeros((D, 2 * FF), jnp.float32),
        jnp.zeros((FF, D), jnp.float32),
        jnp.zeros((D,), jnp.float32),
        jnp.zeros((D,), jnp.float32),
    )
    incoming_grad = jnp.zeros((micro_rows, D), jnp.bfloat16)
    for step_index in range(tick_count):
        micro_index = step_index - (section_count - 1 - section_index)
        active = (micro_index >= 0) & (micro_index < MICRO)
        safe_index = jnp.clip(micro_index, 0, MICRO - 1)
        segments = lax.dynamic_index_in_dim(segment_blocks, safe_index, 0, keepdims=False)
        valid_column = (segments >= 0).astype(jnp.float32)[:, None]
        final_grad = valid_column * lax.dynamic_index_in_dim(
            second_cot, safe_index, 0, keepdims=False
        ).astype(jnp.float32)
        upstream = jnp.where(
            section_index == section_count - 1, final_grad, incoming_grad.astype(jnp.float32)
        )
        rows_in = lax.dynamic_index_in_dim(kept_inputs, safe_index, 0, keepdims=False)
        selector = jnp.where(active, jnp.where(attend_section, 0, 1), 2)
        inputs_grad, accumulated = lax.switch(
            selector,
            [back_attention, back_feedforward, back_nothing],
            rows_in,
            segments,
            upstream,
            accumulated,
        )
        middle_add = valid_column * lax.dynamic_index_in_dim(
            first_cot, safe_index, 0, keepdims=False
        ).astype(jnp.float32)
        inputs_grad = inputs_grad + jnp.where(section_index == 2, middle_add, 0.0)
        sent_rows = inputs_grad.astype(jnp.bfloat16)
        kept_back = keep_slot(kept_back, sent_rows, safe_index, active)
        if step_index + 1 < tick_count:
            incoming_grad = shifted(sent_rows, "section", -1)
    attention_recv = shifted(
        (for_sending(accumulated[0][half_width:]), for_sending(accumulated[1][half_width:])),
        "section",
        1,
    )
    feedforward_recv = shifted(
        (for_sending(accumulated[2][:half_width]), for_sending(accumulated[3][:half_hidden])),
        "section",
        -1,
    )
    joint_mine = jnp.where(attend_section, accumulated[0][:half_width], attention_recv[0])
    mixing_mine = jnp.where(attend_section, accumulated[1][:half_width], attention_recv[1])
    gated_mine = jnp.where(attend_section, feedforward_recv[0], accumulated[2][half_width:])
    down_mine = jnp.where(attend_section, feedforward_recv[1], accumulated[3][half_hidden:])
    summed = lax.psum(
        (joint_mine, mixing_mine, gated_mine, down_mine, accumulated[4], accumulated[5]), "dp"
    )
    joint_sum, mixing_sum, gated_sum, down_sum, gain_sum, bias_sum = summed
    column = (jnp.arange(section_count) == section_index).astype(jnp.float32)
    stat_terms = jnp.stack([residual_square * column, branch_square * column])
    count_term = jnp.where(section_index == 0, jnp.sum((segment_ids >= 0).astype(jnp.float32)), 0.0)
    stat_total, count_total = lax.psum((stat_terms, count_term), ("dp", "section"))
    magnitudes = jnp.sqrt(stat_total / (count_total * D))
    result_rows = jnp.where(attend_section, kept_back, kept_outputs).reshape(1, token_rows, D)
    spread_rows = lax.all_to_all(result_rows, "section", split_axis=1, concat_axis=0, tiled=True)
    return (
        spread_rows[1],
        spread_rows[3],
        spread_rows[0],
        spread_rows[2],
        joint_sum,
        mixing_sum,
        gated_sum,
        down_sum,
        gain_sum[None],
        bias_sum[None],
        magnitudes,
    )


def solution(mesh):
    return jax.shard_map(
        per_device,
        mesh=mesh,
        in_specs=(
            P("dp", None),
            P("dp", None),
            P("dp", None),
            P("dp"),
            P("section", None),
            P("section", None),
            P("section", None),
            P("section", None),
            P("section", None),
            P("section", None),
        ),
        out_specs=(
            P(("dp", "section"), None),
            P(("dp", "section"), None),
            P(("dp", "section"), None),
            P(("dp", "section"), None),
            P("section", None),
            P("section", None),
            P("section", None),
            P("section", None),
            P("section", None),
            P("section", None),
            P(),
        ),
        check_vma=False,
    )
```

profile of v0, /device:TPU:0, one launch (start us, length us, event | category | flops | bytes accessed | tf_op | source)
XLA Modules:
  0.0 1721.5 jit_solution(14382277573970118183)
XLA Ops:
  40.3 16.4 conditional.22
  56.6 46.8 %collective-permute-start.4 = (bf16[128,768]{1,0:T(8,128)(2,1)S(1)}, bf16[128,768]{1,0:T(8,128)(2,1)S(1)}, u32[]{:S(2)}, u32[]{:S(2)}) collective-permute-start(bf16[128,768]{1,0:T(8,128)(2,1)S(1)} %get-tuple-element.1475), channel_id=1, source_target_pairs={{0,1},{1,2},{2,3},{4,5},{5,6},{6,7},{8,9},{9,10},{10,11},{12,13},{... | collective-permute-start | bytes 589832 | tf_op jit(solution)/shard_map/ppermute | solution.py:22
  107.5 16.6 conditional.23
  131.6 24.8 %conditional.24 = (bf16[128,768]{1,0:T(8,128)(2,1)S(1)}, f32[128]{0:T(128)}) conditional(s32[]{:T(128)} %clamp.69, (bf16[128,768]{1,0:T(8,128)(2,1)S(1)}, bf16[768,2304]{1,0:T(8,128)(2,1)S(1)}, s32[128]{0:T(128)}, f32[12]{0:T(128)S(1)}, bf16[768,768]{1,0:T(8,128)(2,1)}, /*index=5*/f32[1,768]{1,0:T(1,128)S(1)}, ...), branch_computations={%region_22.28_spmd, %region_28.32_spmd, %region_32.33_spmd} | conditional | flops 1839562752 | bytes 44655780 | solution.py:296
  163.6 16.4 conditional.25
  187.1 24.9 %conditional.26 = (bf16[128,768]{1,0:T(8,128)(2,1)S(1)}, f32[128]{0:T(128)}) conditional(s32[]{:T(128)} %clamp.71, (bf16[128,768]{1,0:T(8,128)(2,1)S(1)}, bf16[768,2304]{1,0:T(8,128)(2,1)S(1)}, s32[128]{0:T(128)}, f32[12]{0:T(128)S(1)}, bf16[768,768]{1,0:T(8,128)(2,1)}, /*index=5*/f32[1,768]{1,0:T(1,128)S(1)}, ...), branch_computations={%region_44.50_spmd, %region_50.54_spmd, %region_54.55_spmd} | conditional | flops 1839562752 | bytes 44655780 | solution.py:296
  219.1 16.4 conditional.27
  246.5 25.0 %conditional.28 = (bf16[128,768]{1,0:T(8,128)(2,1)S(1)}, f32[128]{0:T(128)}) conditional(s32[]{:T(128)} %clamp.73, (bf16[128,768]{1,0:T(8,128)(2,1)S(1)}, bf16[768,2304]{1,0:T(8,128)(2,1)S(1)}, s32[128]{0:T(128)}, f32[12]{0:T(128)S(1)}, bf16[768,768]{1,0:T(8,128)(2,1)}, /*index=5*/f32[1,768]{1,0:T(1,128)S(1)}, ...), branch_computations={%region_66.72_spmd, %region_72.76_spmd, %region_76.77_spmd} | conditional | flops 1839562752 | bytes 44655780 | solution.py:296
  278.7 16.4 conditional.29
  314.2 13.4 collective-permute-start.12
  333.8 13.9 collective-permute-start.13
  356.4 18.2 %conditional.32 = (f32[128,768]{1,0:T(8,128)}, f32[768,2304]{1,0:T(8,128)}, f32[768,768]{1,0:T(8,128)}, f32[768,6144]{0,1:T(8,128)}, f32[3072,768]{1,0:T(8,128)}, /*index=5*/f32[768]{0:T(1024)S(1)}, f32[768]{0:T(1024)S(1)}) conditional(s32[]{:T(128)} %clamp.66, (bf16[128,768]{1,0:T(8,128)(2,1)}, ...), branch_computations={%region_110.0_spmd, %region_120.127_spmd, %region_127.128_spmd} | conditional | flops 5475629568 | bytes 140209888 | solution.py:339
  380.6 17.8 %collective-permute-done.14 = bf16[128,768]{1,0:T(8,128)(2,1)} collective-permute-done((bf16[128,768]{1,0:T(8,128)(2,1)}, bf16[128,768]{1,0:T(8,128)(2,1)}, u32[]{:S(2)}, u32[]{:S(2)}) %collective-permute-start.14) | collective-permute-done | bytes 196640 | tf_op jit(solution)/shard_map/ppermute | solution.py:22
  410.9 19.3 %collective-permute-done.15 = bf16[128,768]{1,0:T(8,128)(2,1)} collective-permute-done((bf16[128,768]{1,0:T(8,128)(2,1)}, bf16[128,768]{1,0:T(8,128)(2,1)}, u32[]{:S(2)}, u32[]{:S(2)}) %collective-permute-start.15) | collective-permute-done | bytes 196640 | tf_op jit(solution)/shard_map/ppermute | solution.py:22
  443.0 83.8 %collective-permute-done.16 = bf16[128,768]{1,0:T(8,128)(2,1)} collective-permute-done((bf16[128,768]{1,0:T(8,128)(2,1)}, bf16[128,768]{1,0:T(8,128)(2,1)}, u32[]{:S(2)}, u32[]{:S(2)}) %collective-permute-start.16) | collective-permute-done | bytes 196640 | tf_op jit(solution)/shard_map/ppermute | solution.py:22
  528.6 54.9 %conditional.35 = (f32[128,768]{1,0:T(8,128)}, f32[768,2304]{1,0:T(8,128)}, f32[768,768]{1,0:T(8,128)}, f32[768,6144]{0,1:T(8,128)}, f32[3072,768]{1,0:T(8,128)}, /*index=5*/f32[768]{0:T(1024)S(1)}, f32[768]{0:T(1024)S(1)}) conditional(s32[]{:T(128)} %clamp.79, (bf16[128,768]{1,0:T(8,128)(2,1)}, ...), branch_computations={%region_164.174_spmd, %region_174.181_spmd, %region_181.182_spmd} | conditional | flops 5482708992 | bytes 159102688 | solution.py:339
  554.8 8.0 copy.512
  570.0 8.0 copy.458
  592.8 55.0 %conditional.36 = (f32[128,768]{1,0:T(8,128)}, f32[768,2304]{1,0:T(8,128)}, f32[768,768]{1,0:T(8,128)}, f32[768,6144]{0,1:T(8,128)}, f32[3072,768]{1,0:T(8,128)}, /*index=5*/f32[768]{0:T(1024)S(1)}, f32[768]{0:T(1024)S(1)}) conditional(s32[]{:T(128)} %clamp.80, (bf16[128,768]{1,0:T(8,128)(2,1)}, ...), branch_computations={%region_182.192_spmd, %region_192.199_spmd, %region_199.200_spmd} | conditional | flops 5482708992 | bytes 159102688 | solution.py:339
  618.7 8.0 copy.513
  634.0 8.0 copy.465
  657.4 54.8 %conditional.37 = (f32[128,768]{1,0:T(8,128)}, f32[768,2304]{1,0:T(8,128)}, f32[768,768]{1,0:T(8,128)}, f32[768,6144]{0,1:T(8,128)}, f32[3072,768]{1,0:T(8,128)}, /*index=5*/f32[768]{0:T(1024)S(1)}, f32[768]{0:T(1024)S(1)}) conditional(s32[]{:T(128)} %clamp.81, (bf16[128,768]{1,0:T(8,128)(2,1)}, ...), branch_computations={%region_200.210_spmd, %region_210.217_spmd, %region_217.218_spmd} | conditional | flops 5482708992 | bytes 159102688 | solution.py:339
  683.4 8.0 copy.514
  698.7 8.0 copy.472
  721.4 55.2 %conditional.38 = (f32[128,768]{1,0:T(8,128)}, f32[768,2304]{1,0:T(8,128)}, f32[768,768]{1,0:T(8,128)}, f32[768,6144]{0,1:T(8,128)}, f32[3072,768]{1,0:T(8,128)}, /*index=5*/f32[768]{0:T(1024)S(1)}, f32[768]{0:T(1024)S(1)}) conditional(s32[]{:T(128)} %clamp.82, (bf16[128,768]{1,0:T(8,128)(2,1)}, ...), branch_computations={%region_218.228_spmd, %region_228.235_spmd, %region_235.236_spmd} | conditional | flops 5482708992 | bytes 159102688 | solution.py:339
  747.5 8.0 copy.515
  762.8 8.0 copy.479
  785.9 56.2 %conditional.39 = (f32[128,768]{1,0:T(8,128)}, f32[768,2304]{1,0:T(8,128)}, f32[768,768]{1,0:T(8,128)}, f32[768,6144]{0,1:T(8,128)}, f32[3072,768]{1,0:T(8,128)}, /*index=5*/f32[768]{0:T(1024)}, f32[768]{0:T(1024)S(1)}) conditional(s32[]{:T(128)} %clamp.83, (bf16[128,768]{1,0:T(8,128)(2,1)}, ...), branch_computations={%region_236.246_spmd, %region_246.253_spmd, %region_253.254_spmd} | conditional | flops 5482708992 | bytes 159115008 | solution.py:339
  813.3 8.0 copy.516
  828.6 8.0 copy.486
  851.3 55.7 %conditional.40 = (f32[128,768]{1,0:T(8,128)}, f32[768,2304]{1,0:T(8,128)}, f32[768,768]{1,0:T(8,128)}, f32[768,6144]{0,1:T(8,128)}, f32[3072,768]{1,0:T(8,128)}, /*index=5*/f32[768]{0:T(1024)}, f32[768]{0:T(1024)S(1)}) conditional(s32[]{:T(128)} %clamp.84, (bf16[128,768]{1,0:T(8,128)(2,1)}, ...), branch_computations={%region_254.264_spmd, %region_264.271_spmd, %region_271.272_spmd} | conditional | flops 5482708992 | bytes 159102688 | solution.py:339
  878.0 8.0 copy.517
  893.3 8.0 copy.493
  917.2 55.4 %conditional.41 = (f32[128,768]{1,0:T(8,128)}, f32[768,2304]{1,0:T(8,128)}, f32[768,768]{1,0:T(8,128)}, f32[768,6144]{0,1:T(8,128)}, f32[3072,768]{1,0:T(8,128)}, /*index=5*/f32[768]{0:T(1024)}, f32[768]{0:T(1024)S(1)}) conditional(s32[]{:T(128)} %clamp.85, (bf16[128,768]{1,0:T(8,128)(2,1)}, ...), branch_computations={%region_272.282_spmd, %region_282.289_spmd, %region_289.290_spmd} | conditional | flops 5482708992 | bytes 173258496 | solution.py:339
  959.1 8.0 copy.500
  976.0 13.7 collective-permute-done.23
  991.6 55.8 %conditional.42 = (f32[128,768]{1,0:T(8,128)}, f32[768,2304]{1,0:T(8,128)}, f32[768,768]{1,0:T(8,128)}, f32[768,6144]{0,1:T(8,128)}, f32[3072,768]{1,0:T(8,128)}, /*index=5*/f32[768]{0:T(1024)}, f32[768]{0:T(1024)S(1)}) conditional(s32[]{:T(128)} %clamp.86, (bf16[128,768]{1,0:T(8,128)(2,1)}, ...), branch_computations={%region_290.300_spmd, %region_300.307_spmd, %region_307.308_spmd} | conditional | flops 5482708992 | bytes 159102688 | solution.py:339
  1017.6 8.0 copy.519
  1032.8 8.0 copy.507
  1047.4 18.7 %copy.524 = f32[768,6144]{1,0:T(8,128)} copy(f32[768,6144]{0,1:T(8,128)} %get-tuple-element.1559) | data formatting | bytes 37748736 | tf_op jit(solution)/shard_map/cond | solution.py:339
  1097.2 9.3 slice_select_fusion
  1143.0 8.8 conditional.43
  1160.9 11.7 reduce.176
  1176.4 19.5 %all-to-all-start = ((bf16[4,2,98304]{2,1,0:T(2,128)(2,1)}), bf16[4,2,98304]{2,1,0:T(2,128)(2,1)}, u32[]{:S(2)}, u32[]{:S(2)}) async-start(bf16[4,2,98304]{2,1,0:T(2,128)(2,1)} %reshape.3513), calls=%async_computation | async-start | bytes 3145728 | tf_op jit(solution)/shard_map/all_to_all | solution.py:379
  1213.9 46.9 %all-reduce = (f32[2,4]{1,0:T(2,128)S(1)}, f32[]{:T(128)}) all-reduce(f32[2,4]{1,0:T(2,128)S(1)} %pad_maximum_fusion.44, f32[]{:T(128)S(6)} %select_n.835), channel_id=1, replica_groups=mesh['dp'=8,'section'=4] {'dp','section'}, use_global_device_ids=true, to_apply=%region_358.359 | all-reduce | flops 9 | bytes 72 | tf_op jit(solution)/shard_map/psum | solution.py:376
  1262.7 22.0 %all-reduce.1 = (f32[1,768]{1,0:T(1,128)}, f32[1,768]{1,0:T(1,128)}) all-reduce(f32[1,768]{1,0:T(1,128)S(1)} %broadcast_in_dim.660, f32[1,768]{1,0:T(1,128)S(1)} %broadcast_in_dim.661), channel_id=1, replica_groups=mesh['dp'=8,'section'=4] {'dp'}, use_global_device_ids=true, to_apply=%region_323.324 | all-reduce | flops 1536 | bytes 12288 | tf_op jit(solution)/shard_map/psum | solution.py:369
  1293.1 404.6 %all-reduce.5.cloned.1.call-done = (f32[384,2304]{1,0:T(8,128)}, f32[384,768]{1,0:T(8,128)}, f32[384,6144]{1,0:T(8,128)}, f32[1536,768]{1,0:T(8,128)}) async-done(((f32[384,2304]{1,0:T(8,128)}, f32[384,768]{1,0:T(8,128)}, f32[384,6144]{1,0:T(8,128)}, f32[1536,768]{1,0:T(8,128)}), (f32[384,2304]{1,0:T(8,128)}, f32[384,768]{1,0:T(8,128)}, f32[384,6144]{1,0:T(8,128)}, ...) | async-done | bytes 18874384 | tf_op jit(solution)/shard_map/psum | solution.py:369
  1702.8 9.2 copy.931
  (931 shorter events, 739.6 us)
Async XLA Ops:
  7.2 1690.5 %all-reduce.5.cloned.1.call-start = ((), (), s32[]{:S(2)}) async-start(), calls=%async_computation.1 | async-start | bytes 37748736 | tf_op jit(solution)/shard_map/psum | solution.py:369
  7.2 25.5 %collective-permute-start.2 = (bf16[384,6144]{1,0:T(8,128)(2,1)}, bf16[384,6144]{1,0:T(8,128)(2,1)}, u32[]{:S(2)}, u32[]{:S(2)}) collective-permute-start(bf16[384,6144]{1,0:T(8,128)(2,1)} %param.84), channel_id=1, source_target_pairs={{0,1},{1,2},{2,3},{4,5},{5,6},{6,7},{8,9},{9,10},{10,11},{12,13},{... | collective-permute-start | bytes 14155784 | tf_op jit(solution)/shard_map/ppermute | solution.py:22
  11.9 15.9 collective-permute-start.3
  15.7 10.0 collective-permute-start
  17.0 7.6 collective-permute-start.1
  56.6 50.9 %copy-start.194 = (bf16[128,768]{1,0:T(8,128)(2,1)}, bf16[128,768]{1,0:T(8,128)(2,1)S(1)}, u32[]{:S(2)}) copy-start(bf16[128,768]{1,0:T(8,128)(2,1)S(1)} %get-tuple-element.1475) | copy-start | bytes 589828
  56.6 48.6 %collective-permute-start.4 = (bf16[128,768]{1,0:T(8,128)(2,1)S(1)}, bf16[128,768]{1,0:T(8,128)(2,1)S(1)}, u32[]{:S(2)}, u32[]{:S(2)}) collective-permute-start(bf16[128,768]{1,0:T(8,128)(2,1)S(1)} %get-tuple-element.1475), channel_id=1, source_target_pairs={{0,1},{1,2},{2,3},{4,5},{5,6},{6,7},{8,9},{9,10},{10,11},{12,13},{... | collective-permute-start | bytes 589832 | tf_op jit(solution)/shard_map/ppermute | solution.py:22
  124.1 5.1 collective-permute-start.5
  156.4 4.8 collective-permute-start.6
  180.0 4.8 collective-permute-start.7
  212.0 4.8 collective-permute-start.8
  235.5 8.7 collective-permute-start.9
  271.6 4.8 collective-permute-start.10
  295.2 9.4 collective-permute-start.11
  314.2 16.7 collective-permute-start.12
  333.8 16.5 collective-permute-start.13
  374.6 23.8 %copy-start.271 = (f32[128]{0:T(128)S(1)}, f32[128]{0:T(128)}, u32[]{:S(2)}) copy-start(f32[128]{0:T(128)} %get-tuple-element.2889) | copy-start | bytes 1540
  377.7 20.7 %collective-permute-start.14 = (bf16[128,768]{1,0:T(8,128)(2,1)}, bf16[128,768]{1,0:T(8,128)(2,1)}, u32[]{:S(2)}, u32[]{:S(2)}) collective-permute-start(bf16[128,768]{1,0:T(8,128)(2,1)} %get-tuple-element.2647), channel_id=1, source_target_pairs={{1,0},{2,1},{3,2},{5,4},{6,5},{7,6},{9,8},{10,9},{11,10},{13,12},{... | collective-permute-start | bytes 589832 | tf_op jit(solution)/shard_map/ppermute | solution.py:22
  405.9 24.3 %copy-start.270 = (f32[128]{0:T(128)S(1)}, f32[128]{0:T(128)}, u32[]{:S(2)}) copy-start(f32[128]{0:T(128)} %get-tuple-element.2887) | copy-start | bytes 1540
  407.9 22.2 %collective-permute-start.15 = (bf16[128,768]{1,0:T(8,128)(2,1)}, bf16[128,768]{1,0:T(8,128)(2,1)}, u32[]{:S(2)}, u32[]{:S(2)}) collective-permute-start(bf16[128,768]{1,0:T(8,128)(2,1)} %get-tuple-element.2643), channel_id=1, source_target_pairs={{1,0},{2,1},{3,2},{5,4},{6,5},{7,6},{9,8},{10,9},{11,10},{13,12},{... | collective-permute-start | bytes 589832 | tf_op jit(solution)/shard_map/ppermute | solution.py:22
  438.0 88.7 %copy-start.269 = (f32[128]{0:T(128)S(1)}, f32[128]{0:T(128)}, u32[]{:S(2)}) copy-start(f32[128]{0:T(128)} %get-tuple-element.2885) | copy-start | bytes 1540
  440.1 86.7 %collective-permute-start.16 = (bf16[128,768]{1,0:T(8,128)(2,1)}, bf16[128,768]{1,0:T(8,128)(2,1)}, u32[]{:S(2)}, u32[]{:S(2)}) collective-permute-start(bf16[128,768]{1,0:T(8,128)(2,1)} %get-tuple-element.2639), channel_id=1, source_target_pairs={{1,0},{2,1},{3,2},{5,4},{6,5},{7,6},{9,8},{10,9},{11,10},{13,12},{... | collective-permute-start | bytes 589832 | tf_op jit(solution)/shard_map/ppermute | solution.py:22
  585.6 5.3 collective-permute-start.17
  649.9 5.6 collective-permute-start.18
  714.2 5.3 collective-permute-start.19
  778.7 5.3 collective-permute-start.20
  844.1 5.3 collective-permute-start.21
  909.1 6.2 collective-permute-start.22
  974.7 15.0 collective-permute-start.23
  1072.8 24.3 %collective-permute-start.26 = (bf16[384,6144]{1,0:T(8,128)(2,1)}, bf16[384,6144]{1,0:T(8,128)(2,1)S(1)}, u32[]{:S(2)}, u32[]{:S(2)}) collective-permute-start(bf16[384,6144]{1,0:T(8,128)(2,1)} %slice.899), channel_id=1, source_target_pairs={{1,0},{2,1},{3,2},{5,4},{6,5},{7,6},{9,8},{10,9},{11,10},{13,12},{... | collective-permute-start | bytes 14155784 | tf_op jit(solution)/shard_map/ppermute | solution.py:22
  1074.3 15.4 collective-permute-start.24
  1080.0 11.9 collective-permute-start.27
  1082.7 4.7 collective-permute-start.25
  1176.3 19.6 %copy-start.255 = (s32[128]{0:T(128)S(1)}, s32[128]{0:T(128)}, u32[]{:S(2)}) copy-start(s32[128]{0:T(128)} %get-tuple-element.2868) | copy-start | bytes 1540
  1176.3 19.6 %copy-start.283 = (f32[128]{0:T(128)S(1)}, f32[128]{0:T(128)}, u32[]{:S(2)}) copy-start(f32[128]{0:T(128)} %get-tuple-element.2598) | copy-start | bytes 1540
  1176.3 22.2 %copy-start.254 = (s32[128]{0:T(128)S(1)}, s32[128]{0:T(128)}, u32[]{:S(2)}) copy-start(s32[128]{0:T(128)} %get-tuple-element.2867) | copy-start | bytes 1540
  1176.3 22.2 %copy-start.284 = (f32[128]{0:T(128)S(1)}, f32[128]{0:T(128)}, u32[]{:S(2)}) copy-start(f32[128]{0:T(128)} %get-tuple-element.2596) | copy-start | bytes 1540
  1176.3 24.7 %copy-start.253 = (s32[128]{0:T(128)S(1)}, s32[128]{0:T(128)}, u32[]{:S(2)}) copy-start(s32[128]{0:T(128)} %get-tuple-element.2866) | copy-start | bytes 1540
  1176.3 24.7 %copy-start.285 = (f32[128]{0:T(128)S(1)}, f32[128]{0:T(128)}, u32[]{:S(2)}) copy-start(f32[128]{0:T(128)} %get-tuple-element.2594) | copy-start | bytes 1540
  1176.3 27.3 %copy-start.252 = (s32[128]{0:T(128)S(1)}, s32[128]{0:T(128)}, u32[]{:S(2)}) copy-start(s32[128]{0:T(128)} %get-tuple-element.2865) | copy-start | bytes 1540
  1176.3 27.3 %copy-start.286 = (f32[128]{0:T(128)S(1)}, f32[128]{0:T(128)}, u32[]{:S(2)}) copy-start(f32[128]{0:T(128)} %get-tuple-element.2592) | copy-start | bytes 1540
  1176.3 29.8 %copy-start.251 = (s32[128]{0:T(128)S(1)}, s32[128]{0:T(128)}, u32[]{:S(2)}) copy-start(s32[128]{0:T(128)} %get-tuple-element.2864) | copy-start | bytes 1540
  1176.3 29.8 %copy-start.287 = (f32[128]{0:T(128)S(1)}, f32[128]{0:T(128)}, u32[]{:S(2)}) copy-start(f32[128]{0:T(128)} %get-tuple-element.2590) | copy-start | bytes 1540
  1176.3 32.3 %copy-start.250 = (s32[128]{0:T(128)S(1)}, s32[128]{0:T(128)}, u32[]{:S(2)}) copy-start(s32[128]{0:T(128)} %get-tuple-element.2863) | copy-start | bytes 1540
  1176.3 32.3 %copy-start.288 = (f32[128]{0:T(128)S(1)}, f32[128]{0:T(128)}, u32[]{:S(2)}) copy-start(f32[128]{0:T(128)} %get-tuple-element.2588) | copy-start | bytes 1540
  1176.3 34.9 %copy-start.249 = (s32[128]{0:T(128)S(1)}, s32[128]{0:T(128)}, u32[]{:S(2)}) copy-start(s32[128]{0:T(128)} %get-tuple-element.2862) | copy-start | bytes 1540
  1176.4 34.9 %copy-start.289 = (f32[128]{0:T(128)S(1)}, f32[128]{0:T(128)}, u32[]{:S(2)}) copy-start(f32[128]{0:T(128)} %get-tuple-element.2586) | copy-start | bytes 1540
  1176.4 108.4 %all-to-all-start = ((bf16[4,2,98304]{2,1,0:T(2,128)(2,1)}), bf16[4,2,98304]{2,1,0:T(2,128)(2,1)}, u32[]{:S(2)}, u32[]{:S(2)}) async-start(bf16[4,2,98304]{2,1,0:T(2,128)(2,1)} %reshape.3513), calls=%async_computation | async-start | bytes 3145728 | tf_op jit(solution)/shard_map/all_to_all | solution.py:379
  (171 other events, 620.0 us)
Sparse Core Ops, SparseCore 0:
  1106.6 590.9 all-reduce.4
where the time goes:
time: 1740 us; the launch traced here: 1720 us
  waiting for transfers between devices  556 us (32%)
  local copies, waits for them, and re-layouts  345 us (20%)
  matrix products  273 us (16%)
  other arithmetic  202 us (12%)
  starting transfers between devices  145 us (8%)
  loops' own time  98.8 us (6%)
  blocking collectives  68.9 us (4%)
  between operations  31.8 us (2%)
    psum x1, waiting for transfers between devices, per_device(): lax.psum((joint_mine, mixing_mine, gated_mine, down_mine, accumulated[4],...  405 us
    ppermute x28, waiting for transfers between devices, shifted(): return lax.ppermute(value, axis, pairs)  152 us
    another operation x24, local copies, waits for them, and re-layouts  132 us
    ppermute x28, starting transfers between devices, shifted(): return lax.ppermute(value, axis, pairs)  125 us
    dot_general x8, matrix products, attention_backward(): jnp.einsum('nd,ne->de', inputs, joint_grad, preferred_element_type=jnp.fl...  58.4 us
    another operation x11, loops' own time, per_device(): lax.switch(selector, [back_attention, back_feedforward, back_nothing], ro...  57.6 us
    dynamic_update_slice x33, other arithmetic, keep_slot(): return lax.dynamic_update_index_in_dim(buffer, chosen, slot_index, 0)  51.9 us
    psum x1, blocking collectives, per_device(): lax.psum((stat_terms, count_term), ('dp', 'section'))  46.9 us
  transfers between devices with their start and end apart: 30, of which 12 were waited for; matrix products, arithmetic and copies ran while one was open for 8% of the time, Pallas kernels for 0%

commit v1 on v0

v1 whole, which is shorter than its diff:
```python
import functools

import jax
import jax.numpy as jnp
from jax import lax
from jax.experimental import pallas as pl
from jax.experimental.pallas import tpu as pltpu
from jax.sharding import PartitionSpec as P

D = 768
HEADS = 12
HEAD = D // HEADS
FF = 3072
BLOCK = 128
HALF = D // 2
MICRO = 2

EPSILON = 1e-05
MASKED = -1e30
ROOT_HALF = 0.7071067811865476
ROOT_TWO_PI = 2.5066282746310002
SCALE = HEAD**-0.5

MESH = pl.DeviceIdType.MESH
PIECES = 32
PIECE = 384
SIDE = 112
RAIL = 160
WIDTH = 384
AHEAD = 4
LAG = 2


def reduce_kernel(
    lines, mine_ref, theirs_ref, out_ref,
    total, grown, landed, from_side, from_inner, from_low, from_high, from_root,
    load_sem, store_sem, core_send, core_recv, side_send, side_recv, inner_send, inner_recv,
    up_send, low_recv, high_recv, root_send, root_recv,
    line_send, line_recv, back_send, back_recv, low_send, high_send, rail_recv,
):
    dp, section = lax.axis_index("dp"), lax.axis_index("section")
    y, z = lax.rem(dp, 2), lax.div(dp, 2)
    half = lines // 2
    mid = half - 1
    partner = (dp, section + 1 - 2 * lax.rem(section, 2))
    across = (dp + 1 - 2 * y, section)
    below, above = (dp - 2, section), (dp + 2, section)
    lower = z < half
    depth = jnp.where(lower, z, lines - 1 - z)
    has_low, has_high = z > 0, z < lines - 1
    my_rows = pl.ds(pl.multiple_of(y * SIDE, 8), SIDE)
    other_rows = pl.ds(pl.multiple_of((1 - y) * SIDE, 8), SIDE)
    rail_rows = pl.ds(2 * SIDE, RAIL)
    last = PIECES - 1

    def remote(src, dst, send, recv, device):
        return pltpu.make_async_remote_copy(
            src_ref=src, dst_ref=dst, send_sem=send, recv_sem=recv, device_id=device, device_id_type=MESH
        )

    def arrived(dst, sem):
        pltpu.make_async_copy(dst, dst, sem).wait()

    barrier = pltpu.get_barrier_semaphore()
    pl.semaphore_signal(barrier, inc=1, device_id=partner, device_id_type=MESH)
    pl.semaphore_signal(barrier, inc=1, device_id=across, device_id_type=MESH)

    @pl.when(has_low)
    def _():
        pl.semaphore_signal(barrier, inc=1, device_id=below, device_id_type=MESH)

    @pl.when(has_high)
    def _():
        pl.semaphore_signal(barrier, inc=1, device_id=above, device_id_type=MESH)

    pl.semaphore_wait(barrier, 2 + has_low.astype(jnp.int32) + has_high.astype(jnp.int32))

    def to_partner(b):
        return remote(theirs_ref.at[b], landed.at[b], core_send.at[b], core_recv.at[b], partner)

    def load(b):
        return pltpu.make_async_copy(mine_ref.at[b], grown.at[b], load_sem.at[b])

    def store(b):
        return pltpu.make_async_copy(total.at[b], out_ref.at[b], store_sem.at[b])

    def start_all(b, carry):
        to_partner(b).start()
        load(b).start()
        return carry

    lax.fori_loop(0, AHEAD, start_all, 0)

    def add(dst, rows, b, *others):
        value = grown[b, rows].astype(jnp.float32)
        for other in others:
            value = value + other.astype(jnp.float32)
        dst[b, rows] = value.astype(jnp.bfloat16)

    def when(active, b):
        return pl.when(active & (b >= 0) & (b < PIECES))

    def root_of(b):
        odd = lax.rem(b, 2)
        return jnp.where(b < PIECES // 2, odd * (lines - 1), mid + odd)

    def step(i, carry):
        b1 = i - LAG * (1 + depth)

        @when(True, b1)
        def _():
            arrived(from_side.at[b1], side_recv.at[b1])

            @pl.when(depth == 0)
            def _():
                add(grown, my_rows, b1, from_side[b1])

            @pl.when(depth > 0)
            def _():
                arrived(from_inner.at[0, b1], inner_recv.at[0, b1])
                add(grown, my_rows, b1, from_side[b1], from_inner[0, b1])

            inward = (jnp.where(lower, dp + 2, dp - 2), section)
            slot = (depth == mid).astype(jnp.int32)
            remote(
                grown.at[b1, my_rows], from_inner.at[slot, b1], inner_send.at[b1], inner_recv.at[slot, b1], inward
            ).start()

        b2 = i - LAG * (2 + mid + mid - depth)

        @when(True, b2)
        def _():
            @pl.when(depth == mid)
            def _():
                arrived(from_inner.at[1, b2], inner_recv.at[1, b2])
                add(total, my_rows, b2, from_inner[1, b2])

            @pl.when(depth < mid)
            def _():
                arrived(total.at[b2, my_rows], line_recv.at[b2])

            @pl.when(depth > 0)
            def _():
                outward = (jnp.where(lower, dp - 2, dp + 2), section)
                remote(total.at[b2, my_rows], total.at[b2, my_rows], line_send.at[b2], line_recv.at[b2], outward).start()

            remote(total.at[b2, my_rows], total.at[b2, my_rows], back_send.at[b2], back_recv.at[b2], across).start()

        b3 = i - LAG * (3 + mid + mid - depth)

        @when(True, b3)
        def _():
            arrived(total.at[b3, other_rows], back_recv.at[b3])

        for early in (True, False):
            for odd in (0, 1):
                root = (odd * (lines - 1)) if early else mid + odd
                height = max(root, lines - 1 - root)
                distance = jnp.abs(z - root)

                def mine(b, root=root):
                    return (root_of(b) == root) & (lax.rem(b + 4 * PIECES, 2) == odd)

                hop = jnp.where(z < root, z, jnp.where(z > root, lines - 1 - z, height))
                c1 = i - LAG * hop

                @when((z != root) & (hop > 0) & mine(c1), c1)
                def _(root=root, c1=c1):
                    @pl.when(z < root)
                    def _():
                        arrived(from_low.at[c1], low_recv.at[c1])
                        add(grown, rail_rows, c1, from_low[c1])
                        remote(grown.at[c1, rail_rows], from_low.at[c1], up_send.at[c1], low_recv.at[c1], above).start()

                    @pl.when(z > root)
                    def _():
                        arrived(from_high.at[c1], high_recv.at[c1])
                        add(grown, rail_rows, c1, from_high[c1])
                        remote(grown.at[c1, rail_rows], from_high.at[c1], up_send.at[c1], high_recv.at[c1], below).start()

                @when((z == root) & mine(c1), c1)
                def _(root=root, c1=c1):
                    if root > 0:
                        arrived(from_low.at[c1], low_recv.at[c1])
                    if root < lines - 1:
                        arrived(from_high.at[c1], high_recv.at[c1])
                    parts = ([from_low[c1]] if root > 0 else []) + ([from_high[c1]] if root < lines - 1 else [])
                    add(grown, rail_rows, c1, *parts)
                    remote(grown.at[c1, rail_rows], from_root.at[c1], root_send.at[c1], root_recv.at[c1], across).start()

                c2 = i - LAG * (height + 1 + distance)

                @when(mine(c2), c2)
                def _(root=root, c2=c2):
                    @pl.when(z == root)
                    def _():
                        arrived(from_root.at[c2], root_recv.at[c2])
                        add(total, rail_rows, c2, from_root[c2])

                    @pl.when(z != root)
                    def _():
                        arrived(total.at[c2, rail_rows], rail_recv.at[c2])

                    @pl.when(has_low & (z <= root))
                    def _():
                        remote(total.at[c2, rail_rows], total.at[c2, rail_rows], low_send.at[c2], rail_recv.at[c2], below).start()

                    @pl.when(has_high & (z >= root))
                    def _():
                        remote(total.at[c2, rail_rows], total.at[c2, rail_rows], high_send.at[c2], rail_recv.at[c2], above).start()

        b4 = i - LAG * (2 * lines - 1)

        @when(True, b4)
        def _():
            store(b4).start()

        b0 = i

        @when(True, b0)
        def _():
            @pl.when(b0 + AHEAD < PIECES)
            def _():
                start_all(b0 + AHEAD, 0)

            load(b0).wait()
            to_partner(b0).wait_recv()
            grown[b0] = (grown[b0].astype(jnp.float32) + landed[b0].astype(jnp.float32)).astype(jnp.bfloat16)
            remote(grown.at[b0, other_rows], from_side.at[b0], side_send.at[b0], side_recv.at[b0], across).start()
            root = root_of(b0)

            @pl.when((z == 0) & (root != 0))
            def _():
                remote(grown.at[b0, rail_rows], from_low.at[b0], up_send.at[b0], low_recv.at[b0], above).start()

            @pl.when((z == lines - 1) & (root != lines - 1))
            def _():
                remote(grown.at[b0, rail_rows], from_high.at[b0], up_send.at[b0], high_recv.at[b0], below).start()

        return carry

    lax.fori_loop(0, PIECES + LAG * (2 * lines - 1), step, 0)

    def finish(b, carry):
        store(b).wait()
        to_partner(b).wait_send()
        root = root_of(b)
        pltpu.make_async_copy(grown.at[b, other_rows], grown.at[b, other_rows], side_send.at[b]).wait()
        pltpu.make_async_copy(grown.at[b, my_rows], grown.at[b, my_rows], inner_send.at[b]).wait()
        pltpu.make_async_copy(total.at[b, my_rows], total.at[b, my_rows], back_send.at[b]).wait()

        @pl.when(depth > 0)
        def _():
            pltpu.make_async_copy(total.at[b, my_rows], total.at[b, my_rows], line_send.at[b]).wait()

        @pl.when(z != root)
        def _():
            pltpu.make_async_copy(grown.at[b, rail_rows], grown.at[b, rail_rows], up_send.at[b]).wait()

        @pl.when(z == root)
        def _():
            pltpu.make_async_copy(grown.at[b, rail_rows], grown.at[b, rail_rows], root_send.at[b]).wait()

        @pl.when(has_low & (z <= root))
        def _():
            pltpu.make_async_copy(total.at[b, rail_rows], total.at[b, rail_rows], low_send.at[b]).wait()

        @pl.when(has_high & (z >= root))
        def _():
            pltpu.make_async_copy(total.at[b, rail_rows], total.at[b, rail_rows], high_send.at[b]).wait()

        return carry

    lax.fori_loop(0, PIECES, finish, 0)


def reduce_gradients(lines, mine, theirs):
    bf = jnp.bfloat16
    sems = lambda *s: pltpu.SemaphoreType.DMA(s or (PIECES,))
    return pl.pallas_call(
        functools.partial(reduce_kernel, lines),
        out_shape=jax.ShapeDtypeStruct((PIECES, PIECE, WIDTH), bf),
        in_specs=[pl.BlockSpec(memory_space=pl.ANY)] * 2,
        out_specs=pl.BlockSpec(memory_space=pl.ANY),
        scratch_shapes=[
            pltpu.VMEM((PIECES, PIECE, WIDTH), bf),
            pltpu.VMEM((PIECES, PIECE, WIDTH), bf),
            pltpu.VMEM((PIECES, PIECE, WIDTH), bf),
            pltpu.VMEM((PIECES, SIDE, WIDTH), bf),
            pltpu.VMEM((2, PIECES, SIDE, WIDTH), bf),
            pltpu.VMEM((PIECES, RAIL, WIDTH), bf),
            pltpu.VMEM((PIECES, RAIL, WIDTH), bf),
            pltpu.VMEM((PIECES, RAIL, WIDTH), bf),
            sems(), sems(),
            sems(), sems(),
            sems(), sems(),
            sems(), sems(2, PIECES),
            sems(), sems(), sems(),
            sems(), sems(),
            sems(), sems(),
            sems(), sems(),
            sems(), sems(), sems(),
        ],
        compiler_params=pltpu.CompilerParams(collective_id=1, has_side_effects=True, vmem_limit_bytes=60 * 2**20),
    )(mine, theirs)


def alibi_slopes():
    closest = 1 << HEADS.bit_length() - 1
    first_slope = 2.0 ** (-8.0 / closest)
    slopes = [first_slope ** (power_index + 1) for power_index in range(closest)]
    double_slope = 2.0 ** (-8.0 / (2 * closest))
    extra_slopes = [double_slope ** (power_index + 1) for power_index in range(2 * closest)]
    return slopes + extra_slopes[0::2][: HEADS - closest]


def alibi_bias():
    positions = jnp.arange(BLOCK)
    distance = jnp.abs(positions[:, None] - positions[None, :]).astype(jnp.float32)
    return -jnp.array(alibi_slopes(), jnp.float32)[:, None, None] * distance


def dot(a, b):
    return jnp.dot(a, b, preferred_element_type=jnp.float32)


def dot_right(a, b):
    return lax.dot_general(a, b, (((1,), (1,)), ((), ())), preferred_element_type=jnp.float32)


def dot_left(a, b):
    return lax.dot_general(a, b, (((0,), (0,)), ((), ())), preferred_element_type=jnp.float32)


def post_norm(inputs, branch, gain, bias):
    summed = inputs.astype(jnp.float32) + branch
    center = summed - jnp.mean(summed, axis=-1, keepdims=True)
    spread = jnp.mean(center * center, axis=-1, keepdims=True)
    inverse = lax.rsqrt(spread + EPSILON)
    scaled = center * inverse
    return ((scaled * gain + bias).astype(jnp.bfloat16), scaled, inverse)


def norm_back(upstream, scaled, inverse, gain):
    scaled_grad = upstream * gain
    gain_term = jnp.sum(upstream * scaled, axis=0)
    bias_term = jnp.sum(upstream, axis=0)
    through = inverse * (
        scaled_grad
        - jnp.mean(scaled_grad, axis=-1, keepdims=True)
        - scaled * jnp.mean(scaled_grad * scaled, axis=-1, keepdims=True)
    )
    return (through, gain_term, bias_term)


def squares(rows, valid):
    rows = rows.astype(jnp.float32)
    return jnp.sum(valid * jnp.sum(rows * rows, axis=-1))


def attend(rows, segments, joint, mixing, gain, bias):
    count = rows.shape[0] // BLOCK
    joint_rows = dot(rows, joint).astype(jnp.bfloat16).reshape(count, BLOCK, 3, HEADS, HEAD)
    queries, keys, values = joint_rows[:, :, 0], joint_rows[:, :, 1], joint_rows[:, :, 2]
    scores = jnp.einsum("bqhd,bkhd->bhqk", queries, keys, preferred_element_type=jnp.float32)
    scores = scores * SCALE + alibi_bias()[None]
    blocks = segments.reshape(count, BLOCK)
    same = blocks[:, None, :, None] == blocks[:, None, None, :]
    scores = jnp.where(same, scores, MASKED)
    exponents = jnp.exp(scores - jnp.max(scores, axis=-1, keepdims=True))
    probs = exponents / jnp.sum(exponents, axis=-1, keepdims=True)
    low = probs.astype(jnp.bfloat16)
    mixed = jnp.einsum("bhqk,bkhd->bqhd", low, values, preferred_element_type=jnp.float32)
    mixed = mixed.reshape(rows.shape[0], D).astype(jnp.bfloat16)
    branch = dot(mixed, mixing)
    out, scaled, inverse = post_norm(rows, branch, gain, bias)
    return out, branch, (queries, keys, values, probs, low, mixed, scaled, inverse)


def attend_back(upstream, kept, joint, mixing, gain):
    queries, keys, values, probs, low, mixed, scaled, inverse = kept
    through, gain_term, bias_term = norm_back(upstream, scaled, inverse, gain)
    branch_grad = through.astype(jnp.bfloat16)
    mixed_grad = dot_right(branch_grad, mixing).astype(jnp.bfloat16).reshape(queries.shape)
    probs_grad = jnp.einsum("bqhd,bkhd->bhqk", mixed_grad, values, preferred_element_type=jnp.float32)
    values_grad = jnp.einsum("bhqk,bqhd->bkhd", low, mixed_grad, preferred_element_type=jnp.float32)
    score_grad = probs * (probs_grad - jnp.sum(probs_grad * probs, axis=-1, keepdims=True))
    score_grad = score_grad.astype(jnp.bfloat16)
    queries_grad = SCALE * jnp.einsum("bhqk,bkhd->bqhd", score_grad, keys, preferred_element_type=jnp.float32)
    keys_grad = SCALE * jnp.einsum("bhqk,bqhd->bkhd", score_grad, queries, preferred_element_type=jnp.float32)
    joint_grad = jnp.stack([queries_grad, keys_grad, values_grad], axis=2)
    joint_grad = joint_grad.reshape(upstream.shape[0], 3 * D).astype(jnp.bfloat16)
    rows_grad = through + dot_right(joint_grad, joint)
    return rows_grad, (mixed, branch_grad, joint_grad), (gain_term, bias_term)


def feed(rows, gated, down, gain, bias):
    gate_up = dot(rows, gated)
    gate, up = gate_up[:, :FF], gate_up[:, FF:]
    normal = 0.5 * (1.0 + lax.erf(gate * ROOT_HALF))
    density = jnp.exp(-0.5 * gate * gate) / ROOT_TWO_PI
    active = gate * normal
    hidden = (active * up).astype(jnp.bfloat16)
    slope = up * (normal + gate * density)
    branch = dot(hidden, down)
    out, scaled, inverse = post_norm(rows, branch, gain, bias)
    return out, branch, (hidden, active, slope, scaled, inverse)


def feed_back(upstream, kept, gated, down, gain):
    hidden, active, slope, scaled, inverse = kept
    through, gain_term, bias_term = norm_back(upstream, scaled, inverse, gain)
    branch_grad = through.astype(jnp.bfloat16)
    hidden_grad = dot_right(branch_grad, down)
    both_grad = jnp.concatenate([hidden_grad * slope, hidden_grad * active], axis=-1).astype(jnp.bfloat16)
    rows_grad = through + dot_right(both_grad, gated)
    return rows_grad, (hidden, branch_grad, both_grad), (gain_term, bias_term)


def per_device(
    inputs, cotangent_first, cotangent_second, segment_ids,
    joint_projection, mixing_weight, gated_weight, down_weight, norm_gain, norm_bias,
):
    section = lax.axis_index("section")
    plane, core = section // 2, section % 2
    micro_rows = inputs.shape[0] // (2 * MICRO)
    lines = lax.axis_size("dp") // 2
    swap = [(0, 1), (1, 0), (2, 3), (3, 2)]
    forward = [(0, 2), (1, 3)]
    backward = [(2, 0), (3, 1)]

    def send(value, pairs):
        return lax.ppermute(value, "section", pairs)

    def whole(mine):
        other = send(mine, swap)
        return jnp.where(core == 0, jnp.concatenate([mine, other]), jnp.concatenate([other, mine]))

    joint, mixing, gated, down = [whole(w) for w in (joint_projection, mixing_weight, gated_weight, down_weight)]
    gains, biases = whole(norm_gain), whole(norm_bias)

    def micro(array, m):
        return lax.dynamic_slice_in_dim(array, (2 * m + core) * micro_rows, micro_rows, 0)

    segments = [micro(segment_ids, m) for m in range(MICRO)]
    valid = [(s >= 0).astype(jnp.float32) for s in segments]

    def layer(rows, m):
        attended, first_branch, first_kept = attend(rows, segments[m], joint, mixing, gains[0], biases[0])
        out, second_branch, second_kept = feed(attended, gated, down, gains[1], biases[1])
        stats = jnp.stack([
            jnp.stack([squares(rows, valid[m]), squares(attended, valid[m])]),
            jnp.stack([squares(first_branch, valid[m]), squares(second_branch, valid[m])]),
        ])
        return out, (rows, attended, first_kept, second_kept, stats)

    def layer_back(upstream, kept):
        rows, attended, first_kept, second_kept, _ = kept
        middle, second_terms, second_norm = feed_back(upstream, second_kept, gated, down, gains[1])
        middle = middle.astype(jnp.bfloat16).astype(jnp.float32)
        grad, first_terms, first_norm = attend_back(middle, first_kept, joint, mixing, gains[0])
        return grad, (first_terms, second_terms, first_norm, second_norm)

    starts = [micro(inputs, m) for m in range(MICRO)]
    early = [layer(starts[m], m)[0] for m in range(MICRO)]
    passed = [send(early[m], forward) for m in range(MICRO)]
    rows = [jnp.where(plane == 0, starts[m], passed[m]) for m in range(MICRO)]
    outs, kept = zip(*[layer(rows[m], m) for m in range(MICRO)])
    first_output = jnp.where(plane == 0, early[0], passed[1])
    second_output = jnp.where(plane == 0, send(outs[0], backward), outs[1])

    final = [valid[m][:, None] * micro(cotangent_second, m).astype(jnp.float32) for m in range(MICRO)]
    middle_add = [valid[m][:, None] * micro(cotangent_first, m).astype(jnp.float32) for m in range(MICRO)]
    early_back = [
        (layer_back(final[m], kept[m])[0] + middle_add[m]).astype(jnp.bfloat16) for m in range(MICRO)
    ]
    passed_back = [send(early_back[m], backward) for m in range(MICRO)]
    upstream = [jnp.where(plane == 0, passed_back[m].astype(jnp.float32), final[m]) for m in range(MICRO)]
    grads, terms = zip(*[layer_back(upstream[m], kept[m]) for m in range(MICRO)])
    grads = [g.astype(jnp.bfloat16) for g in grads]
    middle_gradient = jnp.where(plane == 0, passed_back[0], early_back[1])
    input_gradient = jnp.where(plane == 0, grads[0], send(grads[1], forward))

    def joined(get):
        return jnp.concatenate([get(m) for m in range(MICRO)])

    mixed = joined(lambda m: terms[m][0][0])
    first_branch = joined(lambda m: terms[m][0][1])
    joint_grad = joined(lambda m: terms[m][0][2])
    hidden = joined(lambda m: terms[m][1][0])
    second_branch = joined(lambda m: terms[m][1][1])
    both_grad = joined(lambda m: terms[m][1][2])
    first_rows = joined(lambda m: kept[m][0])
    second_rows = joined(lambda m: kept[m][1])
    weights = [
        dot_left(first_rows, joint_grad),
        dot_left(mixed, first_branch),
        dot_left(second_rows, both_grad),
        dot_left(hidden, second_branch),
    ]
    weights = [w.astype(jnp.bfloat16) for w in weights]

    def pieces(which):
        parts = []
        for w in weights:
            part = lax.dynamic_slice_in_dim(w, which * (w.shape[0] // 2), w.shape[0] // 2, 0)
            height, width = part.shape
            part = part.reshape(height // PIECE, PIECE, width // WIDTH, WIDTH).transpose(0, 2, 1, 3)
            parts.append(part.reshape(-1, PIECE, WIDTH))
        return jnp.concatenate(parts)

    reduced = reduce_gradients(lines, pieces(core), pieces(1 - core))
    results, at = [], 0
    for w in weights:
        height, width = w.shape[0] // 2, w.shape[1]
        count = height * width // (PIECE * WIDTH)
        part = reduced[at : at + count].reshape(height // PIECE, width // WIDTH, PIECE, WIDTH)
        results.append(part.transpose(0, 2, 1, 3).reshape(height, width).astype(jnp.float32))
        at += count

    norms = [
        jnp.stack([sum(terms[m][2 + k][0] for m in range(MICRO)), sum(terms[m][2 + k][1] for m in range(MICRO))])
        for k in range(2)
    ]
    own = jnp.where(core == 0, norms[0], norms[1]) + send(jnp.where(core == 0, norms[1], norms[0]), swap)
    gain_bias = lax.psum(own, "dp")

    stats = sum(kept[m][4] for m in range(MICRO))
    blank = jnp.zeros_like(stats)
    stats = jnp.where(plane == 0, jnp.concatenate([stats, blank], 1), jnp.concatenate([blank, stats], 1))
    count = jnp.where(plane == 0, sum(jnp.sum(v) for v in valid), 0.0)
    stats, count = lax.psum((stats, count), ("dp", "section"))
    magnitudes = jnp.sqrt(stats / (count * D))
    return (
        first_output, second_output, input_gradient, middle_gradient,
        results[0], results[1], results[2], results[3],
        gain_bias[:1], gain_bias[1:], magnitudes,
    )


def solution(mesh):
    tokens, rows = P("dp", None), P("section", None)
    return jax.shard_map(
        per_device,
        mesh=mesh,
        in_specs=(tokens, tokens, tokens, P("dp"), rows, rows, rows, rows, rows, rows),
        out_specs=(P(("dp", "section"), None),) * 4 + (rows,) * 6 + (P(),),
        check_vma=False,
    )
```

time: 1740 us -> 741 us (0.43)
  waiting for transfers between devices: 556 us -> 22.4 us
  local copies, waits for them, and re-layouts: 345 us -> 162 us
  Pallas kernels: 0 us -> 182 us
  starting transfers between devices: 145 us -> 20.9 us
  other arithmetic: 202 us -> 85.1 us
  loops' own time: 98.8 us -> 0 us
  matrix products: 273 us -> 188 us
  between operations: 31.8 us -> 5.48 us
    psum x1 -> x0, waiting for transfers between devices: 405 us -> none  [per_device(): lax.psum((joint_mine, mixing_mine, gated_mine, down_mine, accumulated[4],...]
    pallas_call x0 -> x1, Pallas kernels: none -> 182 us  [reduce_gradients(): pl.pallas_call(functools.partial(reduce_kernel, lines), out_shape=jax.Sha...]
    ppermute x28 -> x13, waiting for transfers between devices: 152 us -> 22.4 us  [send(): return lax.ppermute(value, 'section', pairs)]
    another operation x24 -> x4, local copies, waits for them, and re-layouts: 132 us -> 6.89 us  [attend_back(): joint_grad = jnp.stack([queries_grad, keys_grad, values_grad], axis=2)]
    ppermute x28 -> x13, starting transfers between devices: 125 us -> 20.9 us  [send(): return lax.ppermute(value, 'section', pairs)]
    another operation x22 -> x0, loops' own time: 98.8 us -> none  [the longest x11 57.6 us: per_device(): lax.switch(selector, [back_attention, back_feedforward, back_nothing], ro...]
    dynamic_update_slice x33 -> x0, other arithmetic: 51.9 us -> none  [keep_slot(): return lax.dynamic_update_index_in_dim(buffer, chosen, slot_index, 0)]
    dot_general x120 -> x60, matrix products: 233 us -> 188 us  [the longest x16 88.4 us: dot_right(): lax.dot_general(a, b, (((1,), (1,)), ((), ())), preferred_element_type=jn...]
  transfers between devices with their start and end apart: 30 -> 13, of which waited for: 12 -> 4; matrix products, arithmetic and copies ran while one was open for 8% -> 12% of each run, Pallas kernels for 0% -> 0%
where the time goes in v1:
time: 741 us; the launch traced here: 729 us
  matrix products  188 us (25%)
  Pallas kernels  182 us (25%)
  local copies, waits for them, and re-layouts  162 us (22%)
  other arithmetic  85.1 us (11%)
  blocking collectives  63.9 us (9%)
  waiting for transfers between devices  22.4 us (3%)
  starting transfers between devices  20.9 us (3%)
    pallas_call x1, Pallas kernels, reduce_gradients(): pl.pallas_call(functools.partial(reduce_kernel, lines), out_shape=jax.Sha...  182 us
    dot_general x16, matrix products, dot_right(): lax.dot_general(a, b, (((1,), (1,)), ((), ())), preferred_element_type=jn...  88.4 us
    dot_general x16, matrix products, dot(): return jnp.dot(a, b, preferred_element_type=jnp.float32)  46.6 us
    psum x1, blocking collectives, per_device(): stats, count = lax.psum((stats, count), ('dp', 'section'))  45.1 us
    unnamed x354, local copies, waits for them, and re-layouts  36.5 us
    dynamic_slice x8, local copies, waits for them, and re-layouts, pieces(): lax.dynamic_slice_in_dim(w, which * (w.shape[0] // 2), w.shape[0] // 2, 0)  34.6 us
    reshape x8, local copies, waits for them, and re-layouts, pieces(): part.reshape(height // PIECE, PIECE, width // WIDTH, WIDTH)  31.8 us
    ppermute x13, waiting for transfers between devices, send(): return lax.ppermute(value, 'section', pairs)  22.4 us
  transfers between devices with their start and end apart: 13, of which 4 were waited for; matrix products, arithmetic and copies ran while one was open for 12% of the time, Pallas kernels for 0%

profile of v1, /device:TPU:0, one launch (start us, length us, event | category | flops | bytes accessed | tf_op | source)
XLA Modules:
  0.0 729.0 jit_solution(9733573410453140625)
XLA Ops:
  5.9 4.5 convolution_convert_fusion.5
  14.1 4.5 convolution_convert_fusion.6
  28.7 3.9 maximum_select_fusion.1
  32.7 9.5 %maximum_select_fusion = bf16[768,6144]{1,0:T(8,128)(2,1)S(1)} fusion(bf16[384,6144]{1,0:T(8,128)(2,1)} %collective-permute-done.4, bf16[384,6144]{1,0:T(8,128)(2,1)S(1)} %bitcast.356, pred[]{:T(512)S(6)} %eq.33), kind=kLoop, calls=%fused_computation.5 | loop fusion | flops 42467328 | bytes 18874368 | tf_op jit(solution)/shard_map/jit(_where)/select_n | solution.py:437
  47.3 4.5 collective-permute-start.6
  56.8 4.0 collective-permute-done.6
  61.7 4.4 collective-permute-start.7
  66.2 8.0 %collective-permute-done.7 = bf16[256,768]{1,0:T(8,128)(2,1)S(1)} collective-permute-done((bf16[256,768]{1,0:T(8,128)(2,1)S(1)}, bf16[256,768]{1,0:T(8,128)(2,1)S(1)}, u32[]{:S(2)}, u32[]{:S(2)}) %collective-permute-start.7) | collective-permute-done | bytes 393248 | tf_op jit(solution)/shard_map/ppermute | solution.py:433
  86.3 3.8 fusion.130
  95.5 4.2 convolution_convert_fusion.4
  102.1 3.5 reshape.400
  119.5 6.0 fusion.242
  145.0 7.8 %multiply_convert_fusion.7 = (bf16[256,3072]{1,0:T(8,128)(2,1)}, bf16[256,3072]{1,0:T(8,128)(2,1)}) fusion(f32[256,3072]{1,0:T(8,128)} %get-tuple-element.91, f32[256,6144]{1,0:T(8,128)S(1)} %fusion.241, bf16[3072,768]{1,0:T(8,128)(2,1)} %copy-done.27, f32[256,768]{1,0:T(8,128)S(1)} %get-tuple-element.85, f32[256]{0:T(256)S(1)} %broadcast_multiply_fusion.15, ...), kind=kOutput, calls=%fused_computation.68 | convolution fusion | flops 1218183168 | bytes 18489348 | tf_op jit(solution)/shard_map/dot_general | solution.py:328
  152.9 6.1 fusion.224
  183.8 6.0 fusion.107
  191.1 45.1 %all-reduce.2 = (f32[2,4]{1,0:T(2,128)S(1)}, f32[]{:T(128)}) all-reduce(f32[2,4]{1,0:T(2,128)} %pad_select_fusion, f32[]{:T(128)S(6)} %select_n.190), channel_id=1, replica_groups=mesh['dp'=8,'section'=4] {'dp','section'}, use_global_device_ids=true, to_apply=%region_69.70 | all-reduce | flops 9 | bytes 72 | tf_op jit(solution)/shard_map/psum | solution.py:532
  241.5 8.9 %multiply_convert_fusion.3 = (bf16[256,3072]{1,0:T(8,128)(2,1)}, bf16[256,3072]{1,0:T(8,128)(2,1)}) fusion(f32[256,3072]{1,0:T(8,128)} %get-tuple-element.87, f32[256,6144]{1,0:T(8,128)} %copy-done.1, bf16[3072,768]{1,0:T(8,128)(2,1)} %copy-done.27, f32[256,768]{1,0:T(8,128)S(1)} %get-tuple-element.84, f32[256]{0:T(256)S(1)} %broadcast_multiply_fusion.7, ...), kind=kOutput, calls=%fused_computation.64 | convolution fusion | flops 1218183168 | bytes 18489348 | tf_op jit(solution)/shard_map/dot_general | solution.py:328
  250.4 6.1 fusion.225
  272.8 4.8 broadcast_select_fusion
  279.4 10.3 %collective-permute-done.10 = bf16[256,768]{1,0:T(8,128)(2,1)S(1)} collective-permute-done((bf16[256,768]{1,0:T(8,128)(2,1)S(1)}, bf16[256,768]{1,0:T(8,128)(2,1)S(1)}, u32[]{:S(2)}, u32[]{:S(2)}) %collective-permute-start.10) | collective-permute-done | bytes 393248 | tf_op jit(solution)/shard_map/ppermute | solution.py:433
  289.7 3.5 fusion.226
  293.3 7.2 multiply_convert_fusion.5
  300.6 6.7 multiply_reduce_fusion.11
  309.6 7.8 %multiply_convert_fusion.1 = (bf16[256,3072]{1,0:T(8,128)(2,1)}, bf16[256,3072]{1,0:T(8,128)(2,1)}) fusion(f32[256,3072]{1,0:T(8,128)} %get-tuple-element.87, f32[256,6144]{1,0:T(8,128)S(1)} %bitcast.328, bf16[256,768]{1,0:T(8,128)(2,1)S(1)} %get-tuple-element.82, bf16[3072,768]{1,0:T(8,128)(2,1)} %copy-done.27), kind=kOutput, calls=%fused_computation.62 | convolution fusion | flops 1216610304 | bytes 17694720 | tf_op jit(solution)/shard_map/dot_general | solution.py:328
  317.5 7.1 multiply_reduce_fusion.10
  343.3 4.5 convolution_convert_fusion.1
  347.9 11.7 %convolution_convert_fusion = bf16[768,6144]{1,0:T(8,128)(2,1)} fusion(bf16[256,3072]{1,0:T(8,128)(2,1)} %get-tuple-element.99, bf16[256,3072]{1,0:T(8,128)(2,1)} %get-tuple-element.98, bf16[256,3072]{1,0:T(8,128)(2,1)} %get-tuple-element.97, bf16[256,3072]{1,0:T(8,128)(2,1)} %get-tuple-element.96, bf16[256,768]{1,0:T(8,128)(2,1)S(1)} %copy-done.26, ...), kind=kOutput, calls=%fused_computation.4 | convolution fusion | flops 4863295488 | bytes 16515072 | tf_op jit(solution)/shard_map/dot_general | solution.py:332
  369.2 8.7 %constant_dynamic-slice_fusion.1 = (bf16[384,6144]{1,0:T(8,128)(2,1)}, bf16[384,6144]{1,0:T(8,128)(2,1)}) fusion(bf16[768,6144]{1,0:T(8,128)(2,1)} %convolution_convert_fusion, s32[]{:T(128)S(6)} %select_n.184, s32[]{:T(128)S(6)} %select_n.182), kind=kLoop, calls=%fused_computation.335 | loop fusion | bytes 18874376 | tf_op jit(solution)/shard_map/dynamic_slice | solution.py:506
  377.9 6.6 copy.117
  384.5 7.0 copy.118
  402.8 3.9 copy.114
  406.7 3.8 copy.115
  410.5 5.8 reshape.420
  419.7 6.6 copy.123
  426.3 6.7 copy.124
  433.3 3.9 copy.120
  437.1 3.9 copy.121
  441.1 9.3 %pad_maximum_fusion.mine_ref = bf16[32,384,384]{2,1,0:T(8,128)(2,1)} fusion(bf16[8,384,384]{2,1,0:T(8,128)(2,1)S(1)} %bitcast.339, bf16[16,384,384]{2,1,0:T(8,128)(2,1)} %bitcast.334, bf16[2,384,384]{2,1,0:T(8,128)(2,1)S(1)} %bitcast.357, bf16[6,384,384]{2,1,0:T(8,128)(2,1)} %bitcast.343), kind=kLoop, calls=%fused_computation.6 | loop fusion | flops 14155776 | bytes 18874368 | tf_op jit(solution)/shard_map/concatenate | solution.py:510
  450.4 4.9 pad_maximum_fusion.1.theirs_ref
  455.3 182.0 %shard_map.221 = bf16[32,384,384]{2,1,0:T(8,128)(2,1)} custom-call(bf16[32,384,384]{2,1,0:T(8,128)(2,1)} %pad_maximum_fusion.mine_ref, bf16[32,384,384]{2,1,0:T(8,128)(2,1)} %pad_maximum_fusion.1.theirs_ref), custom_call_target="tpu_custom_call" | custom-call | tf_op jit(solution)/shard_map/pallas_call | solution.py:280
  639.5 7.2 convert_bitcast_fusion
  648.6 5.0 fusion.110
  653.6 5.3 collective-permute-start.11
  673.6 9.6 %copy.128 = f32[1,384,16,384]{1,3,2,0:T(8,128)} copy(f32[1,384,16,384]{3,1,2,0:T(8,128)} %convert_bitcast_fusion) | data formatting | bytes 18874368 | tf_op jit(solution)/shard_map/convert_element_type | solution.py:518
  683.2 9.6 %copy.132 = f32[384,6144]{1,0:T(8,128)} copy(f32[384,6144]{0,1:T(8,128)} %bitcast.326) | data formatting | bytes 18874368
  692.8 6.0 copy.129
  702.1 18.8 %psum.21 = f32[2,768]{1,0:T(2,128)S(1)} all-reduce(f32[2,768]{1,0:T(2,128)S(1)} %select_add_fusion), channel_id=1, replica_groups=mesh['dp'=8,'section'=4] {'dp'}, use_global_device_ids=true, to_apply=%region_52.53 | all-reduce | flops 1536 | bytes 12288 | tf_op jit(solution)/shard_map/psum | solution.py:526
  723.3 5.5 fusion.139
  (556 shorter events, 199.1 us)
Async XLA Ops:
  0.6 5.3 collective-permute-start
  1.2 27.5 %collective-permute-start.5 = (bf16[1536,768]{1,0:T(8,128)(2,1)}, bf16[1536,768]{1,0:T(8,128)(2,1)}, u32[]{:S(2)}, u32[]{:S(2)}) collective-permute-start(bf16[1536,768]{1,0:T(8,128)(2,1)} %param.21), channel_id=1, source_target_pairs={{0,1},{1,0},{2,3},{3,2},{4,5},{5,4},{6,7},{7,6},{8,9},{9,8},{10,11... | collective-permute-start | bytes 7077896 | tf_op jit(solution)/shard_map/ppermute | solution.py:433
  1.2 31.4 %collective-permute-start.4 = (bf16[384,6144]{1,0:T(8,128)(2,1)}, bf16[384,6144]{1,0:T(8,128)(2,1)}, u32[]{:S(2)}, u32[]{:S(2)}) collective-permute-start(bf16[384,6144]{1,0:T(8,128)(2,1)} %param.20), channel_id=1, source_target_pairs={{0,1},{1,0},{2,3},{3,2},{4,5},{5,4},{6,7},{7,6},{8,9},{9,8},{10,11... | collective-permute-start | bytes 14155784 | tf_op jit(solution)/shard_map/ppermute | solution.py:433
  1.7 3.0 collective-permute-start.2
  1.8 3.3 collective-permute-start.3
  4.7 18.8 %collective-permute-start.1 = (bf16[384,768]{1,0:T(8,128)(2,1)}, bf16[384,768]{1,0:T(8,128)(2,1)}, u32[]{:S(2)}, u32[]{:S(2)}) collective-permute-start(bf16[384,768]{1,0:T(8,128)(2,1)} %param.19), channel_id=1, source_target_pairs={{0,1},{1,0},{2,3},{3,2},{4,5},{5,4},{6,7},{7,6},{8,9},{9,8},{10,11... | collective-permute-start | bytes 1769480 | tf_op jit(solution)/shard_map/ppermute | solution.py:433
  32.6 22.0 %copy-start.27 = (bf16[3072,768]{1,0:T(8,128)(2,1)}, bf16[3072,768]{1,0:T(8,128)(2,1)S(1)}, u32[]{:S(2)}) copy-start(bf16[3072,768]{1,0:T(8,128)(2,1)S(1)} %maximum_select_fusion.1) | copy-start | bytes 14155780
  47.3 13.4 %collective-permute-start.6 = (bf16[256,768]{1,0:T(8,128)(2,1)S(1)}, bf16[256,768]{1,0:T(8,128)(2,1)S(1)}, u32[]{:S(2)}, u32[]{:S(2)}) collective-permute-start(bf16[256,768]{1,0:T(8,128)(2,1)S(1)} %add_convert_fusion.4), channel_id=1, source_target_pairs={{0,2},{1,3},{4,6},{5,7},{8,10},{9,11},{12,14},{13,15},{16,18},{17,... | collective-permute-start | bytes 1179656 | tf_op jit(solution)/shard_map/ppermute | solution.py:433
  56.5 17.7 %copy-start.78 = (bf16[1024,768]{1,0:T(8,128)(2,1)S(1)}, bf16[1024,768]{1,0:T(8,128)(2,1)}, u32[]{:S(2)}) copy-start(bf16[1024,768]{1,0:T(8,128)(2,1)} %param.14) | copy-start | bytes 4718596
  61.7 12.5 %collective-permute-start.7 = (bf16[256,768]{1,0:T(8,128)(2,1)S(1)}, bf16[256,768]{1,0:T(8,128)(2,1)S(1)}, u32[]{:S(2)}, u32[]{:S(2)}) collective-permute-start(bf16[256,768]{1,0:T(8,128)(2,1)S(1)} %get-tuple-element.95), channel_id=1, source_target_pairs={{0,2},{1,3},{4,6},{5,7},{8,10},{9,11},{12,14},{13,15},{16,18},{17,... | collective-permute-start | bytes 1179656 | tf_op jit(solution)/shard_map/ppermute | solution.py:433
  86.3 182.5 %copy-start.3 = (f32[2,12,128,128]{2,3,1,0:T(8,128)}, f32[2,12,128,128]{2,3,1,0:T(8,128)S(1)}, u32[]{:S(2)}) copy-start(f32[2,12,128,128]{2,3,1,0:T(8,128)S(1)} %get-tuple-element.153) | copy-start | bytes 4718596
  118.2 40.8 %copy-start.125 = (f32[256]{0:T(256)}, f32[256]{0:T(256)S(1)}, u32[]{:S(2)}) copy-start(f32[256]{0:T(256)S(1)} %add_rsqrt_fusion.3) | copy-start | bytes 3076
  118.2 12.0 %slice-start.19 = ((s8[4718592]{0:T(1024)(128)(4,1)}), s8[4194304]{0:T(1024)(128)(4,1)S(1)}, s32[]{:S(2)}) async-start(s8[4718592]{0:T(1024)(128)(4,1)} %bitcast.347), calls=%async_computation.19 | async-start | bytes 8388608
  119.5 22.4 %copy-start.25 = (bf16[256,768]{1,0:T(8,128)(2,1)}, bf16[256,768]{1,0:T(8,128)(2,1)S(1)}, u32[]{:S(2)}) copy-start(bf16[256,768]{1,0:T(8,128)(2,1)S(1)} %get-tuple-element.88) | copy-start | bytes 1179652
  119.5 25.0 %copy-start.23 = (bf16[256,768]{1,0:T(8,128)(2,1)}, bf16[256,768]{1,0:T(8,128)(2,1)S(1)}, u32[]{:S(2)}) copy-start(bf16[256,768]{1,0:T(8,128)(2,1)S(1)} %get-tuple-element.131) | copy-start | bytes 1179652
  119.5 39.5 %copy-start.63 = (f32[256,768]{1,0:T(8,128)}, f32[256,768]{1,0:T(8,128)S(1)}, u32[]{:S(2)}) copy-start(f32[256,768]{1,0:T(8,128)S(1)} %get-tuple-element.132) | copy-start | bytes 2359300
  119.5 10.7 %slice-start.20 = ((s8[4718592]{0:T(1024)(128)(4,1)}), s8[524288]{0:T(1024)(128)(4,1)S(1)}, s32[]{:S(2)}) async-start(s8[4718592]{0:T(1024)(128)(4,1)} %bitcast.347), calls=%async_computation.20 | async-start | bytes 1048576
  131.8 10.2 %copy-start.47 = (f32[256,768]{1,0:T(8,128)}, f32[256,768]{1,0:T(8,128)S(1)}, u32[]{:S(2)}) copy-start(f32[256,768]{1,0:T(8,128)S(1)} %get-tuple-element.161) | copy-start | bytes 2359300
  131.8 10.2 %copy-start.111 = (f32[256]{0:T(256)}, f32[256]{0:T(256)S(1)}, u32[]{:S(2)}) copy-start(f32[256]{0:T(256)S(1)} %broadcast_multiply_fusion.17) | copy-start | bytes 3076
  189.8 48.5 %collective-permute-start.9 = (bf16[256,768]{1,0:T(8,128)(2,1)}, bf16[256,768]{1,0:T(8,128)(2,1)}, u32[]{:S(2)}, u32[]{:S(2)}) collective-permute-start(bf16[256,768]{1,0:T(8,128)(2,1)} %fusion.107), channel_id=1, source_target_pairs={{2,0},{3,1},{6,4},{7,5},{10,8},{11,9},{14,12},{15,13},{18,16},{19,... | collective-permute-start | bytes 1179656 | tf_op jit(solution)/shard_map/ppermute | solution.py:433
  237.6 12.7 %copy-start.104 = (f32[256]{0:T(256)}, f32[256]{0:T(256)S(1)}, u32[]{:S(2)}) copy-start(f32[256]{0:T(256)S(1)} %add_rsqrt_fusion) | copy-start | bytes 3076
  238.2 12.1 %slice-start.3 = ((s8[9437184]{0:T(1024)(128)(4,1)}), s8[4194304]{0:T(1024)(128)(4,1)S(1)}, s32[]{:S(2)}) async-start(s8[9437184]{0:T(1024)(128)(4,1)} %bitcast.319), calls=%async_computation.3 | async-start | bytes 8388608
  241.4 48.3 %copy-start.7 = (f32[256,768]{1,0:T(8,128)}, f32[256,768]{1,0:T(8,128)S(1)}, u32[]{:S(2)}) copy-start(f32[256,768]{1,0:T(8,128)S(1)} %get-tuple-element.84) | copy-start | bytes 2359300
  271.0 22.3 %slice-start.15 = ((s8[6291456]{0:T(1024)(128)(4,1)}), s8[4194304]{0:T(1024)(128)(4,1)S(1)}, s32[]{:S(2)}) async-start(s8[6291456]{0:T(1024)(128)(4,1)} %bitcast.329), calls=%async_computation.15 | async-start | bytes 8388608
  272.7 17.0 %copy-start.34 = (bf16[1024,768]{1,0:T(8,128)(2,1)S(1)}, bf16[1024,768]{1,0:T(8,128)(2,1)}, u32[]{:S(2)}) copy-start(bf16[1024,768]{1,0:T(8,128)(2,1)} %param.16) | copy-start | bytes 4718596
  272.7 17.0 %copy-start.98 = (f32[256]{0:T(256)S(1)}, f32[256]{0:T(256)}, u32[]{:S(2)}) copy-start(f32[256]{0:T(256)} %copy-done.97) | copy-start | bytes 3076
  272.7 17.0 %copy-start.101 = (f32[256]{0:T(256)S(1)}, f32[256]{0:T(256)}, u32[]{:S(2)}) copy-start(f32[256]{0:T(256)} %copy-done.99) | copy-start | bytes 3076
  272.7 17.0 %copy-start.103 = (f32[256]{0:T(256)S(1)}, f32[256]{0:T(256)}, u32[]{:S(2)}) copy-start(f32[256]{0:T(256)} %convert_element_type.389) | copy-start | bytes 3076
  272.7 20.6 %slice-start.16 = ((s8[6291456]{0:T(1024)(128)(4,1)}), s8[2097152]{0:T(1024)(128)(4,1)S(1)}, s32[]{:S(2)}) async-start(s8[6291456]{0:T(1024)(128)(4,1)} %bitcast.329), calls=%async_computation.16 | async-start | bytes 4194304
  277.6 12.1 %collective-permute-start.10 = (bf16[256,768]{1,0:T(8,128)(2,1)S(1)}, bf16[256,768]{1,0:T(8,128)(2,1)S(1)}, u32[]{:S(2)}, u32[]{:S(2)}) collective-permute-start(bf16[256,768]{1,0:T(8,128)(2,1)S(1)} %get-tuple-element.177), channel_id=1, source_target_pairs={{2,0},{3,1},{6,4},{7,5},{10,8},{11,9},{14,12},{15,13},{18,16},{19,... | collective-permute-start | bytes 1179656 | tf_op jit(solution)/shard_map/ppermute | solution.py:433
  279.4 13.9 %copy-start.42 = (f32[256,3072]{1,0:T(8,128)S(1)}, f32[256,3072]{1,0:T(8,128)}, u32[]{:S(2)}) copy-start(f32[256,3072]{1,0:T(8,128)} %get-tuple-element.91) | copy-start | bytes 9437188
  289.7 10.8 %slice-start.6 = ((s8[9437184]{0:T(1024)(128)(4,1)}), s8[4194304]{0:T(1024)(128)(4,1)S(1)}, s32[]{:S(2)}) async-start(s8[9437184]{0:T(1024)(128)(4,1)} %bitcast.321), calls=%async_computation.6 | async-start | bytes 8388608
  307.3 10.1 %copy-start.132 = (f32[256]{0:T(256)}, f32[256]{0:T(256)S(1)}, u32[]{:S(2)}) copy-start(f32[256]{0:T(256)S(1)} %broadcast_multiply_fusion.10) | copy-start | bytes 3076
  347.9 11.8 %copy-start.75 = (bf16[2,128,1,12,64]{1,4,3,0,2:T(8,128)(2,1)S(1)}, bf16[2,128,1,12,64]{1,4,3,0,2:T(8,128)(2,1)}, u32[]{:S(2)}) copy-start(bf16[2,128,1,12,64]{1,4,3,0,2:T(8,128)(2,1)} %fusion.134) | copy-start | bytes 1179652
  363.4 35.2 %copy-start.29 = (bf16[2,128,3,12,64]{1,0,4,3,2:T(2,128)(2,1)}, bf16[2,128,3,12,64]{1,0,4,3,2:T(2,128)(2,1)S(1)}, u32[]{:S(2)}) copy-start(bf16[2,128,3,12,64]{1,0,4,3,2:T(2,128)(2,1)S(1)} %copy.99) | copy-start | bytes 3538948
  646.8 15.5 %slice-start.9 = ((s8[9437184]{0:T(1024)(128)(4,1)}), s8[4194304]{0:T(1024)(128)(4,1)S(1)}, s32[]{:S(2)}) async-start(s8[9437184]{0:T(1024)(128)(4,1)} %bitcast.323), calls=%async_computation.9 | async-start | bytes 8388608
  646.8 12.1 %slice-start.12 = ((bf16[32,384,384]{2,1,0:T(8,128)(2,1)}), bf16[8,384,384]{2,1,0:T(8,128)(2,1)S(1)}, s32[]{:S(2)}) async-start(bf16[32,384,384]{2,1,0:T(8,128)(2,1)} %shard_map.221), calls=%async_computation.12 | async-start | bytes 4718592 | tf_op jit(solution)/shard_map/slice | solution.py:517
  646.8 15.5 %slice-start.10 = ((s8[9437184]{0:T(1024)(128)(4,1)}), s8[4194304]{0:T(1024)(128)(4,1)S(1)}, s32[]{:S(2)}) async-start(s8[9437184]{0:T(1024)(128)(4,1)} %bitcast.323), calls=%async_computation.10 | async-start | bytes 8388608
  646.8 15.4 %slice-start.11 = ((s8[9437184]{0:T(1024)(128)(4,1)}), s8[1048576]{0:T(1024)(128)(4,1)S(1)}, s32[]{:S(2)}) async-start(s8[9437184]{0:T(1024)(128)(4,1)} %bitcast.323), calls=%async_computation.11 | async-start | bytes 2097152
  646.8 74.6 %collective-permute-start.8 = (bf16[256,768]{1,0:T(8,128)(2,1)}, bf16[256,768]{1,0:T(8,128)(2,1)}, u32[]{:S(2)}, u32[]{:S(2)}) collective-permute-start(bf16[256,768]{1,0:T(8,128)(2,1)} %get-tuple-element.130), channel_id=1, source_target_pairs={{2,0},{3,1},{6,4},{7,5},{10,8},{11,9},{14,12},{15,13},{18,16},{19,... | collective-permute-start | bytes 1179656 | tf_op jit(solution)/shard_map/ppermute | solution.py:433
  653.6 69.7 %collective-permute-start.11 = (bf16[256,768]{1,0:T(8,128)(2,1)}, bf16[256,768]{1,0:T(8,128)(2,1)}, u32[]{:S(2)}, u32[]{:S(2)}) collective-permute-start(bf16[256,768]{1,0:T(8,128)(2,1)} %fusion.110), channel_id=1, source_target_pairs={{0,2},{1,3},{4,6},{5,7},{8,10},{9,11},{12,14},{13,15},{16,18},{17,... | collective-permute-start | bytes 1179656 | tf_op jit(solution)/shard_map/ppermute | solution.py:433
  662.2 39.1 %collective-permute-start.12 = (f32[2,768]{1,0:T(2,128)}, f32[2,768]{1,0:T(2,128)}, u32[]{:S(2)}, u32[]{:S(2)}) collective-permute-start(f32[2,768]{1,0:T(2,128)} %broadcast_select_fusion.4), channel_id=1, source_target_pairs={{0,1},{1,0},{2,3},{3,2},{4,5},{5,4},{6,7},{7,6},{8,9},{9,8},{10,11... | collective-permute-start | bytes 18440 | tf_op jit(solution)/shard_map/ppermute | solution.py:433
  698.8 22.7 %copy-start.9 = (f32[256,768]{1,0:T(8,128)S(1)}, f32[256,768]{1,0:T(8,128)}, u32[]{:S(2)}) copy-start(f32[256,768]{1,0:T(8,128)} %copy-done.7) | copy-start | bytes 2359300
  698.8 24.5 %copy-start.30 = (bf16[2,128,3,12,64]{1,0,4,3,2:T(2,128)(2,1)S(1)}, bf16[2,128,3,12,64]{1,0,4,3,2:T(2,128)(2,1)}, u32[]{:S(2)}) copy-start(bf16[2,128,3,12,64]{1,0,4,3,2:T(2,128)(2,1)} %copy-done.29) | copy-start | bytes 3538948
  698.8 24.5 %copy-start.65 = (f32[256,768]{1,0:T(8,128)S(1)}, f32[256,768]{1,0:T(8,128)}, u32[]{:S(2)}) copy-start(f32[256,768]{1,0:T(8,128)} %copy-done.63) | copy-start | bytes 2359300
  698.8 24.5 %copy-start.127 = (f32[256]{0:T(256)S(1)}, f32[256]{0:T(256)}, u32[]{:S(2)}) copy-start(f32[256]{0:T(256)} %copy-done.125) | copy-start | bytes 3076
  698.8 24.5 %copy-start.131 = (f32[256]{0:T(256)S(1)}, f32[256]{0:T(256)}, u32[]{:S(2)}) copy-start(f32[256]{0:T(256)} %copy-done.130) | copy-start | bytes 3076
  698.8 24.5 %copy-start.133 = (f32[256]{0:T(256)S(1)}, f32[256]{0:T(256)}, u32[]{:S(2)}) copy-start(f32[256]{0:T(256)} %copy-done.132) | copy-start | bytes 3076
  (139 other events, 560.2 us)

commit v2 on v1

v2 whole, which is shorter than its diff:
```python
import functools

import jax
import jax.numpy as jnp
from jax import lax
from jax.experimental import pallas as pl
from jax.experimental.pallas import tpu as pltpu
from jax.sharding import PartitionSpec as P

D = 768
HEADS = 12
HEAD = D // HEADS
FF = 3072
BLOCK = 128
HALF = D // 2
PAIRS = HEADS // 2
TOKENS = 512
MICRO = 2
ROWS = TOKENS // MICRO
CHUNK = 512
CHUNKS = FF // CHUNK
SMALL = 16
PIECES = 32
PIECE = 384
SIDE = 112
RAIL = 160
WIDTH = 384
AHEAD = 6
LAG = 2
TILES = 16
SLOTS = 8

EPSILON = 1e-05
FAR = 1e30
ROOT_HALF = 0.7071067811865476
ROOT_TWO_PI = 2.5066282746310002
SCALE = HEAD**-0.5

MESH = pl.DeviceIdType.MESH
BF = jnp.bfloat16
F32 = jnp.float32


def alibi_slopes():
    closest = 1 << HEADS.bit_length() - 1
    first_slope = 2.0 ** (-8.0 / closest)
    slopes = [first_slope ** (power_index + 1) for power_index in range(closest)]
    double_slope = 2.0 ** (-8.0 / (2 * closest))
    extra_slopes = [double_slope ** (power_index + 1) for power_index in range(2 * closest)]
    return slopes + extra_slopes[0::2][: HEADS - closest]


SLOPES = alibi_slopes()


def dot(a, b):
    return jnp.dot(a, b, preferred_element_type=F32)


def dot_right(a, b):
    return lax.dot_general(a, b, (((1,), (1,)), ((), ())), preferred_element_type=F32)


def dot_left(a, b):
    return lax.dot_general(a, b, (((0,), (0,)), ((), ())), preferred_element_type=F32)


def lane_mean(x):
    return jnp.sum(x, axis=-1, keepdims=True) * (1.0 / D)


def remote(src, dst, send, recv, device):
    return pltpu.make_async_remote_copy(
        src_ref=src, dst_ref=dst, send_sem=send, recv_sem=recv, device_id=device, device_id_type=MESH
    )


def settled(ref, sem):
    pltpu.make_async_copy(ref, ref, sem).wait()


def layer_kernel(
    inputs_ref, first_ref, second_ref, segments_ref, joint_ref, mixing_ref, gated_ref, down_ref, gain_ref, bias_ref,
    first_out, second_out, input_out, middle_out, mine_out, landed_out, small_out,
    joint_w, mixing_w, gated_w, down_w, norms,
    rows, attended, out, swapped, upstream, back,
    joint_rows, probs, mixed, hidden, active, slope, both_grad,
    branch_first, branch_second, scaled_first, scaled_second, spread, columns, total, small, mixed_grad,
    load_sem, local_sem, weight_send, weight_recv, norm_sem, norm_send, norm_recv,
    ahead_send, ahead_recv, behind_send, behind_recv, swap_send, swap_recv, out_sem,
    keep_sem, give_send, give_recv,
):
    dp, section = lax.axis_index("dp"), lax.axis_index("section")
    plane, core = lax.div(section, 2), lax.rem(section, 2)
    partner = (dp, section + 1 - 2 * core)
    peer = (dp, section + 2 - 4 * plane)

    barrier = pltpu.get_barrier_semaphore()
    pl.semaphore_signal(barrier, inc=1, device_id=partner, device_id_type=MESH)
    pl.semaphore_signal(barrier, inc=1, device_id=peer, device_id_type=MESH)
    pl.semaphore_wait(barrier, 2)

    mine = pl.ds(pl.multiple_of(core * HALF, HALF), HALF)
    theirs = pl.ds(pl.multiple_of((1 - core) * HALF, HALF), HALF)

    def micro_rows(m):
        return pl.ds(pl.multiple_of(m * ROWS, ROWS), ROWS)

    def token_loads():
        copies = []
        for m in range(2):
            there = pl.ds(pl.multiple_of((2 * m + core) * (TOKENS // 2), TOKENS // 2), TOKENS // 2)
            here = pl.ds(m * (TOKENS // 2), TOKENS // 2)
            copies.append(pltpu.make_async_copy(first_ref.at[there], back.at[here], load_sem.at[2 * m]))
            copies.append(pltpu.make_async_copy(second_ref.at[there], upstream.at[here], load_sem.at[2 * m + 1]))
        return copies

    def input_loads():
        copies = []
        for m in range(2):
            there = pl.ds(pl.multiple_of((2 * m + core) * (TOKENS // 2), TOKENS // 2), TOKENS // 2)
            here = pl.ds(m * (TOKENS // 2), TOKENS // 2)
            copies.append(pltpu.make_async_copy(inputs_ref.at[there], rows.at[here], load_sem.at[4 + m]))
        return copies

    def chunk(k):
        return pl.ds(pl.multiple_of(k * CHUNK, CHUNK), CHUNK)

    def upper(k):
        return pl.ds(pl.multiple_of(FF + k * CHUNK, CHUNK), CHUNK)

    def weight_copies(which):
        if which == 0:
            return [(joint_ref, joint_w.at[mine], joint_w.at[theirs], 0), (mixing_ref, mixing_w.at[mine], mixing_w.at[theirs], 1)]
        copies = []
        for k in range(CHUNKS):
            copies.append((gated_ref.at[:, chunk(k)], gated_w.at[mine, chunk(k)], gated_w.at[theirs, chunk(k)], 2 + 2 * k))
            copies.append((gated_ref.at[:, upper(k)], gated_w.at[mine, upper(k)], gated_w.at[theirs, upper(k)], 3 + 2 * k))
            if k % 2 == 1:
                j = k // 2
                part = pl.ds(j * CHUNK, CHUNK)
                here = pl.ds(pl.multiple_of(core * (FF // 2) + j * CHUNK, CHUNK), CHUNK)
                there = pl.ds(pl.multiple_of((1 - core) * (FF // 2) + j * CHUNK, CHUNK), CHUNK)
                copies.append((down_ref.at[part], down_w.at[here], down_w.at[there], 2 + 2 * CHUNKS + j))
        return copies

    def start_weights(which):
        for source, place, _, n in weight_copies(which):
            remote(source, place, weight_send.at[n], weight_recv.at[n], partner).start()
            pltpu.make_async_copy(source, place, local_sem.at[n]).start()

    def wait_weights(which):
        for source, place, other, n in weight_copies(which):
            pltpu.make_async_copy(source, place, local_sem.at[n]).wait()
            settled(other, weight_recv.at[n])

    def wait_weights_sent(which):
        for source, place, _, n in weight_copies(which):
            remote(source, place, weight_send.at[n], weight_recv.at[n], partner).wait_send()

    norm_copies = []
    for n, source in enumerate((gain_ref, bias_ref)):
        norm_copies.append((source, norms.at[n, core], norms.at[n, 1 - core], n))
    for source, place, _, n in norm_copies:
        remote(source, place, norm_send.at[n], norm_recv.at[n], partner).start()
        pltpu.make_async_copy(source, place, norm_sem.at[n]).start()
    start_weights(0)

    @pl.when(plane == 0)
    def _():
        for copy in input_loads():
            copy.start()

    @pl.when(plane == 1)
    def _():
        for copy in token_loads():
            copy.start()

    start_weights(1)

    first = lax.broadcasted_iota(jnp.int32, (BLOCK, BLOCK), 0)
    second = lax.broadcasted_iota(jnp.int32, (BLOCK, BLOCK), 1)
    distance = jnp.abs(first - second).astype(F32)
    half_blocks = TOKENS // (2 * BLOCK)
    for b in range(TOKENS // BLOCK):
        at = (2 * (b // half_blocks) + core) * half_blocks + b % half_blocks
        across = jnp.broadcast_to(segments_ref[pl.ds(at, 1), :].astype(F32), (BLOCK, BLOCK))
        down = across.T
        spread[b] = jnp.where(across == down, distance, FAR)
        columns[pl.ds(b * BLOCK, BLOCK), :] = jnp.where(down >= 0.0, 1.0, 0.0)
    small[...] = jnp.zeros_like(small)
    small[8:9, :BLOCK] = jnp.sum(columns[...], axis=0, keepdims=True)

    lane = lax.broadcasted_iota(jnp.int32, (1, BLOCK), 1)
    low_lanes = jnp.where(lane < HEAD, 1.0, 0.0).astype(BF)
    high_lanes = jnp.where(lane < HEAD, 0.0, 1.0).astype(BF)

    def stacked(x):
        return jnp.concatenate([x * low_lanes, x * high_lanes], axis=0)

    def beside(x):
        return jnp.concatenate([x[:BLOCK], x[BLOCK:]], axis=1)

    for source, place, other, n in norm_copies:
        pltpu.make_async_copy(source, place, norm_sem.at[n]).wait()
        settled(other, norm_recv.at[n])

    def add_small(row, value):
        small[row : row + 1, :] += value

    def keep_column(r, at, value):
        columns[r] = jnp.where(lane == at, value, columns[r])

    def column(value):
        return jnp.sum(value, axis=0, keepdims=True)

    def post_norm(r, source, branch, kind, scaled_ref, result_ref):
        before = source[r].astype(F32)
        ok = columns[r, :1]
        add_small(4 + kind, column(ok * (before * before)))
        add_small(6 + kind, column(ok * (branch * branch)))
        summed = before + branch
        center = summed - lane_mean(summed)
        inverse = lax.rsqrt(lane_mean(center * center) + EPSILON)
        scaled = center * inverse
        scaled_ref[r] = scaled
        keep_column(r, 1 + kind, inverse)
        result_ref[r] = (scaled * norms[0, kind] + norms[1, kind]).astype(BF)

    def norm_back(r, grad, kind, scaled_ref):
        scaled = scaled_ref[r]
        add_small(2 * kind, column(grad * scaled))
        add_small(2 * kind + 1, column(grad))
        inner = grad * norms[0, kind]
        return columns[r, 1 + kind : 2 + kind] * (inner - lane_mean(inner) - scaled * lane_mean(inner * scaled))

    def attend(m):
        r = micro_rows(m)
        joint_rows[r] = dot(rows[r], joint_w[...]).astype(BF)
        for j in range(ROWS // BLOCK):
            b = m * (ROWS // BLOCK) + j
            at = pl.ds(pl.multiple_of(b * BLOCK, BLOCK), BLOCK)
            far = spread[b]
            for p in range(PAIRS):
                lanes = pl.ds(p * BLOCK, BLOCK)
                queries = joint_rows[at, lanes]
                keys = joint_rows[at, pl.ds(D + p * BLOCK, BLOCK)]
                values = joint_rows[at, pl.ds(2 * D + p * BLOCK, BLOCK)]
                raw = dot_right(stacked(queries), keys)
                parts = []
                for e in range(2):
                    scores = raw[e * BLOCK : (e + 1) * BLOCK] * SCALE - SLOPES[2 * p + e] * far
                    weights = jnp.exp(scores - jnp.max(scores, axis=-1, keepdims=True))
                    parts.append(weights / jnp.sum(weights, axis=-1, keepdims=True))
                soft = jnp.concatenate(parts, axis=0)
                probs[b * PAIRS + p] = soft
                mixed[at, lanes] = dot(beside(soft.astype(BF)), stacked(values)).astype(BF)
        branch = dot(mixed[r], mixing_w[...])
        post_norm(r, rows, branch, 0, scaled_first, attended)

    def feed(m):
        r = micro_rows(m)
        total[...] = jnp.zeros_like(total)

        def body(k, carry):
            gate = dot(attended[r], gated_w[:, chunk(k)])
            up = dot(attended[r], gated_w[:, upper(k)])
            normal = 0.5 + 0.5 * lax.erf(gate * ROOT_HALF)
            density = jnp.exp(-0.5 * gate * gate) * (1.0 / ROOT_TWO_PI)
            gelu = gate * normal
            low = (gelu * up).astype(BF)
            hidden[r, chunk(k)] = low
            active[r, chunk(k)] = gelu
            slope[r, chunk(k)] = up * (normal + gate * density)
            total[...] += dot(low, down_w[chunk(k)])
            return carry

        lax.fori_loop(0, CHUNKS, body, 0)
        post_norm(r, attended, total[...], 1, scaled_second, out)

    def feed_back(m, grad):
        r = micro_rows(m)
        through = norm_back(r, grad, 1, scaled_second)
        branch_second[r] = through.astype(BF)
        total[...] = through

        def body(k, carry):
            hidden_grad = dot_right(branch_second[r], down_w[chunk(k)])
            gate_grad = (hidden_grad * slope[r, chunk(k)]).astype(BF)
            up_grad = (hidden_grad * active[r, chunk(k)]).astype(BF)
            both_grad[r, chunk(k)] = gate_grad
            both_grad[r, upper(k)] = up_grad
            total[...] += dot_right(gate_grad, gated_w[:, chunk(k)]) + dot_right(up_grad, gated_w[:, upper(k)])
            return carry

        lax.fori_loop(0, CHUNKS, body, 0)

    def attend_back(m, grad):
        r = micro_rows(m)
        through = norm_back(r, grad, 0, scaled_first)
        branch_first[r] = through.astype(BF)
        total[...] = through
        mixed_grad[...] = dot_right(branch_first[r], mixing_w[...]).astype(BF)
        for j in range(ROWS // BLOCK):
            b = m * (ROWS // BLOCK) + j
            at = pl.ds(pl.multiple_of(b * BLOCK, BLOCK), BLOCK)
            for p in range(PAIRS):
                lanes = pl.ds(p * BLOCK, BLOCK)
                key_lanes, value_lanes = pl.ds(D + p * BLOCK, BLOCK), pl.ds(2 * D + p * BLOCK, BLOCK)
                queries, keys, values = joint_rows[at, lanes], joint_rows[at, key_lanes], joint_rows[at, value_lanes]
                above = stacked(mixed_grad[j * BLOCK : (j + 1) * BLOCK, p * BLOCK : (p + 1) * BLOCK])
                soft = probs[b * PAIRS + p]
                probs_grad = dot_right(above, values)
                joint_rows[at, value_lanes] = dot_left(soft.astype(BF), above).astype(BF)
                score_grad = soft * (probs_grad - jnp.sum(probs_grad * soft, axis=-1, keepdims=True))
                score_grad = score_grad.astype(BF)
                joint_rows[at, lanes] = (SCALE * dot(beside(score_grad), stacked(keys))).astype(BF)
                joint_rows[at, key_lanes] = (SCALE * dot_left(score_grad, stacked(queries))).astype(BF)
        total[...] += dot_right(joint_rows[r], joint_w[...])

    def ahead(m):
        r = micro_rows(m)
        return remote(out.at[r], rows.at[r], ahead_send.at[m], ahead_recv.at[m], peer)

    def behind(m):
        r = micro_rows(m)
        return remote(back.at[r], upstream.at[r], behind_send.at[m], behind_recv.at[m], peer)

    front, rear = pl.ds(0, TOKENS // 2), pl.ds(TOKENS // 2, TOKENS // 2)

    with jax.named_scope("first_weights"):
        wait_weights(0)

    @pl.when(plane == 0)
    def _():
        for copy in input_loads():
            copy.wait()

    def forward_step(step, carry):
        feeding = jnp.where(plane == 0, lax.div(step, MICRO), lax.rem(step, 2))
        m = jnp.where(plane == 0, lax.rem(step, MICRO), lax.div(step, 2))

        @pl.when(feeding == 0)
        def _():
            @pl.when(plane == 1)
            def _():
                with jax.named_scope("rows_wait"):
                    ahead(m).wait_recv()

            with jax.named_scope("attend"):
                attend(m)

        @pl.when(feeding == 1)
        def _():
            @pl.when(m == 0)
            def _():
                with jax.named_scope("weights"):
                    wait_weights(1)

            with jax.named_scope("feed"):
                feed(m)

            @pl.when(plane == 0)
            def _():
                ahead(m).start()

        return carry

    lax.fori_loop(0, 2 * MICRO, forward_step, 0)

    @pl.when(plane == 1)
    def _():
        remote(out.at[front], swapped, swap_send, swap_recv, peer).start()

    @pl.when(plane == 1)
    def _():
        for copy in token_loads():
            copy.wait()

    def backward_step(m, carry):
        r = micro_rows(m)

        @pl.when(plane == 0)
        def _():
            with jax.named_scope("grad_wait"):
                behind(m).wait_recv()

        @pl.when(plane == 1)
        def _():
            upstream[r] = (columns[r, :1] * upstream[r].astype(F32)).astype(BF)

        with jax.named_scope("feed_back"):
            feed_back(m, upstream[r].astype(F32))
        with jax.named_scope("attend_back"):
            attend_back(m, total[...].astype(BF).astype(F32))

        @pl.when(plane == 0)
        def _():
            back[r] = total[...].astype(BF)

        @pl.when(plane == 1)
        def _():
            back[r] = (total[...] + columns[r, :1] * back[r].astype(F32)).astype(BF)
            behind(m).start()

        return carry

    lax.fori_loop(0, MICRO, backward_step, 0)

    @pl.when(plane == 0)
    def _():
        remote(back.at[rear], swapped, swap_send, swap_recv, peer).start()

    def keep(tile, a, b, piece):
        source = gated_w.at[pl.ds(pl.multiple_of(a * PIECE, PIECE), PIECE), pl.ds(pl.multiple_of(lax.rem(tile, SLOTS) * D + b * WIDTH, WIDTH), WIDTH)]
        return pltpu.make_async_copy(source, mine_out.at[piece], keep_sem.at[piece])

    def give(tile, a, b, piece):
        source = gated_w.at[pl.ds(pl.multiple_of(a * PIECE, PIECE), PIECE), pl.ds(pl.multiple_of(lax.rem(tile, SLOTS) * D + b * WIDTH, WIDTH), WIDTH)]
        return remote(source, landed_out.at[piece], give_send.at[piece], give_recv.at[piece], partner)

    def wide(k):
        return pl.ds(pl.multiple_of(k * D, D), D)

    def finish_tile(tile):
        for b in range(2):
            @pl.when(tile < 4)
            def _(b=b):
                for a in range(2):
                    piece = lax.rem(tile, 2) * 4 + 2 * a + b

                    @pl.when(lax.div(tile, 2) == core)
                    def _(a=a, piece=piece):
                        keep(tile, a, b, piece).wait()

                    @pl.when(lax.div(tile, 2) != core)
                    def _(a=a, piece=piece):
                        give(tile, a, b, piece).wait_send()

            @pl.when(tile >= 4)
            def _(b=b):
                piece = 8 + (tile - 4) * 2 + b
                keep(tile, core, b, piece).wait()
                give(tile, 1 - core, b, piece).wait_send()

    def launch_tile(tile, value):
        @pl.when(tile >= SLOTS)
        def _():
            finish_tile(tile - SLOTS)

        gated_w[:, wide(lax.rem(tile, SLOTS))] = value.astype(BF)
        for b in range(2):
            @pl.when(tile < 4)
            def _(b=b):
                for a in range(2):
                    piece = lax.rem(tile, 2) * 4 + 2 * a + b

                    @pl.when(lax.div(tile, 2) == core)
                    def _(a=a, piece=piece):
                        keep(tile, a, b, piece).start()

                    @pl.when(lax.div(tile, 2) != core)
                    def _(a=a, piece=piece):
                        give(tile, a, b, piece).start()

            @pl.when(tile >= 4)
            def _(b=b):
                piece = 8 + (tile - 4) * 2 + b
                keep(tile, core, b, piece).start()
                give(tile, 1 - core, b, piece).start()

    def down_tile(k, carry):
        launch_tile(k, dot_left(hidden[:, wide(k)], branch_second[...]))
        return carry

    def gated_tile(k, carry):
        launch_tile(4 + k, dot_left(attended[...], both_grad[:, wide(k)]))
        return carry

    def joint_tile(k, carry):
        launch_tile(12 + k, dot_left(rows[...], joint_rows[:, wide(k)]))
        return carry

    with jax.named_scope("down_gradient"):
        lax.fori_loop(0, 4, down_tile, 0)
    with jax.named_scope("gated_gradient"):
        lax.fori_loop(0, 8, gated_tile, 0)
    with jax.named_scope("joint_gradient"):
        lax.fori_loop(0, 3, joint_tile, 0)
    launch_tile(jnp.int32(15), dot_left(mixed[...], branch_first[...]))

    def drain(tile, carry):
        finish_tile(tile)
        return carry

    lax.fori_loop(TILES - SLOTS, TILES, drain, 0)

    remote(out.at[front], swapped, swap_send, swap_recv, peer).wait_recv()

    def writes(which):
        pairs = [
            [(out.at[front], first_out), (swapped, second_out), (back.at[front], input_out), (upstream.at[front], middle_out)],
            [(rows.at[rear], first_out), (out.at[rear], second_out), (swapped, input_out), (back.at[rear], middle_out)],
        ][which]
        return [pltpu.make_async_copy(a, b, out_sem.at[n]) for n, (a, b) in enumerate(pairs)]

    for which in range(2):
        @pl.when(plane == which)
        def _(which=which):
            for copy in writes(which):
                copy.start()

    small_copy = pltpu.make_async_copy(small, small_out, out_sem.at[4])
    small_copy.start()
    small_copy.wait()
    for which in range(2):
        @pl.when(plane == which)
        def _(which=which):
            for copy in writes(which):
                copy.wait()

    remote(out.at[front], swapped, swap_send, swap_recv, peer).wait_send()
    for m in range(MICRO):
        @pl.when(plane == 0)
        def _(m=m):
            ahead(m).wait_send()

        @pl.when(plane == 1)
        def _(m=m):
            behind(m).wait_send()

    for n, (source, place, _, _) in enumerate(norm_copies):
        remote(source, place, norm_send.at[n], norm_recv.at[n], partner).wait_send()
    wait_weights_sent(0)
    wait_weights_sent(1)
    for piece in range(PIECES):
        settled(landed_out.at[piece], give_recv.at[piece])


def run_layer(inputs, first, second, segments, joint, mixing, gated, down, gain, bias):
    sems = lambda *s: pltpu.SemaphoreType.DMA(s)
    half = TOKENS // 2
    copies = 2 + 2 * CHUNKS + CHUNKS // 2
    any_spec, vmem = pl.BlockSpec(memory_space=pl.ANY), pl.BlockSpec(memory_space=pltpu.VMEM)
    rows_out = jax.ShapeDtypeStruct((half, D), BF)
    pieces = jax.ShapeDtypeStruct((PIECES, PIECE, WIDTH), BF)
    tokens = pltpu.VMEM((TOKENS, D), BF)
    return pl.pallas_call(
        layer_kernel,
        out_shape=[rows_out] * 4 + [pieces, pieces, jax.ShapeDtypeStruct((SMALL, D), F32)],
        in_specs=[any_spec] * 3 + [vmem] + [any_spec] * 6,
        out_specs=[any_spec] * 7,
        scratch_shapes=[
            pltpu.VMEM((D, 3 * D), BF), pltpu.VMEM((D, D), BF), pltpu.VMEM((D, 2 * FF), BF), pltpu.VMEM((FF, D), BF),
            pltpu.VMEM((2, 2, 1, D), F32),
            tokens, tokens, tokens, pltpu.VMEM((half, D), BF), tokens, tokens,
            pltpu.VMEM((TOKENS, 3 * D), BF),
            pltpu.VMEM((TOKENS // BLOCK * PAIRS, 2 * BLOCK, BLOCK), F32),
            tokens, pltpu.VMEM((TOKENS, FF), BF), pltpu.VMEM((TOKENS, FF), F32), pltpu.VMEM((TOKENS, FF), F32),
            pltpu.VMEM((TOKENS, 2 * FF), BF),
            tokens, tokens, pltpu.VMEM((TOKENS, D), F32), pltpu.VMEM((TOKENS, D), F32),
            pltpu.VMEM((TOKENS // BLOCK, BLOCK, BLOCK), F32), pltpu.VMEM((TOKENS, BLOCK), F32),
            pltpu.VMEM((ROWS, D), F32), pltpu.VMEM((SMALL, D), F32),
            pltpu.VMEM((ROWS, D), BF),
            sems(6), sems(copies), sems(copies), sems(copies), sems(2), sems(2), sems(2),
            sems(MICRO), sems(MICRO), sems(MICRO), sems(MICRO), pltpu.SemaphoreType.DMA, pltpu.SemaphoreType.DMA, sems(5),
            sems(PIECES), sems(PIECES), sems(PIECES),
        ],
        compiler_params=pltpu.CompilerParams(collective_id=2, has_side_effects=True, vmem_limit_bytes=62 * 2**20),
    )(inputs, first, second, segments, joint, mixing, gated, down, gain, bias)


def reduce_kernel(
    lines, mine_ref, landed_ref, small_ref, out_ref, small_out, other_out,
    total, grown, small, small_in, from_side, from_inner, from_low, from_high, from_root,
    load_sem, other_sem, store_sem, small_send, small_recv, small_load, side_send, side_recv, inner_send, inner_recv,
    up_send, low_recv, high_recv, root_send, root_recv,
    line_send, line_recv, back_send, back_recv, low_send, high_send, rail_recv,
):
    dp, section = lax.axis_index("dp"), lax.axis_index("section")
    y, z = lax.rem(dp, 2), lax.div(dp, 2)
    half = lines // 2
    mid = half - 1
    partner = (dp, section + 1 - 2 * lax.rem(section, 2))
    across = (dp + 1 - 2 * y, section)
    peer = (dp, lax.rem(section + 2, 4))
    below, above = (dp - 2, section), (dp + 2, section)
    lower = z < half
    depth = jnp.where(lower, z, lines - 1 - z)
    has_low, has_high = z > 0, z < lines - 1
    my_rows = pl.ds(pl.multiple_of(y * SIDE, 8), SIDE)
    other_rows = pl.ds(pl.multiple_of((1 - y) * SIDE, 8), SIDE)
    rail_rows = pl.ds(2 * SIDE, RAIL)
    last = PIECES - 1

    barrier = pltpu.get_barrier_semaphore()
    pl.semaphore_signal(barrier, inc=1, device_id=partner, device_id_type=MESH)
    pl.semaphore_signal(barrier, inc=1, device_id=across, device_id_type=MESH)
    pl.semaphore_signal(barrier, inc=1, device_id=peer, device_id_type=MESH)

    @pl.when(has_low)
    def _():
        pl.semaphore_signal(barrier, inc=1, device_id=below, device_id_type=MESH)

    @pl.when(has_high)
    def _():
        pl.semaphore_signal(barrier, inc=1, device_id=above, device_id_type=MESH)

    pl.semaphore_wait(barrier, 3 + has_low.astype(jnp.int32) + has_high.astype(jnp.int32))

    def load(b):
        return pltpu.make_async_copy(mine_ref.at[b], grown.at[b], load_sem.at[b])

    def load_other(b):
        return pltpu.make_async_copy(landed_ref.at[b], total.at[b], other_sem.at[b])

    def store(b):
        return pltpu.make_async_copy(total.at[b], out_ref.at[b], store_sem.at[b])

    def start_all(b, carry):
        load_other(b).start()
        load(b).start()
        return carry

    lax.fori_loop(0, AHEAD, start_all, 0)

    def add(dst, rows, b, *others):
        value = grown[b, rows].astype(jnp.float32)
        for other in others:
            value = value + other.astype(jnp.float32)
        dst[b, rows] = value.astype(jnp.bfloat16)

    def when(active, b):
        return pl.when(active & (b >= 0) & (b < PIECES))

    def root_of(b):
        odd = lax.rem(b, 2)
        return jnp.where(b < PIECES // 2, odd * (lines - 1), mid + odd)

    inward = (jnp.where(lower, dp + 2, dp - 2), section)
    outward = (jnp.where(lower, dp - 2, dp + 2), section)

    def small_copy(n, device, into=None):
        into = n if into is None else into
        return remote(small.at[n], small_in.at[into], small_send.at[n], small_recv.at[into], device)

    def small_sum(n, source, arrival):
        settled(small_in.at[arrival], small_recv.at[arrival])
        small[n] = small[source] + small_in[arrival]

    def small_steps(i):
        @pl.when(i == 2)
        def _():
            small_copy(0, partner).start()

        @pl.when(i == 4)
        def _():
            small_sum(1, 0, 0)
            small_copy(1, across).start()

        @pl.when(i == 6 + 2 * depth)
        def _():
            small_sum(2, 1, 1)

            @pl.when(depth > 0)
            def _():
                small_sum(3, 2, 2)

            @pl.when(depth == 0)
            def _():
                small[3] = small[2]

            slot = jnp.where(depth == mid, 3, 2)
            remote(small.at[3], small_in.at[slot], small_send.at[2], small_recv.at[slot], inward).start()

        @pl.when(i == 8 + 2 * (2 * mid - depth))
        def _():
            @pl.when(depth == mid)
            def _():
                small_sum(4, 3, 3)

            @pl.when(depth < mid)
            def _():
                settled(small.at[4], small_recv.at[4])

            @pl.when(depth > 0)
            def _():
                remote(small.at[4], small.at[4], small_send.at[3], small_recv.at[4], outward).start()

            remote(small.at[4], small_in.at[4], small_send.at[4], small_recv.at[5], peer).start()

    def small_finish():
        settled(small_in.at[4], small_recv.at[5])
        settled(small.at[0], small_send.at[0])
        settled(small.at[1], small_send.at[1])
        settled(small.at[3], small_send.at[2])
        settled(small.at[4], small_send.at[4])

        @pl.when(depth > 0)
        def _():
            settled(small.at[4], small_send.at[3])

        for n, (source, place) in enumerate(((small.at[4], small_out), (small_in.at[4], other_out))):
            copy = pltpu.make_async_copy(source, place, small_load.at[n])
            copy.start()
            copy.wait()

    first_small = pltpu.make_async_copy(small_ref, small.at[0], small_load.at[2])
    first_small.start()
    first_small.wait()

    def step(i, carry):
        small_steps(i)

        b1 = i - LAG * (1 + depth)

        @when(True, b1)
        def _():
            settled(from_side.at[b1], side_recv.at[b1])

            @pl.when(depth == 0)
            def _():
                add(grown, my_rows, b1, from_side[b1])

            @pl.when(depth > 0)
            def _():
                settled(from_inner.at[0, b1], inner_recv.at[0, b1])
                add(grown, my_rows, b1, from_side[b1], from_inner[0, b1])

            slot = (depth == mid).astype(jnp.int32)
            remote(
                grown.at[b1, my_rows], from_inner.at[slot, b1], inner_send.at[b1], inner_recv.at[slot, b1], inward
            ).start()

        b2 = i - LAG * (2 + mid + mid - depth)

        @when(True, b2)
        def _():
            @pl.when(depth == mid)
            def _():
                settled(from_inner.at[1, b2], inner_recv.at[1, b2])
                add(total, my_rows, b2, from_inner[1, b2])

            @pl.when(depth < mid)
            def _():
                settled(total.at[b2, my_rows], line_recv.at[b2])

            @pl.when(depth > 0)
            def _():
                remote(total.at[b2, my_rows], total.at[b2, my_rows], line_send.at[b2], line_recv.at[b2], outward).start()

            remote(total.at[b2, my_rows], total.at[b2, my_rows], back_send.at[b2], back_recv.at[b2], across).start()

        b3 = i - LAG * (3 + mid + mid - depth)

        @when(True, b3)
        def _():
            settled(total.at[b3, other_rows], back_recv.at[b3])

        for early in (True, False):
            for odd in (0, 1):
                root = (odd * (lines - 1)) if early else mid + odd
                height = max(root, lines - 1 - root)
                distance = jnp.abs(z - root)

                def mine(b, root=root):
                    return (root_of(b) == root) & (lax.rem(b + 4 * PIECES, 2) == odd)

                hop = jnp.where(z < root, z, jnp.where(z > root, lines - 1 - z, height))
                c1 = i - LAG * hop

                @when((z != root) & (hop > 0) & mine(c1), c1)
                def _(root=root, c1=c1):
                    @pl.when(z < root)
                    def _():
                        settled(from_low.at[c1], low_recv.at[c1])
                        add(grown, rail_rows, c1, from_low[c1])
                        remote(grown.at[c1, rail_rows], from_low.at[c1], up_send.at[c1], low_recv.at[c1], above).start()

                    @pl.when(z > root)
                    def _():
                        settled(from_high.at[c1], high_recv.at[c1])
                        add(grown, rail_rows, c1, from_high[c1])
                        remote(grown.at[c1, rail_rows], from_high.at[c1], up_send.at[c1], high_recv.at[c1], below).start()

                @when((z == root) & mine(c1), c1)
                def _(root=root, c1=c1):
                    if root > 0:
                        settled(from_low.at[c1], low_recv.at[c1])
                    if root < lines - 1:
                        settled(from_high.at[c1], high_recv.at[c1])
                    parts = ([from_low[c1]] if root > 0 else []) + ([from_high[c1]] if root < lines - 1 else [])
                    add(grown, rail_rows, c1, *parts)
                    remote(grown.at[c1, rail_rows], from_root.at[c1], root_send.at[c1], root_recv.at[c1], across).start()

                c2 = i - LAG * (height + 1 + distance)

                @when(mine(c2), c2)
                def _(root=root, c2=c2):
                    @pl.when(z == root)
                    def _():
                        settled(from_root.at[c2], root_recv.at[c2])
                        add(total, rail_rows, c2, from_root[c2])

                    @pl.when(z != root)
                    def _():
                        settled(total.at[c2, rail_rows], rail_recv.at[c2])

                    @pl.when(has_low & (z <= root))
                    def _():
                        remote(total.at[c2, rail_rows], total.at[c2, rail_rows], low_send.at[c2], rail_recv.at[c2], below).start()

                    @pl.when(has_high & (z >= root))
                    def _():
                        remote(total.at[c2, rail_rows], total.at[c2, rail_rows], high_send.at[c2], rail_recv.at[c2], above).start()

        b4 = i - LAG * (2 * lines - 1)

        @when(True, b4)
        def _():
            store(b4).start()

        b0 = i

        @when(True, b0)
        def _():
            @pl.when(b0 + AHEAD < PIECES)
            def _():
                start_all(b0 + AHEAD, 0)

            load(b0).wait()
            load_other(b0).wait()
            grown[b0] = (grown[b0].astype(jnp.float32) + total[b0].astype(jnp.float32)).astype(jnp.bfloat16)
            remote(grown.at[b0, other_rows], from_side.at[b0], side_send.at[b0], side_recv.at[b0], across).start()
            root = root_of(b0)

            @pl.when((z == 0) & (root != 0))
            def _():
                remote(grown.at[b0, rail_rows], from_low.at[b0], up_send.at[b0], low_recv.at[b0], above).start()

            @pl.when((z == lines - 1) & (root != lines - 1))
            def _():
                remote(grown.at[b0, rail_rows], from_high.at[b0], up_send.at[b0], high_recv.at[b0], below).start()

        return carry

    lax.fori_loop(0, PIECES + LAG * (2 * lines - 1), step, 0)

    small_finish()

    def finish(b, carry):
        store(b).wait()
        root = root_of(b)
        pltpu.make_async_copy(grown.at[b, other_rows], grown.at[b, other_rows], side_send.at[b]).wait()
        pltpu.make_async_copy(grown.at[b, my_rows], grown.at[b, my_rows], inner_send.at[b]).wait()
        pltpu.make_async_copy(total.at[b, my_rows], total.at[b, my_rows], back_send.at[b]).wait()

        @pl.when(depth > 0)
        def _():
            pltpu.make_async_copy(total.at[b, my_rows], total.at[b, my_rows], line_send.at[b]).wait()

        @pl.when(z != root)
        def _():
            pltpu.make_async_copy(grown.at[b, rail_rows], grown.at[b, rail_rows], up_send.at[b]).wait()

        @pl.when(z == root)
        def _():
            pltpu.make_async_copy(grown.at[b, rail_rows], grown.at[b, rail_rows], root_send.at[b]).wait()

        @pl.when(has_low & (z <= root))
        def _():
            pltpu.make_async_copy(total.at[b, rail_rows], total.at[b, rail_rows], low_send.at[b]).wait()

        @pl.when(has_high & (z >= root))
        def _():
            pltpu.make_async_copy(total.at[b, rail_rows], total.at[b, rail_rows], high_send.at[b]).wait()

        return carry

    lax.fori_loop(0, PIECES, finish, 0)


def reduce_gradients(lines, mine, landed, small):
    sems = lambda *s: pltpu.SemaphoreType.DMA(s or (PIECES,))
    any_spec = pl.BlockSpec(memory_space=pl.ANY)
    block = jax.ShapeDtypeStruct((SMALL, D), F32)
    return pl.pallas_call(
        functools.partial(reduce_kernel, lines),
        out_shape=[jax.ShapeDtypeStruct((PIECES, PIECE, WIDTH), BF), block, block],
        in_specs=[any_spec] * 3,
        out_specs=[any_spec] * 3,
        scratch_shapes=[
            pltpu.VMEM((PIECES, PIECE, WIDTH), BF), pltpu.VMEM((PIECES, PIECE, WIDTH), BF),
            pltpu.VMEM((5, SMALL, D), F32), pltpu.VMEM((5, SMALL, D), F32),
            pltpu.VMEM((PIECES, SIDE, WIDTH), BF), pltpu.VMEM((2, PIECES, SIDE, WIDTH), BF),
            pltpu.VMEM((PIECES, RAIL, WIDTH), BF), pltpu.VMEM((PIECES, RAIL, WIDTH), BF),
            pltpu.VMEM((PIECES, RAIL, WIDTH), BF),
            sems(), sems(), sems(), sems(5), sems(6), sems(3), sems(), sems(), sems(), sems(2, PIECES),
            sems(), sems(), sems(), sems(), sems(), sems(), sems(), sems(), sems(), sems(), sems(), sems(),
        ],
        compiler_params=pltpu.CompilerParams(collective_id=1, has_side_effects=True, vmem_limit_bytes=60 * 2**20),
    )(mine, landed, small)


def place_kernel(pieces_ref, joint_out, mixing_out, gated_out, down_out, held, wide, load_sem, store_sem):
    def place(piece):
        if piece < 8:
            return down_out.at[pl.ds(piece // 2 * PIECE, PIECE), pl.ds(piece % 2 * WIDTH, WIDTH)]
        if piece < 24:
            return gated_out.at[:, pl.ds((piece - 8) * WIDTH, WIDTH)]
        if piece < 30:
            return joint_out.at[:, pl.ds((piece - 24) * WIDTH, WIDTH)]
        return mixing_out.at[:, pl.ds((piece - 30) * WIDTH, WIDTH)]

    loads = [pltpu.make_async_copy(pieces_ref.at[p], held.at[p], load_sem.at[p]) for p in range(PIECES)]
    stores = [pltpu.make_async_copy(wide.at[p % 4], place(p), store_sem.at[p % 4]) for p in range(PIECES)]
    for load in loads:
        load.start()
    for p in range(PIECES):
        loads[p].wait()
        if p >= 4:
            stores[p - 4].wait()
        wide[p % 4] = held[p].astype(F32)
        stores[p].start()
    for p in range(PIECES - 4, PIECES):
        stores[p].wait()


def place_gradients(pieces):
    any_spec = pl.BlockSpec(memory_space=pl.ANY)
    shapes = ((HALF, 3 * D), (HALF, D), (HALF, 2 * FF), (FF // 2, D))
    return pl.pallas_call(
        place_kernel,
        out_shape=[jax.ShapeDtypeStruct(s, F32) for s in shapes],
        in_specs=[any_spec],
        out_specs=[any_spec] * 4,
        scratch_shapes=[
            pltpu.VMEM((PIECES, PIECE, WIDTH), BF), pltpu.VMEM((4, PIECE, WIDTH), F32),
            pltpu.SemaphoreType.DMA((PIECES,)), pltpu.SemaphoreType.DMA((4,)),
        ],
        compiler_params=pltpu.CompilerParams(vmem_limit_bytes=40 * 2**20),
    )(pieces)


def per_device(
    inputs, cotangent_first, cotangent_second, segment_ids,
    joint_projection, mixing_weight, gated_weight, down_weight, norm_gain, norm_bias,
):
    section = lax.axis_index("section")
    plane, core = section // 2, section % 2
    segments = segment_ids.reshape(-1, BLOCK)
    first, second, input_gradient, middle, mine, landed, small = run_layer(
        inputs, cotangent_first, cotangent_second, segments,
        joint_projection, mixing_weight, gated_weight, down_weight, norm_gain, norm_bias,
    )
    pieces, small, other = reduce_gradients(lax.axis_size("dp") // 2, mine, landed, small)
    joint, mixing, gated, down = place_gradients(pieces)
    norms = lax.dynamic_slice_in_dim(small, 2 * core, 2, 0)
    own, across = jnp.sum(small[4:8], axis=1).reshape(2, 2), jnp.sum(other[4:8], axis=1).reshape(2, 2)
    squares = jnp.where(plane == 0, jnp.concatenate([own, across], 1), jnp.concatenate([across, own], 1))
    magnitudes = jnp.sqrt(squares / (small[8, 0] * D))
    return (
        first, second, input_gradient, middle, joint, mixing, gated, down, norms[:1], norms[1:], magnitudes,
    )


def solution(mesh):
    tokens, rows = P("dp", None), P("section", None)
    return jax.shard_map(
        per_device,
        mesh=mesh,
        in_specs=(tokens, tokens, tokens, P("dp"), rows, rows, rows, rows, rows, rows),
        out_specs=(P(("dp", "section"), None),) * 4 + (rows,) * 6 + (P(),),
        check_vma=False,
    )
```

time: 741 us -> 333 us (0.45); the launches traced: 729 us -> 333 us
  matrix products: 188 us -> 0 us
  local copies, waits for them, and re-layouts: 162 us -> 9.49 us
  Pallas kernels: 182 us -> 320 us
  other arithmetic: 85.1 us -> 1.55 us
  blocking collectives: 63.9 us -> 0 us
  waiting for transfers between devices: 22.4 us -> 0 us
  starting transfers between devices: 20.9 us -> 0 us
    dot_general x60 -> x0, matrix products: 188 us -> none  [the longest x16 88.4 us: dot_right(): lax.dot_general(a, b, (((1,), (1,)), ((), ())), preferred_element_type=jn...]
    pallas_call x1 -> x3, Pallas kernels: 182 us -> 320 us  [the longest x1 185 us: reduce_gradients(): pl.pallas_call(functools.partial(reduce_kernel, lines), out_shape=[jax.Sh...]
    psum x2 -> x0, blocking collectives: 63.9 us -> none  [the longest x1 45.1 us: per_device(): stats, count = lax.psum((stats, count), ('dp', 'section'))]
    reshape x16 -> x2, local copies, waits for them, and re-layouts: 39.1 us -> 0.17 us  [the longest x1 0.08 us: per_device(): jnp.sum(small[4:8], axis=1).reshape(2, 2)]
    dynamic_slice x8 -> x0, local copies, waits for them, and re-layouts: 34.6 us -> none  [pieces(): lax.dynamic_slice_in_dim(w, which * (w.shape[0] // 2), w.shape[0] // 2, 0)]
    convert_element_type x16 -> x0, local copies, waits for them, and re-layouts: 31.2 us -> none  [the longest x4 20.5 us: per_device(): part.transpose(0, 2, 1, 3).reshape(height, width).astype(jnp.float32)]
    unnamed x354 -> x14, local copies, waits for them, and re-layouts: 36.5 us -> 6.72 us
    convert_element_type x18 -> x0, other arithmetic: 28 us -> none  [the longest x4 13.9 us: per_device(): part.transpose(0, 2, 1, 3).reshape(height, width).astype(jnp.float32)]
  transfers between devices with their start and end apart: 13 -> 0, of which waited for: 4 -> 0; matrix products, arithmetic and copies ran while one was open for 12% -> 0% of each run, Pallas kernels for 0% -> 0%
where the time goes in v2:
time: 333 us
  Pallas kernels  320 us (96%)
  local copies, waits for them, and re-layouts  9.49 us (3%)
    pallas_call x1, Pallas kernels, reduce_gradients(): pl.pallas_call(functools.partial(reduce_kernel, lines), out_shape=[jax.Sh...  185 us
    pallas_call x1, Pallas kernels, run_layer(): pl.pallas_call(layer_kernel, out_shape=[rows_out] * 4 + [pieces, pieces,...  126 us
    pallas_call x1, Pallas kernels, place_gradients(): pl.pallas_call(place_kernel, out_shape=[jax.ShapeDtypeStruct(s, F32) for...  9.64 us
    unnamed x14, local copies, waits for them, and re-layouts  6.72 us

profile of v2, /device:TPU:0, one launch (start us, length us, event | category | flops | bytes accessed | tf_op | source)
XLA Modules:
  0.0 332.7 jit_solution(13821565584708563937)
XLA Ops:
  0.6 125.8 %shard_map.185 = (bf16[256,768]{1,0:T(8,128)(2,1)}, bf16[256,768]{1,0:T(8,128)(2,1)}, bf16[256,768]{1,0:T(8,128)(2,1)}, bf16[256,768]{1,0:T(8,128)(2,1)}, bf16[3...) custom-call(bf16[1024,768]{1,0:T(8,128)(2,1)} %inputs_ref.1, ...), custom_call_target="tpu_custom_call" | custom-call | tf_op jit(solution)/shard_map/pallas_call | solution.py:548
  126.4 184.9 %shard_map.186 = (bf16[32,384,384]{2,1,0:T(8,128)(2,1)}, f32[16,768]{1,0:T(8,128)}, f32[16,768]{1,0:T(8,128)}) custom-call(bf16[32,384,384]{2,1,0:T(8,128)(2,1)} %get-tuple-element.29.mine_ref, bf16[32,384,384]{2,1,0:T(8,128)(2,1)} %get-tuple-element.30.landed_ref, f32[16,768]{1,0:T(8,128)} %get-tuple-element.31.small_ref), custom_call_target="tpu_custom_call" | custom-call | tf_op jit(solution)/shard_map/pallas_call | solution.py:887
  311.3 0.0 copy-start
  311.3 3.7 %copy-done = bf16[32,384,384]{2,1,0:T(8,128)(2,1)S(1)} copy-done((bf16[32,384,384]{2,1,0:T(8,128)(2,1)S(1)}, bf16[32,384,384]{2,1,0:T(8,128)(2,1)}, u32[]{:S(2)}) %copy-start) | copy-done | bytes 9437208
  315.1 0.0 copy-start.4
  315.1 0.0 copy-start.3
  315.1 0.0 copy-start.2
  315.1 0.0 copy-start.1
  315.1 9.6 %shard_map.187 = (f32[384,2304]{1,0:T(8,128)}, f32[384,768]{1,0:T(8,128)}, f32[384,6144]{1,0:T(8,128)}, f32[1536,768]{1,0:T(8,128)}) custom-call(bf16[32,384,384]{2,1,0:T(8,128)(2,1)S(1)} %copy-done), custom_call_target="tpu_custom_call" | custom-call | tf_op jit(solution)/shard_map/pallas_call | solution.py:932
  324.7 1.4 constant_dynamic-slice_fusion.1
  326.1 0.9 slice_reduce_fusion
  327.0 0.1 reshape.34
  327.1 0.1 reshape.35
  327.2 1.2 slice.19
  329.1 0.6 fusion.1
  329.7 0.0 copy-done.4
  329.7 0.7 copy.25
  330.5 0.0 copy-done.3
  330.5 0.7 copy.26
  331.2 0.0 copy-done.2
  331.2 0.7 copy.27
  332.0 0.0 copy-done.1
  332.0 0.7 copy.28
Async XLA Ops:
  311.3 3.7 %copy-start = (bf16[32,384,384]{2,1,0:T(8,128)(2,1)S(1)}, bf16[32,384,384]{2,1,0:T(8,128)(2,1)}, u32[]{:S(2)}) copy-start(bf16[32,384,384]{2,1,0:T(8,128)(2,1)} %get-tuple-element.32.pieces_ref) | copy-start | bytes 28311556
  315.1 14.7 %copy-start.4 = (bf16[256,768]{1,0:T(8,128)(2,1)S(1)}, bf16[256,768]{1,0:T(8,128)(2,1)}, u32[]{:S(2)}) copy-start(bf16[256,768]{1,0:T(8,128)(2,1)} %get-tuple-element.54) | copy-start | bytes 1179652
  315.1 15.4 %copy-start.3 = (bf16[256,768]{1,0:T(8,128)(2,1)S(1)}, bf16[256,768]{1,0:T(8,128)(2,1)}, u32[]{:S(2)}) copy-start(bf16[256,768]{1,0:T(8,128)(2,1)} %get-tuple-element.55) | copy-start | bytes 1179652
  315.1 16.2 %copy-start.2 = (bf16[256,768]{1,0:T(8,128)(2,1)S(1)}, bf16[256,768]{1,0:T(8,128)(2,1)}, u32[]{:S(2)}) copy-start(bf16[256,768]{1,0:T(8,128)(2,1)} %get-tuple-element.56) | copy-start | bytes 1179652
  315.1 16.9 %copy-start.1 = (bf16[256,768]{1,0:T(8,128)(2,1)S(1)}, bf16[256,768]{1,0:T(8,128)(2,1)}, u32[]{:S(2)}) copy-start(bf16[256,768]{1,0:T(8,128)(2,1)} %get-tuple-element.57) | copy-start | bytes 1179652

commit v3 on v2

v3 whole, which is shorter than its diff:
```python
import functools

import jax
import jax.numpy as jnp
from jax import lax
from jax.experimental import pallas as pl
from jax.experimental.pallas import tpu as pltpu
from jax.sharding import PartitionSpec as P

D = 768
HEADS = 12
HEAD = D // HEADS
FF = 3072
BLOCK = 128
HALF = D // 2
PAIRS = HEADS // 2
TOKENS = 512
MICRO = 2
ROWS = TOKENS // MICRO
CHUNK = 1024
PART = 512
CHUNKS = FF // CHUNK
SMALL = 16
PIECES = 32
PIECE = 384
SIDE = 112
RAIL = 160
WIDTH = 384
AHEAD = 6
LAG = 2
RING = 16
TILES = 16
SLOTS = 8

EPSILON = 1e-05
FAR = 1e30
ROOT_HALF = 0.7071067811865476
ROOT_TWO_PI = 2.5066282746310002
SCALE = HEAD**-0.5

MESH = pl.DeviceIdType.MESH
BF = jnp.bfloat16
F32 = jnp.float32


def alibi_slopes():
    closest = 1 << HEADS.bit_length() - 1
    first_slope = 2.0 ** (-8.0 / closest)
    slopes = [first_slope ** (power_index + 1) for power_index in range(closest)]
    double_slope = 2.0 ** (-8.0 / (2 * closest))
    extra_slopes = [double_slope ** (power_index + 1) for power_index in range(2 * closest)]
    return slopes + extra_slopes[0::2][: HEADS - closest]


SLOPES = alibi_slopes()


def dot(a, b):
    return jnp.dot(a, b, preferred_element_type=F32)


def dot_right(a, b):
    return lax.dot_general(a, b, (((1,), (1,)), ((), ())), preferred_element_type=F32)


def dot_left(a, b):
    return lax.dot_general(a, b, (((0,), (0,)), ((), ())), preferred_element_type=F32)


def lane_mean(x):
    return jnp.sum(x, axis=-1, keepdims=True) * (1.0 / D)


def remote(src, dst, send, recv, device):
    return pltpu.make_async_remote_copy(
        src_ref=src, dst_ref=dst, send_sem=send, recv_sem=recv, device_id=device, device_id_type=MESH
    )


def settled(ref, sem):
    pltpu.make_async_copy(ref, ref, sem).wait()


def layer_kernel(
    lines,
    inputs_ref, first_ref, second_ref, segments_ref, joint_ref, mixing_ref, gated_ref, down_ref, gain_ref, bias_ref,
    first_out, second_out, input_out, middle_out, mine_out, landed_out, pieces_out, small_out, other_out,
    joint_w, mixing_w, gated_w, down_w, norms,
    rows, attended, out, swapped, upstream, back,
    joint_rows, probs, mixed, hidden, active, slope, both_grad,
    branch_first, branch_second, scaled_first, scaled_second, spread, columns,
    total, small, small_in, mixed_grad, staged,
    load_sem, local_sem, weight_send, weight_recv, norm_sem, norm_send, norm_recv,
    ahead_send, ahead_recv, behind_send, behind_recv, swap_send, swap_recv, out_sem,
    keep_sem, give_send, give_recv, ready_sem,
    own_sem, other_sem, store_sem, small_send, small_recv, side_send, side_recv, inner_send, inner_recv,
    up_send, low_recv, high_recv, root_send, root_recv, line_send, line_recv, back_send, back_recv,
    low_send, high_send, rail_recv,
):
    dp, section = lax.axis_index("dp"), lax.axis_index("section")
    plane, core = lax.div(section, 2), lax.rem(section, 2)
    partner = (dp, section + 1 - 2 * core)
    peer = (dp, section + 2 - 4 * plane)

    y, z = lax.rem(dp, 2), lax.div(dp, 2)
    across, below, above = (dp + 1 - 2 * y, section), (dp - 2, section), (dp + 2, section)
    has_low, has_high = z > 0, z < lines - 1
    near = 1 + has_low.astype(jnp.int32) + has_high.astype(jnp.int32)

    def signal_near(semaphore):
        pl.semaphore_signal(semaphore, inc=1, device_id=across, device_id_type=MESH)

        @pl.when(has_low)
        def _():
            pl.semaphore_signal(semaphore, inc=1, device_id=below, device_id_type=MESH)

        @pl.when(has_high)
        def _():
            pl.semaphore_signal(semaphore, inc=1, device_id=above, device_id_type=MESH)

    barrier = pltpu.get_barrier_semaphore()
    pl.semaphore_signal(barrier, inc=1, device_id=partner, device_id_type=MESH)
    pl.semaphore_signal(barrier, inc=1, device_id=peer, device_id_type=MESH)
    signal_near(barrier)
    pl.semaphore_wait(barrier, 2 + near)

    mine = pl.ds(pl.multiple_of(core * HALF, HALF), HALF)
    theirs = pl.ds(pl.multiple_of((1 - core) * HALF, HALF), HALF)

    def micro_rows(m):
        return pl.ds(pl.multiple_of(m * ROWS, ROWS), ROWS)

    def token_loads():
        copies = []
        for m in range(2):
            there = pl.ds(pl.multiple_of((2 * m + core) * (TOKENS // 2), TOKENS // 2), TOKENS // 2)
            here = pl.ds(m * (TOKENS // 2), TOKENS // 2)
            copies.append(pltpu.make_async_copy(first_ref.at[there], back.at[here], load_sem.at[2 * m]))
            copies.append(pltpu.make_async_copy(second_ref.at[there], upstream.at[here], load_sem.at[2 * m + 1]))
        return copies

    def input_loads():
        copies = []
        for m in range(2):
            there = pl.ds(pl.multiple_of((2 * m + core) * (TOKENS // 2), TOKENS // 2), TOKENS // 2)
            here = pl.ds(m * (TOKENS // 2), TOKENS // 2)
            copies.append(pltpu.make_async_copy(inputs_ref.at[there], rows.at[here], load_sem.at[4 + m]))
        return copies

    def chunk(k):
        return pl.ds(pl.multiple_of(k * CHUNK, CHUNK), CHUNK)

    def upper(k):
        return pl.ds(pl.multiple_of(FF + k * CHUNK, CHUNK), CHUNK)

    def weight_copies(which):
        if which == 0:
            return [(joint_ref, joint_w.at[mine], joint_w.at[theirs], 0), (mixing_ref, mixing_w.at[mine], mixing_w.at[theirs], 1)]
        copies = []
        for k in range(CHUNKS):
            for n, columns_at in enumerate((chunk(k), upper(k))):
                copies.append((gated_ref.at[:, columns_at], gated_w.at[mine, columns_at], gated_w.at[theirs, columns_at], 2 + 2 * k + n))
            here = pl.ds(pl.multiple_of(core * (FF // 2) + k * PART, PART), PART)
            there = pl.ds(pl.multiple_of((1 - core) * (FF // 2) + k * PART, PART), PART)
            copies.append((down_ref.at[pl.ds(k * PART, PART)], down_w.at[here], down_w.at[there], 2 + 2 * CHUNKS + k))
        return copies

    def start_weights(which):
        for source, place, _, n in weight_copies(which):
            remote(source, place, weight_send.at[n], weight_recv.at[n], partner).start()
            pltpu.make_async_copy(source, place, local_sem.at[n]).start()

    def wait_weights(which):
        for source, place, other, n in weight_copies(which):
            pltpu.make_async_copy(source, place, local_sem.at[n]).wait()
            settled(other, weight_recv.at[n])

    def wait_chunk(k):
        for source, place, other, n in weight_copies(1)[3 * k : 3 * k + 2]:
            pltpu.make_async_copy(source, place, local_sem.at[n]).wait()
            settled(other, weight_recv.at[n])
        for part in (2 * k, 2 * k + 1):
            source, _, _, n = weight_copies(1)[3 * (part % CHUNKS) + 2]
            place = down_w.at[pl.ds(part * PART, PART)]

            @pl.when(core == part // CHUNKS)
            def _():
                pltpu.make_async_copy(source, place, local_sem.at[n]).wait()

            @pl.when(core != part // CHUNKS)
            def _():
                settled(place, weight_recv.at[n])

    def wait_weights_sent(which):
        for source, place, _, n in weight_copies(which):
            remote(source, place, weight_send.at[n], weight_recv.at[n], partner).wait_send()

    norm_copies = []
    for n, source in enumerate((gain_ref, bias_ref)):
        norm_copies.append((source, norms.at[n, core], norms.at[n, 1 - core], n))
    for source, place, _, n in norm_copies:
        remote(source, place, norm_send.at[n], norm_recv.at[n], partner).start()
        pltpu.make_async_copy(source, place, norm_sem.at[n]).start()
    start_weights(0)

    @pl.when(plane == 0)
    def _():
        for copy in input_loads():
            copy.start()

    @pl.when(plane == 1)
    def _():
        for copy in token_loads():
            copy.start()

    start_weights(1)

    first = lax.broadcasted_iota(jnp.int32, (BLOCK, BLOCK), 0)
    second = lax.broadcasted_iota(jnp.int32, (BLOCK, BLOCK), 1)
    distance = jnp.abs(first - second).astype(F32)
    half_blocks = TOKENS // (2 * BLOCK)
    for b in range(TOKENS // BLOCK):
        at = (2 * (b // half_blocks) + core) * half_blocks + b % half_blocks
        along = jnp.broadcast_to(segments_ref[pl.ds(at, 1), :].astype(F32), (BLOCK, BLOCK))
        down = along.T
        spread[b] = jnp.where(along == down, distance, FAR)
        columns[pl.ds(b * BLOCK, BLOCK), :] = jnp.where(down >= 0.0, 1.0, 0.0)
    small[0] = jnp.zeros_like(small[0])
    small[0, 8:9, :BLOCK] = jnp.sum(columns[...], axis=0, keepdims=True)

    lane = lax.broadcasted_iota(jnp.int32, (1, BLOCK), 1)
    low_lanes = jnp.where(lane < HEAD, 1.0, 0.0).astype(BF)
    high_lanes = jnp.where(lane < HEAD, 0.0, 1.0).astype(BF)

    def stacked(x):
        return jnp.concatenate([x * low_lanes, x * high_lanes], axis=0)

    def beside(x):
        return jnp.concatenate([x[:BLOCK], x[BLOCK:]], axis=1)

    for source, place, other, n in norm_copies:
        pltpu.make_async_copy(source, place, norm_sem.at[n]).wait()
        settled(other, norm_recv.at[n])

    def add_small(row, value):
        small[0, row : row + 1, :] += value

    def keep_column(r, at, value):
        columns[r] = jnp.where(lane == at, value, columns[r])

    def column(value):
        return jnp.sum(value, axis=0, keepdims=True)

    def post_norm(r, source, branch, kind, scaled_ref, result_ref):
        before = source[r].astype(F32)
        ok = columns[r, :1]
        add_small(4 + kind, column(ok * (before * before)))
        add_small(6 + kind, column(ok * (branch * branch)))
        summed = before + branch
        center = summed - lane_mean(summed)
        inverse = lax.rsqrt(lane_mean(center * center) + EPSILON)
        scaled = center * inverse
        scaled_ref[r] = scaled
        keep_column(r, 1 + kind, inverse)
        result_ref[r] = (scaled * norms[0, kind] + norms[1, kind]).astype(BF)

    def norm_back(r, grad, kind, scaled_ref):
        scaled = scaled_ref[r]
        add_small(2 * kind, column(grad * scaled))
        add_small(2 * kind + 1, column(grad))
        inner = grad * norms[0, kind]
        return columns[r, 1 + kind : 2 + kind] * (inner - lane_mean(inner) - scaled * lane_mean(inner * scaled))

    def in_step(units):
        units = list(units)
        while units:
            units = [u for u in units if next(u, units) is not units]

    def attend(m):
        r = micro_rows(m)
        joint_rows[r] = dot(rows[r], joint_w[...]).astype(BF)
        for j in range(ROWS // BLOCK):
            b = m * (ROWS // BLOCK) + j
            at = pl.ds(pl.multiple_of(b * BLOCK, BLOCK), BLOCK)
            far = spread[b]

            def pair(p, b=b, at=at, far=far):
                queries, keys, values = [joint_rows[at, pl.ds(n * D + p * BLOCK, BLOCK)] for n in range(3)]
                raw = dot_right(stacked(queries), keys)
                yield
                parts = []
                for e in range(2):
                    scores = raw[e * BLOCK : (e + 1) * BLOCK] * SCALE - SLOPES[2 * p + e] * far
                    weights = jnp.exp(scores - jnp.max(scores, axis=-1, keepdims=True))
                    parts.append(weights * (1.0 / jnp.sum(weights, axis=-1, keepdims=True)))
                soft = jnp.concatenate(parts, axis=0)
                probs[b * PAIRS + p] = soft
                yield
                mixed[at, pl.ds(p * BLOCK, BLOCK)] = dot(beside(soft.astype(BF)), stacked(values)).astype(BF)

            in_step([pair(p) for p in range(PAIRS)])
        branch = dot(mixed[r], mixing_w[...])
        post_norm(r, rows, branch, 0, scaled_first, attended)

    def feed(m):
        r = micro_rows(m)
        for k in range(CHUNKS):
            @pl.when(m == 0)
            def _(k=k):
                wait_chunk(k)

        branch = 0.0
        for k in range(CHUNKS):
            gate = dot(attended[r], gated_w[:, chunk(k)])
            up = dot(attended[r], gated_w[:, upper(k)])
            normal = 0.5 + 0.5 * lax.erf(gate * ROOT_HALF)
            density = jnp.exp(-0.5 * gate * gate) * (1.0 / ROOT_TWO_PI)
            gelu = gate * normal
            low = (gelu * up).astype(BF)
            hidden[r, chunk(k)] = low
            active[r, chunk(k)] = gelu.astype(BF)
            slope[r, chunk(k)] = (up * (normal + gate * density)).astype(BF)
            branch += dot(low, down_w[chunk(k)])
        total[...] = branch
        post_norm(r, attended, total[...], 1, scaled_second, out)

    def feed_back(m, grad):
        r = micro_rows(m)
        through = norm_back(r, grad, 1, scaled_second)
        branch_second[r] = through.astype(BF)
        for k in range(CHUNKS):
            hidden_grad = dot_right(branch_second[r], down_w[chunk(k)])
            gate_grad = (hidden_grad * slope[r, chunk(k)].astype(F32)).astype(BF)
            up_grad = (hidden_grad * active[r, chunk(k)].astype(F32)).astype(BF)
            both_grad[r, chunk(k)] = gate_grad
            both_grad[r, upper(k)] = up_grad
            through += dot_right(gate_grad, gated_w[:, chunk(k)]) + dot_right(up_grad, gated_w[:, upper(k)])
        total[...] = through

    def attend_back(m, grad):
        r = micro_rows(m)
        through = norm_back(r, grad, 0, scaled_first)
        branch_first[r] = through.astype(BF)
        total[...] = through
        mixed_grad[...] = dot_right(branch_first[r], mixing_w[...]).astype(BF)
        for j in range(ROWS // BLOCK):
            b = m * (ROWS // BLOCK) + j
            at = pl.ds(pl.multiple_of(b * BLOCK, BLOCK), BLOCK)

            def pair(p, b=b, j=j, at=at):
                lanes = [pl.ds(n * D + p * BLOCK, BLOCK) for n in range(3)]
                queries, keys, values = [joint_rows[at, n] for n in lanes]
                above = stacked(mixed_grad[j * BLOCK : (j + 1) * BLOCK, p * BLOCK : (p + 1) * BLOCK])
                soft = probs[b * PAIRS + p]
                probs_grad = dot_right(above, values)
                yield
                values_grad = dot_left(soft.astype(BF), above)
                score_grad = soft * (probs_grad - jnp.sum(probs_grad * soft, axis=-1, keepdims=True))
                score_grad = score_grad.astype(BF)
                yield
                queries_grad = SCALE * dot(beside(score_grad), stacked(keys))
                keys_grad = SCALE * dot_left(score_grad, stacked(queries))
                yield
                for n, grad_part in zip(lanes, (queries_grad, keys_grad, values_grad)):
                    joint_rows[at, n] = grad_part.astype(BF)

            in_step([pair(p) for p in range(PAIRS)])
        total[...] += dot_right(joint_rows[r], joint_w[...])

    def ahead(m):
        r = micro_rows(m)
        return remote(out.at[r], rows.at[r], ahead_send.at[m], ahead_recv.at[m], peer)

    def behind(m):
        r = micro_rows(m)
        return remote(back.at[r], upstream.at[r], behind_send.at[m], behind_recv.at[m], peer)

    front, rear = pl.ds(0, TOKENS // 2), pl.ds(TOKENS // 2, TOKENS // 2)

    wait_weights(0)

    @pl.when(plane == 0)
    def _():
        for copy in input_loads():
            copy.wait()

    def forward_step(step, carry):
        feeding = jnp.where(plane == 0, lax.div(step, MICRO), lax.rem(step, 2))
        m = jnp.where(plane == 0, lax.rem(step, MICRO), lax.div(step, 2))

        @pl.when(feeding == 0)
        def _():
            @pl.when(plane == 1)
            def _():
                ahead(m).wait_recv()

            attend(m)

        @pl.when(feeding == 1)
        def _():
            feed(m)

            @pl.when(plane == 0)
            def _():
                ahead(m).start()

        return carry

    lax.fori_loop(0, 2 * MICRO, forward_step, 0)

    @pl.when(plane == 1)
    def _():
        remote(out.at[front], swapped, swap_send, swap_recv, peer).start()

    @pl.when(plane == 1)
    def _():
        for copy in token_loads():
            copy.wait()

    def backward_step(m, carry):
        r = micro_rows(m)

        @pl.when(plane == 0)
        def _():
            behind(m).wait_recv()

        @pl.when(plane == 1)
        def _():
            upstream[r] = (columns[r, :1] * upstream[r].astype(F32)).astype(BF)

        feed_back(m, upstream[r].astype(F32))

        @pl.when((plane == 1) | (m < MICRO - 1))
        def _():
            attend_back(m, total[...].astype(BF).astype(F32))

            @pl.when(plane == 0)
            def _():
                back[r] = total[...].astype(BF)

            @pl.when(plane == 1)
            def _():
                back[r] = (total[...] + columns[r, :1] * back[r].astype(F32)).astype(BF)
                behind(m).start()

        return carry

    lax.fori_loop(0, MICRO, backward_step, 0)

    def last_attend_back():
        attend_back(MICRO - 1, total[...].astype(BF).astype(F32))
        back[pl.ds((MICRO - 1) * ROWS, ROWS)] = total[...].astype(BF)
        remote(back.at[rear], swapped, swap_send, swap_recv, peer).start()

    def staged_part(tile, a, b):
        return staged.at[lax.rem(tile, 2), pl.ds(pl.multiple_of(a * PIECE, PIECE), PIECE), pl.ds(b * WIDTH, WIDTH)]

    def keep(tile, a, b, piece):
        return pltpu.make_async_copy(staged_part(tile, a, b), mine_out.at[piece], keep_sem.at[piece])

    def give(tile, a, b, piece):
        return remote(staged_part(tile, a, b), landed_out.at[piece], give_send.at[piece], give_recv.at[piece], partner)

    def wide(k):
        return pl.ds(pl.multiple_of(k * D, D), D)

    def finish_tile(tile):
        for b in range(2):
            @pl.when(tile < 4)
            def _(b=b):
                for a in range(2):
                    piece = lax.rem(tile, 2) * 4 + 2 * a + b

                    @pl.when(lax.div(tile, 2) == core)
                    def _(a=a, piece=piece):
                        keep(tile, a, b, piece).wait()

                    @pl.when(lax.div(tile, 2) != core)
                    def _(a=a, piece=piece):
                        give(tile, a, b, piece).wait_send()

            @pl.when(tile >= 4)
            def _(b=b):
                piece = 8 + (tile - 4) * 2 + b
                keep(tile, core, b, piece).wait()
                give(tile, 1 - core, b, piece).wait_send()

    def launch_tile(tile, value):
        @pl.when(tile >= 2)
        def _():
            finish_tile(tile - 2)

        staged[lax.rem(tile, 2)] = value.astype(BF)
        for b in range(2):
            @pl.when(tile < 4)
            def _(b=b):
                for a in range(2):
                    piece = lax.rem(tile, 2) * 4 + 2 * a + b

                    @pl.when(lax.div(tile, 2) == core)
                    def _(a=a, piece=piece):
                        keep(tile, a, b, piece).start()

                    @pl.when(lax.div(tile, 2) != core)
                    def _(a=a, piece=piece):
                        give(tile, a, b, piece).start()

            @pl.when(tile >= 4)
            def _(b=b):
                piece = 8 + (tile - 4) * 2 + b
                keep(tile, core, b, piece).start()
                give(tile, 1 - core, b, piece).start()

    def down_tile(k, carry):
        launch_tile(k, dot_left(hidden[:, wide(k)], branch_second[...]))
        return carry

    def gated_tile(k, carry):
        launch_tile(4 + k, dot_left(attended[...], both_grad[:, wide(k)]))
        return carry

    def task(i):
        @pl.when(i < 6)
        def _():
            gated_tile(2 + i, 0)

        @pl.when((i == 6) & (plane == 0))
        def _():
            last_attend_back()

        @pl.when((i >= 7) & (i < 10))
        def _():
            launch_tile(5 + i, dot_left(rows[...], joint_rows[:, wide(i - 7)]))

        @pl.when(i == 10)
        def _():
            launch_tile(jnp.int32(TILES - 1), dot_left(mixed[...], branch_first[...]))

        @pl.when((i >= 11) & (i < 13))
        def _():
            finish_tile(TILES - 13 + i)

    lax.fori_loop(0, 4, down_tile, 0)
    lax.fori_loop(0, 2, gated_tile, 0)

    half = lines // 2
    mid = half - 1
    lower = z < half
    depth = jnp.where(lower, z, lines - 1 - z)
    inward = (jnp.where(lower, dp + 2, dp - 2), section)
    outward = (jnp.where(lower, dp - 2, dp + 2), section)
    my_side, other_side = y * SIDE, (1 - y) * SIDE
    pause = max(0, LAG * (2 * lines - 1) - (RING - 2))

    def window(ref, row, column, height):
        return ref.at[pl.ds(pl.multiple_of(row, 16), height), pl.ds(pl.multiple_of(column * WIDTH, WIDTH), WIDTH)]

    def slot(b):
        return lax.rem(b, RING)

    def grown(b, row=0, height=PIECE):
        return window(gated_w, row, slot(b), height)

    def sums(b, row=0, height=PIECE):
        return window(gated_w, PIECE + row, slot(b), height)

    def landed(b):
        return window(down_w, lax.rem(b, 8) * PIECE, 0, PIECE)

    def from_side(b):
        return window(down_w, lax.div(slot(b), 2) * PIECE + lax.rem(b, 2) * SIDE, 1, SIDE)

    def from_inner(n, b):
        return window(active, (2 * n + lax.div(slot(b), 8)) * SIDE, lax.rem(b, 8), SIDE)

    def from_low(b):
        return window(slope, lax.div(slot(b), 8) * RAIL, lax.rem(b, 8), RAIL)

    def from_high(b):
        return window(hidden, lax.div(slot(b), 8) * RAIL, lax.rem(b, 8), RAIL)

    def from_root(b):
        return window(slope, 2 * RAIL, lax.rem(lax.div(b, 2), 8), RAIL)

    def load_own(b):
        return pltpu.make_async_copy(mine_out.at[b], grown(b), own_sem.at[b])

    def load_other(b):
        return pltpu.make_async_copy(landed_out.at[b], landed(b), other_sem.at[b])

    def store(b):
        return pltpu.make_async_copy(sums(b), pieces_out.at[b], store_sem.at[b])

    def root_of(b):
        odd = lax.rem(b, 2)
        return jnp.where(b < PIECES // 2, odd * (lines - 1), mid + odd)

    def release_grown(b):
        root = root_of(b)
        settled(grown(b, other_side, SIDE), side_send.at[b])
        settled(grown(b, my_side, SIDE), inner_send.at[b])

        @pl.when(z != root)
        def _():
            settled(grown(b, 2 * SIDE, RAIL), up_send.at[b])

        @pl.when(z == root)
        def _():
            settled(grown(b, 2 * SIDE, RAIL), root_send.at[b])

    def release_sums(b):
        root = root_of(b)
        store(b).wait()
        settled(sums(b, my_side, SIDE), back_send.at[b])

        @pl.when(depth > 0)
        def _():
            settled(sums(b, my_side, SIDE), line_send.at[b])

        @pl.when(has_low & (z <= root))
        def _():
            settled(sums(b, 2 * SIDE, RAIL), low_send.at[b])

        @pl.when(has_high & (z >= root))
        def _():
            settled(sums(b, 2 * SIDE, RAIL), high_send.at[b])

    def load(b):
        @pl.when(b >= RING)
        def _():
            release_grown(b - RING)

        settled(landed_out.at[b], give_recv.at[b])
        load_own(b).start()
        load_other(b).start()

    def add(into, first, *others):
        value = first[...].astype(F32)
        for other in others:
            value = value + other[...].astype(F32)
        into[...] = value.astype(BF)

    def piece_at(j):
        if pause == 0:
            return j
        return jnp.where(j < RING, j, jnp.where(j < RING + pause, -1, j - pause))

    def when(active_now, b):
        return pl.when(active_now & (b >= 0) & (b < PIECES))

    def small_sum(n, source, arrival):
        settled(small_in.at[arrival], small_recv.at[arrival])
        small[n] = small[source] + small_in[arrival]

    def small_step(i):
        @pl.when(i == 14)
        def _():
            remote(small.at[0], small_in.at[0], small_send.at[0], small_recv.at[0], partner).start()

        @pl.when(i == 16)
        def _():
            small_sum(1, 0, 0)
            remote(small.at[1], small_in.at[1], small_send.at[1], small_recv.at[1], across).start()

        @pl.when(i == 18 + 2 * depth)
        def _():
            small_sum(2, 1, 1)

            @pl.when(depth > 0)
            def _():
                small_sum(3, 2, 2)

            @pl.when(depth == 0)
            def _():
                small[3] = small[2]

            into = jnp.where(depth == mid, 3, 2)
            remote(small.at[3], small_in.at[into], small_send.at[2], small_recv.at[into], inward).start()

        @pl.when(i == 20 + 2 * (2 * mid - depth))
        def _():
            @pl.when(depth == mid)
            def _():
                small_sum(4, 3, 3)

            @pl.when(depth < mid)
            def _():
                settled(small.at[4], small_recv.at[4])

            @pl.when(depth > 0)
            def _():
                remote(small.at[4], small.at[4], small_send.at[3], small_recv.at[4], outward).start()

            remote(small.at[4], small_in.at[4], small_send.at[4], small_recv.at[5], peer).start()

    def small_finish():
        settled(small_in.at[4], small_recv.at[5])
        settled(small.at[0], small_send.at[0])
        settled(small.at[1], small_send.at[1])
        settled(small.at[3], small_send.at[2])
        settled(small.at[4], small_send.at[4])

        @pl.when(depth > 0)
        def _():
            settled(small.at[4], small_send.at[3])

    def step(i, carry):
        small_step(i)

        b1 = piece_at(i - LAG * (1 + depth))

        @when(True, b1)
        def _():
            settled(from_side(b1), side_recv.at[b1])

            @pl.when(depth == 0)
            def _():
                add(grown(b1, my_side, SIDE), grown(b1, my_side, SIDE), from_side(b1))

            @pl.when(depth > 0)
            def _():
                settled(from_inner(0, b1), inner_recv.at[0, b1])
                add(grown(b1, my_side, SIDE), grown(b1, my_side, SIDE), from_side(b1), from_inner(0, b1))

            into = (depth == mid).astype(jnp.int32)
            remote(grown(b1, my_side, SIDE), from_inner(into, b1), inner_send.at[b1], inner_recv.at[into, b1], inward).start()

        b2 = piece_at(i - LAG * (2 + mid + mid - depth))

        @when(True, b2)
        def _():
            @pl.when(depth == mid)
            def _():
                settled(from_inner(1, b2), inner_recv.at[1, b2])
                add(sums(b2, my_side, SIDE), grown(b2, my_side, SIDE), from_inner(1, b2))

            @pl.when(depth < mid)
            def _():
                settled(sums(b2, my_side, SIDE), line_recv.at[b2])

            part = sums(b2, my_side, SIDE)

            @pl.when(depth > 0)
            def _():
                remote(part, part, line_send.at[b2], line_recv.at[b2], outward).start()

            remote(part, part, back_send.at[b2], back_recv.at[b2], across).start()

        b3 = piece_at(i - LAG * (3 + mid + mid - depth))

        @when(True, b3)
        def _():
            settled(sums(b3, other_side, SIDE), back_recv.at[b3])

        for early in (True, False):
            for odd in (0, 1):
                root = (odd * (lines - 1)) if early else mid + odd
                height = max(root, lines - 1 - root)
                distance = jnp.abs(z - root)

                def matches(b, root=root, odd=odd):
                    return (root_of(b) == root) & (lax.rem(b + 2 * PIECES, 2) == odd)

                hop = jnp.where(z < root, z, jnp.where(z > root, lines - 1 - z, height))
                c1 = piece_at(i - LAG * hop)

                @when((z != root) & (hop > 0) & matches(c1), c1)
                def _(root=root, c1=c1):
                    part = grown(c1, 2 * SIDE, RAIL)

                    @pl.when(z < root)
                    def _():
                        settled(from_low(c1), low_recv.at[c1])
                        add(part, part, from_low(c1))
                        remote(part, from_low(c1), up_send.at[c1], low_recv.at[c1], above).start()

                    @pl.when(z > root)
                    def _():
                        settled(from_high(c1), high_recv.at[c1])
                        add(part, part, from_high(c1))
                        remote(part, from_high(c1), up_send.at[c1], high_recv.at[c1], below).start()

                @when((z == root) & matches(c1), c1)
                def _(root=root, c1=c1):
                    part = grown(c1, 2 * SIDE, RAIL)
                    others = []
                    if root > 0:
                        settled(from_low(c1), low_recv.at[c1])
                        others.append(from_low(c1))
                    if root < lines - 1:
                        settled(from_high(c1), high_recv.at[c1])
                        others.append(from_high(c1))
                    add(part, part, *others)
                    remote(part, from_root(c1), root_send.at[c1], root_recv.at[c1], across).start()

                c2 = piece_at(i - LAG * (height + 1 + distance))

                @when(matches(c2), c2)
                def _(root=root, c2=c2):
                    part = sums(c2, 2 * SIDE, RAIL)

                    @pl.when(z == root)
                    def _():
                        settled(from_root(c2), root_recv.at[c2])
                        add(part, grown(c2, 2 * SIDE, RAIL), from_root(c2))

                    @pl.when(z != root)
                    def _():
                        settled(part, rail_recv.at[c2])

                    @pl.when(has_low & (z <= root))
                    def _():
                        remote(part, part, low_send.at[c2], rail_recv.at[c2], below).start()

                    @pl.when(has_high & (z >= root))
                    def _():
                        remote(part, part, high_send.at[c2], rail_recv.at[c2], above).start()

        b4 = piece_at(i - LAG * (2 * lines - 1))

        @when(True, b4)
        def _():
            store(b4).start()

        b5 = piece_at(i + AHEAD)

        @when(i > 0, b5)
        def _():
            load(b5)

        b0 = piece_at(i)

        @when(True, b0)
        def _():
            @pl.when(b0 >= RING)
            def _():
                release_sums(b0 - RING)

            load_own(b0).wait()
            load_other(b0).wait()
            add(grown(b0), grown(b0), landed(b0))
            remote(grown(b0, other_side, SIDE), from_side(b0), side_send.at[b0], side_recv.at[b0], across).start()
            part, root = grown(b0, 2 * SIDE, RAIL), root_of(b0)

            @pl.when((z == 0) & (root != 0))
            def _():
                remote(part, from_low(b0), up_send.at[b0], low_recv.at[b0], above).start()

            @pl.when((z == lines - 1) & (root != lines - 1))
            def _():
                remote(part, from_high(b0), up_send.at[b0], high_recv.at[b0], below).start()

        task(i)
        return carry

    signal_near(ready_sem)

    def first_load(b, carry):
        load(b)
        return carry

    lax.fori_loop(0, AHEAD + 1, first_load, 0)
    pl.semaphore_wait(ready_sem, near)
    lax.fori_loop(0, PIECES + pause + LAG * (2 * lines - 1), step, 0)
    small_finish()

    def release_last(b, carry):
        release_grown(b)
        release_sums(b)
        return carry

    lax.fori_loop(PIECES - RING, PIECES, release_last, 0)

    remote(out.at[front], swapped, swap_send, swap_recv, peer).wait_recv()

    def writes(which):
        pairs = [
            [(out.at[front], first_out), (swapped, second_out), (back.at[front], input_out), (upstream.at[front], middle_out)],
            [(rows.at[rear], first_out), (out.at[rear], second_out), (swapped, input_out), (back.at[rear], middle_out)],
        ][which]
        return [pltpu.make_async_copy(a, b, out_sem.at[n]) for n, (a, b) in enumerate(pairs)]

    for which in range(2):
        @pl.when(plane == which)
        def _(which=which):
            for copy in writes(which):
                copy.start()

    for n, (source, target) in enumerate(((small.at[4], small_out), (small_in.at[4], other_out))):
        small_copy = pltpu.make_async_copy(source, target, out_sem.at[4 + n])
        small_copy.start()
        small_copy.wait()

    for which in range(2):
        @pl.when(plane == which)
        def _(which=which):
            for copy in writes(which):
                copy.wait()

    remote(out.at[front], swapped, swap_send, swap_recv, peer).wait_send()
    for m in range(MICRO):
        @pl.when(plane == 0)
        def _(m=m):
            ahead(m).wait_send()

        @pl.when(plane == 1)
        def _(m=m):
            behind(m).wait_send()

    for n, (source, place, _, _) in enumerate(norm_copies):
        remote(source, place, norm_send.at[n], norm_recv.at[n], partner).wait_send()
    wait_weights_sent(0)
    wait_weights_sent(1)


def run_layer(lines, inputs, first, second, segments, joint, mixing, gated, down, gain, bias):
    sems = lambda *s: pltpu.SemaphoreType.DMA(s)
    half = TOKENS // 2
    copies = 2 + 3 * CHUNKS
    any_spec, vmem = pl.BlockSpec(memory_space=pl.ANY), pl.BlockSpec(memory_space=pltpu.VMEM)
    rows_out = jax.ShapeDtypeStruct((half, D), BF)
    pieces = jax.ShapeDtypeStruct((PIECES, PIECE, WIDTH), BF)
    block = jax.ShapeDtypeStruct((SMALL, D), F32)
    tokens, hiddens = pltpu.VMEM((TOKENS, D), BF), pltpu.VMEM((TOKENS, FF), BF)
    return pl.pallas_call(
        functools.partial(layer_kernel, lines),
        out_shape=[rows_out] * 4 + [pieces] * 3 + [block] * 2,
        in_specs=[any_spec] * 3 + [vmem] + [any_spec] * 6,
        out_specs=[any_spec] * 9,
        scratch_shapes=[
            pltpu.VMEM((D, 3 * D), BF), pltpu.VMEM((D, D), BF), pltpu.VMEM((D, 2 * FF), BF), pltpu.VMEM((FF, D), BF),
            pltpu.VMEM((2, 2, 1, D), F32),
            tokens, tokens, tokens, pltpu.VMEM((half, D), BF), tokens, tokens,
            pltpu.VMEM((TOKENS, 3 * D), BF),
            pltpu.VMEM((TOKENS // BLOCK * PAIRS, 2 * BLOCK, BLOCK), F32),
            tokens, hiddens, hiddens, hiddens, pltpu.VMEM((TOKENS, 2 * FF), BF),
            tokens, tokens, pltpu.VMEM((TOKENS, D), F32), pltpu.VMEM((TOKENS, D), F32),
            pltpu.VMEM((TOKENS // BLOCK, BLOCK, BLOCK), F32), pltpu.VMEM((TOKENS, BLOCK), F32),
            pltpu.VMEM((ROWS, D), F32), pltpu.VMEM((5, SMALL, D), F32), pltpu.VMEM((5, SMALL, D), F32),
            pltpu.VMEM((ROWS, D), BF), pltpu.VMEM((2, D, D), BF),
            sems(6), sems(copies), sems(copies), sems(copies), sems(2), sems(2), sems(2),
            sems(MICRO), sems(MICRO), sems(MICRO), sems(MICRO), pltpu.SemaphoreType.DMA, pltpu.SemaphoreType.DMA, sems(6),
            sems(PIECES), sems(PIECES), sems(PIECES), pltpu.SemaphoreType.REGULAR,
            sems(PIECES), sems(PIECES), sems(PIECES), sems(5), sems(6), sems(PIECES), sems(PIECES), sems(PIECES), sems(2, PIECES),
            sems(PIECES), sems(PIECES), sems(PIECES), sems(PIECES), sems(PIECES), sems(PIECES), sems(PIECES),
            sems(PIECES), sems(PIECES), sems(PIECES), sems(PIECES), sems(PIECES),
        ],
        compiler_params=pltpu.CompilerParams(collective_id=2, has_side_effects=True, vmem_limit_bytes=62 * 2**20),
    )(inputs, first, second, segments, joint, mixing, gated, down, gain, bias)


def place_kernel(
    pieces_ref, small_ref, other_ref, first_ref, second_ref, input_ref, middle_ref,
    first_out, second_out, input_out, middle_out, joint_out, mixing_out, gated_out, down_out, gain_out, bias_out, stats_out,
    held, wide, passed, load_sem, store_sem, pass_sem,
):
    section = lax.axis_index("section")
    plane, core = lax.div(section, 2), lax.rem(section, 2)
    loads = [pltpu.make_async_copy(pieces_ref.at[p], held.at[p], load_sem.at[p]) for p in range(PIECES)]
    for load in loads:
        load.start()
    pairs = ((first_ref, first_out), (second_ref, second_out), (input_ref, input_out), (middle_ref, middle_out))
    takes = [pltpu.make_async_copy(a, passed.at[n], pass_sem.at[n]) for n, (a, _) in enumerate(pairs)]
    passes = [pltpu.make_async_copy(passed.at[n], b, pass_sem.at[4 + n]) for n, (_, b) in enumerate(pairs)]
    for copy in takes:
        copy.start()

    def place(piece):
        if piece < 8:
            return down_out.at[pl.ds(piece // 2 * PIECE, PIECE), pl.ds(piece % 2 * WIDTH, WIDTH)]
        if piece < 24:
            return gated_out.at[:, pl.ds((piece - 8) * WIDTH, WIDTH)]
        if piece < 30:
            return joint_out.at[:, pl.ds((piece - 24) * WIDTH, WIDTH)]
        return mixing_out.at[:, pl.ds((piece - 30) * WIDTH, WIDTH)]

    stores = [pltpu.make_async_copy(wide.at[p % SLOTS], place(p), store_sem.at[p % SLOTS]) for p in range(PIECES)]
    for p in range(PIECES):
        loads[p].wait()
        if p >= SLOTS:
            stores[p - SLOTS].wait()
        wide[p % SLOTS] = held[p].astype(F32)
        stores[p].start()

    for take, copy in zip(takes, passes):
        take.wait()
        copy.start()

    gain_out[...] = small_ref[pl.ds(2 * core, 1), :]
    bias_out[...] = small_ref[pl.ds(2 * core + 1, 1), :]
    count = small_ref[8:9, :1] * D
    row = lax.broadcasted_iota(jnp.int32, (2, 4), 0)
    lane = lax.broadcasted_iota(jnp.int32, (2, 4), 1)
    stats = jnp.zeros((2, 4), F32)
    for n in range(4):
        for at, source in ((2 * plane, small_ref), (2 - 2 * plane, other_ref)):
            value = jnp.sum(source[4 + n : 5 + n, :], axis=1, keepdims=True) / count
            stats = jnp.where((row == n // 2) & (lane == at + n % 2), jnp.sqrt(value), stats)
    stats_out[...] = stats
    for p in range(PIECES - SLOTS, PIECES):
        stores[p].wait()
    for copy in passes:
        copy.wait()


def place_results(pieces, small, other, *rows):
    any_spec, vmem = pl.BlockSpec(memory_space=pl.ANY), pl.BlockSpec(memory_space=pltpu.VMEM)
    shapes = ((HALF, 3 * D), (HALF, D), (HALF, 2 * FF), (FF // 2, D), (1, D), (1, D), (2, 4))
    return pl.pallas_call(
        place_kernel,
        out_shape=[jax.ShapeDtypeStruct(r.shape, BF) for r in rows] + [jax.ShapeDtypeStruct(s, F32) for s in shapes],
        in_specs=[any_spec, vmem, vmem] + [any_spec] * 4,
        out_specs=[any_spec] * 8 + [vmem] * 3,
        scratch_shapes=[
            pltpu.VMEM((PIECES, PIECE, WIDTH), BF), pltpu.VMEM((SLOTS, PIECE, WIDTH), F32),
            pltpu.VMEM((4,) + rows[0].shape, BF),
            pltpu.SemaphoreType.DMA((PIECES,)), pltpu.SemaphoreType.DMA((SLOTS,)), pltpu.SemaphoreType.DMA((8,)),
        ],
        compiler_params=pltpu.CompilerParams(vmem_limit_bytes=61 * 2**20),
    )(pieces, small, other, *rows)


def per_device(
    inputs, cotangent_first, cotangent_second, segment_ids,
    joint_projection, mixing_weight, gated_weight, down_weight, norm_gain, norm_bias,
):
    segments = segment_ids.reshape(-1, BLOCK)
    *rows, _, _, pieces, small, other = run_layer(
        lax.axis_size("dp") // 2, inputs, cotangent_first, cotangent_second, segments,
        joint_projection, mixing_weight, gated_weight, down_weight, norm_gain, norm_bias,
    )
    return tuple(place_results(pieces, small, other, *rows))


def solution(mesh):
    tokens, rows = P("dp", None), P("section", None)
    return jax.shard_map(
        per_device,
        mesh=mesh,
        in_specs=(tokens, tokens, tokens, P("dp"), rows, rows, rows, rows, rows, rows),
        out_specs=(P(("dp", "section"), None),) * 4 + (rows,) * 6 + (P(),),
        check_vma=False,
    )
```

time: 333 us -> 290 us (0.87)
  Pallas kernels: 320 us -> 289 us
  local copies, waits for them, and re-layouts: 9.49 us -> 0 us
    pallas_call x3 -> x2, Pallas kernels: 320 us -> 289 us  [the longest x1 277 us: run_layer(): pl.pallas_call(functools.partial(layer_kernel, lines), out_shape=[rows_ou...]
    unnamed x14 -> x0, local copies, waits for them, and re-layouts: 6.72 us -> none
where the time goes in v3:
time: 290 us
  Pallas kernels  289 us (100%)
    pallas_call x1, Pallas kernels, run_layer(): pl.pallas_call(functools.partial(layer_kernel, lines), out_shape=[rows_ou...  277 us
    pallas_call x1, Pallas kernels, place_results(): pl.pallas_call(place_kernel, out_shape=[jax.ShapeDtypeStruct(r.shape, BF)...  12.1 us

profile of v3, /device:TPU:0, one launch (start us, length us, event | category | flops | bytes accessed | tf_op | source)
XLA Modules:
  0.0 289.7 jit_solution(16906919663999621898)
XLA Ops:
  0.6 276.7 %shard_map.185 = (bf16[256,768]{1,0:T(8,128)(2,1)}, bf16[256,768]{1,0:T(8,128)(2,1)}, bf16[256,768]{1,0:T(8,128)(2,1)}, bf16[256,768]{1,0:T(8,128)(2,1)}, bf16[3...) custom-call(bf16[1024,768]{1,0:T(8,128)(2,1)} %inputs_ref.1, ...), custom_call_target="tpu_custom_call" | custom-call | tf_op jit(solution)/shard_map/pallas_call | solution.py:925
  277.4 12.1 %shard_map.186 = (bf16[256,768]{1,0:T(8,128)(2,1)}, bf16[256,768]{1,0:T(8,128)(2,1)}, bf16[256,768]{1,0:T(8,128)(2,1)}, bf16[256,768]{1,0:T(8,128)(2,1)}, f32[38...) custom-call(bf16[32,384,384]{2,1,0:T(8,128)(2,1)} %get-tuple-element, ...), custom_call_target="tpu_custom_call" | custom-call | tf_op jit(solution)/shard_map/pallas_call | solution.py:1009

commit v4 on v3

--- a/solution.py
+++ b/solution.py
@@ -23,12 +23,13 @@
 SMALL = 16
 PIECES = 32
 PIECE = 384
-SIDE = 112
-RAIL = 160
+SIDE = 128
+RAIL = 128
 WIDTH = 384
-AHEAD = 6
+AHEAD = 3
 LAG = 2
 RING = 16
+BLOCKS = ROWS // BLOCK
 TILES = 16
 SLOTS = 8
 
@@ -89,13 +90,12 @@
     rows, attended, out, swapped, upstream, back,
     joint_rows, probs, mixed, hidden, active, slope, both_grad,
     branch_first, branch_second, scaled_first, scaled_second, spread, columns,
-    total, small, small_in, mixed_grad, staged,
+    total, small, small_in, mixed_grad, staged, high,
     load_sem, local_sem, weight_send, weight_recv, norm_sem, norm_send, norm_recv,
     ahead_send, ahead_recv, behind_send, behind_recv, swap_send, swap_recv, out_sem,
     keep_sem, give_send, give_recv, ready_sem,
     own_sem, other_sem, store_sem, small_send, small_recv, side_send, side_recv, inner_send, inner_recv,
-    up_send, low_recv, high_recv, root_send, root_recv, line_send, line_recv, back_send, back_recv,
-    low_send, high_send, rail_recv,
+    up_send, low_recv, high_recv, root_recv, line_send, back_send, back_recv, low_send, high_send,
 ):
     dp, section = lax.axis_index("dp"), lax.axis_index("section")
     plane, core = lax.div(section, 2), lax.rem(section, 2)
@@ -276,12 +276,30 @@
         while units:
             units = [u for u in units if next(u, units) is not units]
 
+    def block_rows(b):
+        return pl.ds(pl.multiple_of(b * BLOCK, BLOCK), BLOCK)
+
+    def ahead(b):
+        r = block_rows(b)
+        return remote(out.at[r], rows.at[r], ahead_send.at[b], ahead_recv.at[b], peer)
+
+    def behind(b):
+        r = block_rows(b)
+        return remote(back.at[r], upstream.at[r], behind_send.at[b], behind_recv.at[b], peer)
+
+    front, rear = pl.ds(0, TOKENS // 2), pl.ds(TOKENS // 2, TOKENS // 2)
+
     def attend(m):
         r = micro_rows(m)
-        joint_rows[r] = dot(rows[r], joint_w[...]).astype(BF)
-        for j in range(ROWS // BLOCK):
-            b = m * (ROWS // BLOCK) + j
-            at = pl.ds(pl.multiple_of(b * BLOCK, BLOCK), BLOCK)
+        for j in range(BLOCKS):
+            b = m * BLOCKS + j
+
+            @pl.when(plane == 1)
+            def _(b=b):
+                ahead(b).wait_recv()
+
+            at = block_rows(b)
+            joint_rows[at] = dot(rows[at], joint_w[...]).astype(BF)
             far = spread[b]
 
             def pair(p, b=b, at=at, far=far):
@@ -302,15 +320,12 @@
         branch = dot(mixed[r], mixing_w[...])
         post_norm(r, rows, branch, 0, scaled_first, attended)
 
-    def feed(m):
+    def feed(m, arriving):
         r = micro_rows(m)
-        for k in range(CHUNKS):
-            @pl.when(m == 0)
-            def _(k=k):
-                wait_chunk(k)
-
         branch = 0.0
         for k in range(CHUNKS):
+            if arriving:
+                wait_chunk(k)
             gate = dot(attended[r], gated_w[:, chunk(k)])
             up = dot(attended[r], gated_w[:, upper(k)])
             normal = 0.5 + 0.5 * lax.erf(gate * ROOT_HALF)
@@ -320,8 +335,12 @@
             hidden[r, chunk(k)] = low
             active[r, chunk(k)] = gelu.astype(BF)
             slope[r, chunk(k)] = (up * (normal + gate * density)).astype(BF)
-            branch += dot(low, down_w[chunk(k)])
-        total[...] = branch
+            if arriving:
+                total[...] = dot(low, down_w[chunk(k)]) + (total[...] if k else 0.0)
+            else:
+                branch += dot(low, down_w[chunk(k)])
+        if not arriving:
+            total[...] = branch
         post_norm(r, attended, total[...], 1, scaled_second, out)
 
     def feed_back(m, grad):
@@ -343,9 +362,9 @@
         branch_first[r] = through.astype(BF)
         total[...] = through
         mixed_grad[...] = dot_right(branch_first[r], mixing_w[...]).astype(BF)
-        for j in range(ROWS // BLOCK):
-            b = m * (ROWS // BLOCK) + j
-            at = pl.ds(pl.multiple_of(b * BLOCK, BLOCK), BLOCK)
+        for j in range(BLOCKS):
+            b = m * BLOCKS + j
+            at = block_rows(b)
 
             def pair(p, b=b, j=j, at=at):
                 lanes = [pl.ds(n * D + p * BLOCK, BLOCK) for n in range(3)]
@@ -365,17 +384,17 @@
                     joint_rows[at, n] = grad_part.astype(BF)
 
             in_step([pair(p) for p in range(PAIRS)])
-        total[...] += dot_right(joint_rows[r], joint_w[...])
-
-    def ahead(m):
-        r = micro_rows(m)
-        return remote(out.at[r], rows.at[r], ahead_send.at[m], ahead_recv.at[m], peer)
-
-    def behind(m):
-        r = micro_rows(m)
-        return remote(back.at[r], upstream.at[r], behind_send.at[m], behind_recv.at[m], peer)
-
-    front, rear = pl.ds(0, TOKENS // 2), pl.ds(TOKENS // 2, TOKENS // 2)
+            grad_rows = total[j * BLOCK : (j + 1) * BLOCK, :] + dot_right(joint_rows[at], joint_w[...])
+
+            @pl.when(plane == 0)
+            def _(at=at, grad_rows=grad_rows):
+                back[at] = grad_rows.astype(BF)
+
+            @pl.when(plane == 1)
+            def _(b=b, at=at, grad_rows=grad_rows):
+                back[at] = (grad_rows + columns[at, :1] * back[at].astype(F32)).astype(BF)
+                behind(b).start()
+
 
     wait_weights(0)
 
@@ -390,19 +409,22 @@
 
         @pl.when(feeding == 0)
         def _():
-            @pl.when(plane == 1)
-            def _():
-                ahead(m).wait_recv()
-
             attend(m)
 
         @pl.when(feeding == 1)
         def _():
-            feed(m)
+            @pl.when(m == 0)
+            def _():
+                feed(0, True)
+
+            @pl.when(m > 0)
+            def _():
+                feed(m, False)
 
             @pl.when(plane == 0)
             def _():
-                ahead(m).start()
+                for j in range(BLOCKS):
+                    ahead(m * BLOCKS + j).start()
 
         return carry
 
@@ -422,7 +444,8 @@
 
         @pl.when(plane == 0)
         def _():
-            behind(m).wait_recv()
+            for j in range(BLOCKS):
+                behind(m * BLOCKS + j).wait_recv()
 
         @pl.when(plane == 1)
         def _():
@@ -433,15 +456,6 @@
         @pl.when((plane == 1) | (m < MICRO - 1))
         def _():
             attend_back(m, total[...].astype(BF).astype(F32))
-
-            @pl.when(plane == 0)
-            def _():
-                back[r] = total[...].astype(BF)
-
-            @pl.when(plane == 1)
-            def _():
-                back[r] = (total[...] + columns[r, :1] * back[r].astype(F32)).astype(BF)
-                behind(m).start()
 
         return carry
 
@@ -449,100 +463,93 @@
 
     def last_attend_back():
         attend_back(MICRO - 1, total[...].astype(BF).astype(F32))
-        back[pl.ds((MICRO - 1) * ROWS, ROWS)] = total[...].astype(BF)
         remote(back.at[rear], swapped, swap_send, swap_recv, peer).start()
 
-    def staged_part(tile, a, b):
-        return staged.at[lax.rem(tile, 2), pl.ds(pl.multiple_of(a * PIECE, PIECE), PIECE), pl.ds(b * WIDTH, WIDTH)]
-
-    def keep(tile, a, b, piece):
-        return pltpu.make_async_copy(staged_part(tile, a, b), mine_out.at[piece], keep_sem.at[piece])
-
-    def give(tile, a, b, piece):
-        return remote(staged_part(tile, a, b), landed_out.at[piece], give_send.at[piece], give_recv.at[piece], partner)
+    def pairs(n, height):
+        tile = tile_of(n)
+        row = jnp.where(tile < 4, lax.rem(tile, 2) * D, tile * PIECE)
+        return pl.ds(pl.multiple_of(row, PIECE), height)
+
+    def half_tile(n, which):
+        return staged.at[lax.rem(n, 2), pl.ds(pl.multiple_of(which * PIECE, PIECE), PIECE)]
+
+    def keep(n, source, height):
+        return pltpu.make_async_copy(source, mine_out.at[pairs(n, height)], keep_sem.at[lax.rem(n, 2)])
+
+    def give(n, source, height):
+        unit = jnp.where(n < 4, lax.rem(tile_of(n), 2), n - 2)
+        return remote(source, landed_out.at[pairs(n, height)], give_send.at[lax.rem(n, 2)], give_recv.at[unit], partner)
 
     def wide(k):
         return pl.ds(pl.multiple_of(k * D, D), D)
 
-    def finish_tile(tile):
-        for b in range(2):
-            @pl.when(tile < 4)
-            def _(b=b):
-                for a in range(2):
-                    piece = lax.rem(tile, 2) * 4 + 2 * a + b
-
-                    @pl.when(lax.div(tile, 2) == core)
-                    def _(a=a, piece=piece):
-                        keep(tile, a, b, piece).wait()
-
-                    @pl.when(lax.div(tile, 2) != core)
-                    def _(a=a, piece=piece):
-                        give(tile, a, b, piece).wait_send()
-
-            @pl.when(tile >= 4)
-            def _(b=b):
-                piece = 8 + (tile - 4) * 2 + b
-                keep(tile, core, b, piece).wait()
-                give(tile, 1 - core, b, piece).wait_send()
-
-    def launch_tile(tile, value):
-        @pl.when(tile >= 2)
-        def _():
-            finish_tile(tile - 2)
-
-        staged[lax.rem(tile, 2)] = value.astype(BF)
-        for b in range(2):
-            @pl.when(tile < 4)
-            def _(b=b):
-                for a in range(2):
-                    piece = lax.rem(tile, 2) * 4 + 2 * a + b
-
-                    @pl.when(lax.div(tile, 2) == core)
-                    def _(a=a, piece=piece):
-                        keep(tile, a, b, piece).start()
-
-                    @pl.when(lax.div(tile, 2) != core)
-                    def _(a=a, piece=piece):
-                        give(tile, a, b, piece).start()
-
-            @pl.when(tile >= 4)
-            def _(b=b):
-                piece = 8 + (tile - 4) * 2 + b
-                keep(tile, core, b, piece).start()
-                give(tile, 1 - core, b, piece).start()
-
-    def down_tile(k, carry):
-        launch_tile(k, dot_left(hidden[:, wide(k)], branch_second[...]))
-        return carry
-
-    def gated_tile(k, carry):
-        launch_tile(4 + k, dot_left(attended[...], both_grad[:, wide(k)]))
-        return carry
+    def tile_of(n):
+        return n + (n == 1).astype(jnp.int32) - (n == 2).astype(jnp.int32)
+
+    def each_part(n, kept, given):
+        tile = tile_of(n)
+
+        @pl.when((tile < 4) & (lax.div(tile, 2) == core))
+        def _():
+            kept(keep(n, staged.at[lax.rem(n, 2)], D))
+
+        @pl.when((tile < 4) & (lax.div(tile, 2) != core))
+        def _():
+            given(give(n, staged.at[lax.rem(n, 2)], D))
+
+        @pl.when(tile >= 4)
+        def _():
+            kept(keep(n, half_tile(n, core), PIECE))
+            given(give(n, half_tile(n, 1 - core), PIECE))
+
+    def finish(n):
+        each_part(n, lambda copy: copy.wait(), lambda copy: copy.wait_send())
+
+    def launch(n, value):
+        staged[lax.rem(n, 2)] = value.astype(BF)
+        each_part(n, lambda copy: copy.start(), lambda copy: copy.start())
+
+    def down_tile(n):
+        launch(n, dot_left(hidden[:, wide(tile_of(n))], branch_second[...]))
 
     def task(i):
-        @pl.when(i < 6)
-        def _():
-            gated_tile(2 + i, 0)
-
-        @pl.when((i == 6) & (plane == 0))
+        n = i + 3
+
+        @pl.when(i == 0)
+        def _():
+            down_tile(n)
+            finish(n - 1)
+
+        @pl.when((i > 0) & (i < 9))
+        def _():
+            launch(n, dot_left(attended[...], both_grad[:, wide(n - 4)]))
+            finish(n - 1)
+
+        @pl.when((i == 9) & (plane == 0))
         def _():
             last_attend_back()
 
-        @pl.when((i >= 7) & (i < 10))
-        def _():
-            launch_tile(5 + i, dot_left(rows[...], joint_rows[:, wide(i - 7)]))
-
-        @pl.when(i == 10)
-        def _():
-            launch_tile(jnp.int32(TILES - 1), dot_left(mixed[...], branch_first[...]))
-
-        @pl.when((i >= 11) & (i < 13))
-        def _():
-            finish_tile(TILES - 13 + i)
-
-    lax.fori_loop(0, 4, down_tile, 0)
-    lax.fori_loop(0, 2, gated_tile, 0)
-
+        @pl.when((i >= 10) & (i < 13))
+        def _():
+            launch(n - 1, dot_left(rows[...], joint_rows[:, wide(n - 13)]))
+            finish(n - 2)
+
+        @pl.when(i == 13)
+        def _():
+            launch(n - 1, dot_left(mixed[...], branch_first[...]))
+            finish(n - 2)
+
+        @pl.when(i == 14)
+        def _():
+            finish(n - 2)
+
+    signal_near(ready_sem)
+    down_first = [jnp.int32(n) for n in range(3)]
+    down_tile(down_first[0])
+    down_tile(down_first[1])
+    finish(down_first[0])
+    down_tile(down_first[2])
+    finish(down_first[1])
     half = lines // 2
     mid = half - 1
     lower = z < half
@@ -577,19 +584,23 @@
         return window(slope, lax.div(slot(b), 8) * RAIL, lax.rem(b, 8), RAIL)
 
     def from_high(b):
-        return window(hidden, lax.div(slot(b), 8) * RAIL, lax.rem(b, 8), RAIL)
+        return high.at[slot(b)]
 
     def from_root(b):
         return window(slope, 2 * RAIL, lax.rem(lax.div(b, 2), 8), RAIL)
 
+    def from_pair(ref, b):
+        row = pl.multiple_of(lax.div(b, 2) * PIECE, PIECE)
+        return ref.at[pl.ds(row, PIECE), pl.ds(pl.multiple_of(lax.rem(b, 2) * WIDTH, WIDTH), WIDTH)]
+
     def load_own(b):
-        return pltpu.make_async_copy(mine_out.at[b], grown(b), own_sem.at[b])
+        return pltpu.make_async_copy(from_pair(mine_out, b), grown(b), own_sem.at[lax.rem(b, AHEAD + 1)])
 
     def load_other(b):
-        return pltpu.make_async_copy(landed_out.at[b], landed(b), other_sem.at[b])
+        return pltpu.make_async_copy(from_pair(landed_out, b), landed(b), other_sem.at[lax.rem(b, AHEAD + 1)])
 
     def store(b):
-        return pltpu.make_async_copy(sums(b), pieces_out.at[b], store_sem.at[b])
+        return pltpu.make_async_copy(sums(b), pieces_out.at[b], store_sem.at[slot(b)])
 
     def root_of(b):
         odd = lax.rem(b, 2)
@@ -597,40 +608,47 @@
 
     def release_grown(b):
         root = root_of(b)
-        settled(grown(b, other_side, SIDE), side_send.at[b])
-        settled(grown(b, my_side, SIDE), inner_send.at[b])
+        settled(grown(b, other_side, SIDE), side_send.at[slot(b)])
+        settled(grown(b, my_side, SIDE), inner_send.at[slot(b)])
 
         @pl.when(z != root)
         def _():
-            settled(grown(b, 2 * SIDE, RAIL), up_send.at[b])
+            settled(grown(b, 2 * SIDE, RAIL), up_send.at[slot(b)])
 
         @pl.when(z == root)
         def _():
-            settled(grown(b, 2 * SIDE, RAIL), root_send.at[b])
+            settled(grown(b, 2 * SIDE, RAIL), up_send.at[slot(b)])
 
     def release_sums(b):
         root = root_of(b)
         store(b).wait()
-        settled(sums(b, my_side, SIDE), back_send.at[b])
+        settled(sums(b, my_side, SIDE), back_send.at[slot(b)])
 
         @pl.when(depth > 0)
         def _():
-            settled(sums(b, my_side, SIDE), line_send.at[b])
+            settled(sums(b, my_side, SIDE), line_send.at[slot(b)])
 
         @pl.when(has_low & (z <= root))
         def _():
-            settled(sums(b, 2 * SIDE, RAIL), low_send.at[b])
+            settled(sums(b, 2 * SIDE, RAIL), low_send.at[slot(b)])
 
         @pl.when(has_high & (z >= root))
         def _():
-            settled(sums(b, 2 * SIDE, RAIL), high_send.at[b])
+            settled(sums(b, 2 * SIDE, RAIL), high_send.at[slot(b)])
 
     def load(b):
         @pl.when(b >= RING)
         def _():
             release_grown(b - RING)
 
-        settled(landed_out.at[b], give_recv.at[b])
+        @pl.when((b < 8) & (lax.rem(b, 4) == 0))
+        def _():
+            settled(landed_out.at[pl.ds(0, D)], give_recv.at[lax.div(b, 4)])
+
+        @pl.when((b >= 8) & (lax.rem(b, 2) == 0))
+        def _():
+            settled(landed_out.at[pl.ds(0, PIECE)], give_recv.at[lax.div(b, 2) - 2])
+
         load_own(b).start()
         load_other(b).start()
 
@@ -711,7 +729,7 @@
 
         @when(True, b1)
         def _():
-            settled(from_side(b1), side_recv.at[b1])
+            settled(from_side(b1), side_recv.at[slot(b1)])
 
             @pl.when(depth == 0)
             def _():
@@ -719,11 +737,11 @@
 
             @pl.when(depth > 0)
             def _():
-                settled(from_inner(0, b1), inner_recv.at[0, b1])
+                settled(from_inner(0, b1), inner_recv.at[0, slot(b1)])
                 add(grown(b1, my_side, SIDE), grown(b1, my_side, SIDE), from_side(b1), from_inner(0, b1))
 
             into = (depth == mid).astype(jnp.int32)
-            remote(grown(b1, my_side, SIDE), from_inner(into, b1), inner_send.at[b1], inner_recv.at[into, b1], inward).start()
+            remote(grown(b1, my_side, SIDE), from_inner(into, b1), inner_send.at[slot(b1)], inner_recv.at[into, slot(b1)], inward).start()
 
         b2 = piece_at(i - LAG * (2 + mid + mid - depth))
 
@@ -731,26 +749,26 @@
         def _():
             @pl.when(depth == mid)
             def _():
-                settled(from_inner(1, b2), inner_recv.at[1, b2])
+                settled(from_inner(1, b2), inner_recv.at[1, slot(b2)])
                 add(sums(b2, my_side, SIDE), grown(b2, my_side, SIDE), from_inner(1, b2))
 
             @pl.when(depth < mid)
             def _():
-                settled(sums(b2, my_side, SIDE), line_recv.at[b2])
+                settled(sums(b2, my_side, SIDE), inner_recv.at[1, slot(b2)])
 
             part = sums(b2, my_side, SIDE)
 
             @pl.when(depth > 0)
             def _():
-                remote(part, part, line_send.at[b2], line_recv.at[b2], outward).start()
-
-            remote(part, part, back_send.at[b2], back_recv.at[b2], across).start()
+                remote(part, part, line_send.at[slot(b2)], inner_recv.at[1, slot(b2)], outward).start()
+
+            remote(part, part, back_send.at[slot(b2)], back_recv.at[slot(b2)], across).start()
 
         b3 = piece_at(i - LAG * (3 + mid + mid - depth))
 
         @when(True, b3)
         def _():
-            settled(sums(b3, other_side, SIDE), back_recv.at[b3])
+            settled(sums(b3, other_side, SIDE), back_recv.at[slot(b3)])
 
         for early in (True, False):
             for odd in (0, 1):
@@ -770,28 +788,28 @@
 
                     @pl.when(z < root)
                     def _():
-                        settled(from_low(c1), low_recv.at[c1])
+                        settled(from_low(c1), low_recv.at[slot(c1)])
                         add(part, part, from_low(c1))
-                        remote(part, from_low(c1), up_send.at[c1], low_recv.at[c1], above).start()
+                        remote(part, from_low(c1), up_send.at[slot(c1)], low_recv.at[slot(c1)], above).start()
 
                     @pl.when(z > root)
                     def _():
-                        settled(from_high(c1), high_recv.at[c1])
+                        settled(from_high(c1), high_recv.at[slot(c1)])
                         add(part, part, from_high(c1))
-                        remote(part, from_high(c1), up_send.at[c1], high_recv.at[c1], below).start()
+                        remote(part, from_high(c1), up_send.at[slot(c1)], high_recv.at[slot(c1)], below).start()
 
                 @when((z == root) & matches(c1), c1)
                 def _(root=root, c1=c1):
                     part = grown(c1, 2 * SIDE, RAIL)
                     others = []
                     if root > 0:
-                        settled(from_low(c1), low_recv.at[c1])
+                        settled(from_low(c1), low_recv.at[slot(c1)])
                         others.append(from_low(c1))
                     if root < lines - 1:
-                        settled(from_high(c1), high_recv.at[c1])
+                        settled(from_high(c1), high_recv.at[slot(c1)])
                         others.append(from_high(c1))
                     add(part, part, *others)
-                    remote(part, from_root(c1), root_send.at[c1], root_recv.at[c1], across).start()
+                    remote(part, from_root(c1), up_send.at[slot(c1)], root_recv.at[slot(c1)], across).start()
 
                 c2 = piece_at(i - LAG * (height + 1 + distance))
 
@@ -801,32 +819,26 @@
 
                     @pl.when(z == root)
                     def _():
-                        settled(from_root(c2), root_recv.at[c2])
+                        settled(from_root(c2), root_recv.at[slot(c2)])
                         add(part, grown(c2, 2 * SIDE, RAIL), from_root(c2))
 
                     @pl.when(z != root)
                     def _():
-                        settled(part, rail_recv.at[c2])
+                        settled(part, root_recv.at[slot(c2)])
 
                     @pl.when(has_low & (z <= root))
                     def _():
-                        remote(part, part, low_send.at[c2], rail_recv.at[c2], below).start()
+                        remote(part, part, low_send.at[slot(c2)], root_recv.at[slot(c2)], below).start()
 
                     @pl.when(has_high & (z >= root))
                     def _():
-                        remote(part, part, high_send.at[c2], rail_recv.at[c2], above).start()
+                        remote(part, part, high_send.at[slot(c2)], root_recv.at[slot(c2)], above).start()
 
         b4 = piece_at(i - LAG * (2 * lines - 1))
 
         @when(True, b4)
         def _():
             store(b4).start()
-
-        b5 = piece_at(i + AHEAD)
-
-        @when(i > 0, b5)
-        def _():
-            load(b5)
 
         b0 = piece_at(i)
 
@@ -839,21 +851,25 @@
             load_own(b0).wait()
             load_other(b0).wait()
             add(grown(b0), grown(b0), landed(b0))
-            remote(grown(b0, other_side, SIDE), from_side(b0), side_send.at[b0], side_recv.at[b0], across).start()
+            remote(grown(b0, other_side, SIDE), from_side(b0), side_send.at[slot(b0)], side_recv.at[slot(b0)], across).start()
             part, root = grown(b0, 2 * SIDE, RAIL), root_of(b0)
 
             @pl.when((z == 0) & (root != 0))
             def _():
-                remote(part, from_low(b0), up_send.at[b0], low_recv.at[b0], above).start()
+                remote(part, from_low(b0), up_send.at[slot(b0)], low_recv.at[slot(b0)], above).start()
 
             @pl.when((z == lines - 1) & (root != lines - 1))
             def _():
-                remote(part, from_high(b0), up_send.at[b0], high_recv.at[b0], below).start()
+                remote(part, from_high(b0), up_send.at[slot(b0)], high_recv.at[slot(b0)], below).start()
 
         task(i)
+        b5 = piece_at(i + AHEAD)
+
+        @when(i > 0, b5)
+        def _():
+            load(b5)
+
         return carry
-
-    signal_near(ready_sem)
 
     def first_load(b, carry):
         load(b)
@@ -898,14 +914,14 @@
                 copy.wait()
 
     remote(out.at[front], swapped, swap_send, swap_recv, peer).wait_send()
-    for m in range(MICRO):
+    for b in range(TOKENS // BLOCK):
         @pl.when(plane == 0)
-        def _(m=m):
-            ahead(m).wait_send()
+        def _(b=b):
+            ahead(b).wait_send()
 
         @pl.when(plane == 1)
-        def _(m=m):
-            behind(m).wait_send()
+        def _(b=b):
+            behind(b).wait_send()
 
     for n, (source, place, _, _) in enumerate(norm_copies):
         remote(source, place, norm_send.at[n], norm_recv.at[n], partner).wait_send()
@@ -917,14 +933,16 @@
     sems = lambda *s: pltpu.SemaphoreType.DMA(s)
     half = TOKENS // 2
     copies = 2 + 3 * CHUNKS
+    ring = sems(RING)
     any_spec, vmem = pl.BlockSpec(memory_space=pl.ANY), pl.BlockSpec(memory_space=pltpu.VMEM)
     rows_out = jax.ShapeDtypeStruct((half, D), BF)
     pieces = jax.ShapeDtypeStruct((PIECES, PIECE, WIDTH), BF)
+    paired = jax.ShapeDtypeStruct((PIECES // 2 * PIECE, 2 * WIDTH), BF)
     block = jax.ShapeDtypeStruct((SMALL, D), F32)
     tokens, hiddens = pltpu.VMEM((TOKENS, D), BF), pltpu.VMEM((TOKENS, FF), BF)
     return pl.pallas_call(
         functools.partial(layer_kernel, lines),
-        out_shape=[rows_out] * 4 + [pieces] * 3 + [block] * 2,
+        out_shape=[rows_out] * 4 + [paired] * 2 + [pieces] + [block] * 2,
         in_specs=[any_spec] * 3 + [vmem] + [any_spec] * 6,
         out_specs=[any_spec] * 9,
         scratch_shapes=[
@@ -937,13 +955,12 @@
             tokens, tokens, pltpu.VMEM((TOKENS, D), F32), pltpu.VMEM((TOKENS, D), F32),
             pltpu.VMEM((TOKENS // BLOCK, BLOCK, BLOCK), F32), pltpu.VMEM((TOKENS, BLOCK), F32),
             pltpu.VMEM((ROWS, D), F32), pltpu.VMEM((5, SMALL, D), F32), pltpu.VMEM((5, SMALL, D), F32),
-            pltpu.VMEM((ROWS, D), BF), pltpu.VMEM((2, D, D), BF),
+            pltpu.VMEM((ROWS, D), BF), pltpu.VMEM((2, D, D), BF), pltpu.VMEM((RING, RAIL, WIDTH), BF),
             sems(6), sems(copies), sems(copies), sems(copies), sems(2), sems(2), sems(2),
-            sems(MICRO), sems(MICRO), sems(MICRO), sems(MICRO), pltpu.SemaphoreType.DMA, pltpu.SemaphoreType.DMA, sems(6),
-            sems(PIECES), sems(PIECES), sems(PIECES), pltpu.SemaphoreType.REGULAR,
-            sems(PIECES), sems(PIECES), sems(PIECES), sems(5), sems(6), sems(PIECES), sems(PIECES), sems(PIECES), sems(2, PIECES),
-            sems(PIECES), sems(PIECES), sems(PIECES), sems(PIECES), sems(PIECES), sems(PIECES), sems(PIECES),
-            sems(PIECES), sems(PIECES), sems(PIECES), sems(PIECES), sems(PIECES),
+            sems(4), sems(4), sems(4), sems(4), pltpu.SemaphoreType.DMA, pltpu.SemaphoreType.DMA, sems(6),
+            sems(2), sems(2), sems(TILES - 2), pltpu.SemaphoreType.REGULAR,
+            sems(AHEAD + 1), sems(AHEAD + 1), ring, sems(5), sems(6), ring, ring, ring, sems(2, RING),
+            ring, ring, ring, ring, ring, ring, ring, ring, ring,
         ],
         compiler_params=pltpu.CompilerParams(collective_id=2, has_side_effects=True, vmem_limit_bytes=62 * 2**20),
     )(inputs, first, second, segments, joint, mixing, gated, down, gain, bias)

time: 290 us -> 269 us (0.928)
  Pallas kernels: 289 us -> 267 us
    pallas_call x1, Pallas kernels: 277 us -> 255 us  [run_layer(): pl.pallas_call(functools.partial(layer_kernel, lines), out_shape=[rows_ou...]
where the time goes in v4:
time: 269 us; the launch traced here: 268 us
  Pallas kernels  267 us (99%)
    pallas_call x1, Pallas kernels, run_layer(): pl.pallas_call(functools.partial(layer_kernel, lines), out_shape=[rows_ou...  255 us
    pallas_call x1, Pallas kernels, place_results(): pl.pallas_call(place_kernel, out_shape=[jax.ShapeDtypeStruct(r.shape, BF)...  12.1 us

profile of v4, /device:TPU:0, one launch (start us, length us, event | category | flops | bytes accessed | tf_op | source)
XLA Modules:
  0.0 268.3 jit_solution(13031780018787391483)
XLA Ops:
  0.6 255.3 %shard_map.185 = (bf16[256,768]{1,0:T(8,128)(2,1)}, bf16[256,768]{1,0:T(8,128)(2,1)}, bf16[256,768]{1,0:T(8,128)(2,1)}, bf16[256,768]{1,0:T(8,128)(2,1)}, bf16[6...) custom-call(bf16[1024,768]{1,0:T(8,128)(2,1)} %inputs_ref.1, ...), custom_call_target="tpu_custom_call" | custom-call | tf_op jit(solution)/shard_map/pallas_call | solution.py:943
  256.0 12.1 %shard_map.186 = (bf16[256,768]{1,0:T(8,128)(2,1)}, bf16[256,768]{1,0:T(8,128)(2,1)}, bf16[256,768]{1,0:T(8,128)(2,1)}, bf16[256,768]{1,0:T(8,128)(2,1)}, f32[38...) custom-call(bf16[32,384,384]{2,1,0:T(8,128)(2,1)} %get-tuple-element, ...), custom_call_target="tpu_custom_call" | custom-call | tf_op jit(solution)/shard_map/pallas_call | solution.py:1026

commit v5 on v4

--- a/solution.py
+++ b/solution.py
@@ -343,10 +343,15 @@
             total[...] = branch
         post_norm(r, attended, total[...], 1, scaled_second, out)
 
-    def feed_back(m, grad):
+    def feed_norm_back(m, grad):
         r = micro_rows(m)
         through = norm_back(r, grad, 1, scaled_second)
         branch_second[r] = through.astype(BF)
+        total[...] = through
+
+    def feed_back(m):
+        r = micro_rows(m)
+        through = total[...]
         for k in range(CHUNKS):
             hidden_grad = dot_right(branch_second[r], down_w[chunk(k)])
             gate_grad = (hidden_grad * slope[r, chunk(k)].astype(F32)).astype(BF)
@@ -434,6 +439,57 @@
     def _():
         remote(out.at[front], swapped, swap_send, swap_recv, peer).start()
 
+    def pairs(n, height):
+        tile = tile_of(n)
+        row = jnp.where(tile < 4, lax.rem(tile, 2) * D, tile * PIECE)
+        return pl.ds(pl.multiple_of(row, PIECE), height)
+
+    def half_tile(n, which):
+        return staged.at[lax.rem(n, 2), pl.ds(pl.multiple_of(which * PIECE, PIECE), PIECE)]
+
+    def keep(n, source, height):
+        return pltpu.make_async_copy(source, mine_out.at[pairs(n, height)], keep_sem.at[lax.rem(n, 2)])
+
+    def give(n, source, height):
+        unit = jnp.where(n < 4, lax.rem(tile_of(n), 2), n - 2)
+        return remote(source, landed_out.at[pairs(n, height)], give_send.at[lax.rem(n, 2)], give_recv.at[unit], partner)
+
+    def wide(k):
+        return pl.ds(pl.multiple_of(k * D, D), D)
+
+    def tile_of(n):
+        return n + (n == 1).astype(jnp.int32) - (n == 2).astype(jnp.int32)
+
+    def each_part(n, kept, given):
+        tile = tile_of(n)
+
+        @pl.when((tile < 4) & (lax.div(tile, 2) == core))
+        def _():
+            kept(keep(n, staged.at[lax.rem(n, 2)], D))
+
+        @pl.when((tile < 4) & (lax.div(tile, 2) != core))
+        def _():
+            given(give(n, staged.at[lax.rem(n, 2)], D))
+
+        @pl.when(tile >= 4)
+        def _():
+            kept(keep(n, half_tile(n, core), PIECE))
+            given(give(n, half_tile(n, 1 - core), PIECE))
+
+    def finish(n):
+        each_part(n, lambda copy: copy.wait(), lambda copy: copy.wait_send())
+
+    def launch(n, value):
+        staged[lax.rem(n, 2)] = value.astype(BF)
+        each_part(n, lambda copy: copy.start(), lambda copy: copy.start())
+
+    def down_tile(n):
+        launch(n, dot_left(hidden[:, wide(tile_of(n))], branch_second[...]))
+
+    def first_tiles():
+        down_tile(jnp.int32(0))
+        down_tile(jnp.int32(1))
+
     @pl.when(plane == 1)
     def _():
         for copy in token_loads():
@@ -451,7 +507,13 @@
         def _():
             upstream[r] = (columns[r, :1] * upstream[r].astype(F32)).astype(BF)
 
-        feed_back(m, upstream[r].astype(F32))
+        feed_norm_back(m, upstream[r].astype(F32))
+
+        @pl.when((plane == 0) & (m == MICRO - 1))
+        def _():
+            first_tiles()
+
+        feed_back(m)
 
         @pl.when((plane == 1) | (m < MICRO - 1))
         def _():
@@ -465,53 +527,6 @@
         attend_back(MICRO - 1, total[...].astype(BF).astype(F32))
         remote(back.at[rear], swapped, swap_send, swap_recv, peer).start()
 
-    def pairs(n, height):
-        tile = tile_of(n)
-        row = jnp.where(tile < 4, lax.rem(tile, 2) * D, tile * PIECE)
-        return pl.ds(pl.multiple_of(row, PIECE), height)
-
-    def half_tile(n, which):
-        return staged.at[lax.rem(n, 2), pl.ds(pl.multiple_of(which * PIECE, PIECE), PIECE)]
-
-    def keep(n, source, height):
-        return pltpu.make_async_copy(source, mine_out.at[pairs(n, height)], keep_sem.at[lax.rem(n, 2)])
-
-    def give(n, source, height):
-        unit = jnp.where(n < 4, lax.rem(tile_of(n), 2), n - 2)
-        return remote(source, landed_out.at[pairs(n, height)], give_send.at[lax.rem(n, 2)], give_recv.at[unit], partner)
-
-    def wide(k):
-        return pl.ds(pl.multiple_of(k * D, D), D)
-
-    def tile_of(n):
-        return n + (n == 1).astype(jnp.int32) - (n == 2).astype(jnp.int32)
-
-    def each_part(n, kept, given):
-        tile = tile_of(n)
-
-        @pl.when((tile < 4) & (lax.div(tile, 2) == core))
-        def _():
-            kept(keep(n, staged.at[lax.rem(n, 2)], D))
-
-        @pl.when((tile < 4) & (lax.div(tile, 2) != core))
-        def _():
-            given(give(n, staged.at[lax.rem(n, 2)], D))
-
-        @pl.when(tile >= 4)
-        def _():
-            kept(keep(n, half_tile(n, core), PIECE))
-            given(give(n, half_tile(n, 1 - core), PIECE))
-
-    def finish(n):
-        each_part(n, lambda copy: copy.wait(), lambda copy: copy.wait_send())
-
-    def launch(n, value):
-        staged[lax.rem(n, 2)] = value.astype(BF)
-        each_part(n, lambda copy: copy.start(), lambda copy: copy.start())
-
-    def down_tile(n):
-        launch(n, dot_left(hidden[:, wide(tile_of(n))], branch_second[...]))
-
     def task(i):
         n = i + 3
 
@@ -544,12 +559,13 @@
             finish(n - 2)
 
     signal_near(ready_sem)
-    down_first = [jnp.int32(n) for n in range(3)]
-    down_tile(down_first[0])
-    down_tile(down_first[1])
-    finish(down_first[0])
-    down_tile(down_first[2])
-    finish(down_first[1])
+    @pl.when(plane == 1)
+    def _():
+        first_tiles()
+
+    finish(jnp.int32(0))
+    down_tile(jnp.int32(2))
+    finish(jnp.int32(1))
     half = lines // 2
     mid = half - 1
     lower = z < half
@@ -637,10 +653,6 @@
             settled(sums(b, 2 * SIDE, RAIL), high_send.at[slot(b)])
 
     def load(b):
-        @pl.when(b >= RING)
-        def _():
-            release_grown(b - RING)
-
         @pl.when((b < 8) & (lax.rem(b, 4) == 0))
         def _():
             settled(landed_out.at[pl.ds(0, D)], give_recv.at[lax.div(b, 4)])
@@ -710,6 +722,33 @@
                 remote(small.at[4], small.at[4], small_send.at[3], small_recv.at[4], outward).start()
 
             remote(small.at[4], small_in.at[4], small_send.at[4], small_recv.at[5], peer).start()
+
+    def writes(which):
+        pairs = [
+            [(out.at[front], first_out), (swapped, second_out), (back.at[front], input_out), (upstream.at[front], middle_out)],
+            [(rows.at[rear], first_out), (out.at[rear], second_out), (swapped, input_out), (back.at[rear], middle_out)],
+        ][which]
+        return [pltpu.make_async_copy(a, b, out_sem.at[n]) for n, (a, b) in enumerate(pairs)]
+
+    def small_writes():
+        pairs = ((small.at[4], small_out), (small_in.at[4], other_out))
+        return [pltpu.make_async_copy(a, b, out_sem.at[4 + n]) for n, (a, b) in enumerate(pairs)]
+
+    def output_step(i):
+        @pl.when(i == 20)
+        def _():
+            remote(out.at[front], swapped, swap_send, swap_recv, peer).wait_recv()
+            for which in range(2):
+                @pl.when(plane == which)
+                def _(which=which):
+                    for copy in writes(which):
+                        copy.start()
+
+        @pl.when(i == 24 + 4 * mid)
+        def _():
+            small_finish()
+            for copy in small_writes():
+                copy.start()
 
     def small_finish():
         settled(small_in.at[4], small_recv.at[5])
@@ -724,6 +763,7 @@
 
     def step(i, carry):
         small_step(i)
+        output_step(i)
 
         b1 = piece_at(i - LAG * (1 + depth))
 
@@ -834,6 +874,12 @@
                     def _():
                         remote(part, part, high_send.at[slot(c2)], root_recv.at[slot(c2)], above).start()
 
+        b6 = piece_at(i - LAG * (2 * lines - 2))
+
+        @when(True, b6)
+        def _():
+            release_grown(b6)
+
         b4 = piece_at(i - LAG * (2 * lines - 1))
 
         @when(True, b4)
@@ -878,34 +924,14 @@
     lax.fori_loop(0, AHEAD + 1, first_load, 0)
     pl.semaphore_wait(ready_sem, near)
     lax.fori_loop(0, PIECES + pause + LAG * (2 * lines - 1), step, 0)
-    small_finish()
-
     def release_last(b, carry):
-        release_grown(b)
         release_sums(b)
         return carry
 
     lax.fori_loop(PIECES - RING, PIECES, release_last, 0)
 
-    remote(out.at[front], swapped, swap_send, swap_recv, peer).wait_recv()
-
-    def writes(which):
-        pairs = [
-            [(out.at[front], first_out), (swapped, second_out), (back.at[front], input_out), (upstream.at[front], middle_out)],
-            [(rows.at[rear], first_out), (out.at[rear], second_out), (swapped, input_out), (back.at[rear], middle_out)],
-        ][which]
-        return [pltpu.make_async_copy(a, b, out_sem.at[n]) for n, (a, b) in enumerate(pairs)]
-
-    for which in range(2):
-        @pl.when(plane == which)
-        def _(which=which):
-            for copy in writes(which):
-                copy.start()
-
-    for n, (source, target) in enumerate(((small.at[4], small_out), (small_in.at[4], other_out))):
-        small_copy = pltpu.make_async_copy(source, target, out_sem.at[4 + n])
-        small_copy.start()
-        small_copy.wait()
+    for copy in small_writes():
+        copy.wait()
 
     for which in range(2):
         @pl.when(plane == which)

time: 269 us -> 265 us (0.985)
  Pallas kernels: 267 us -> 264 us
    pallas_call x1, Pallas kernels: 255 us -> 252 us  [run_layer(): pl.pallas_call(functools.partial(layer_kernel, lines), out_shape=[rows_ou...]
where the time goes in v5:
time: 265 us
  Pallas kernels  264 us (100%)
    pallas_call x1, Pallas kernels, run_layer(): pl.pallas_call(functools.partial(layer_kernel, lines), out_shape=[rows_ou...  252 us
    pallas_call x1, Pallas kernels, place_results(): pl.pallas_call(place_kernel, out_shape=[jax.ShapeDtypeStruct(r.shape, BF)...  12.1 us

profile of v5, /device:TPU:0, one launch (start us, length us, event | category | flops | bytes accessed | tf_op | source)
XLA Modules:
  0.0 265.2 jit_solution(10306920710447799789)
XLA Ops:
  0.6 252.3 %shard_map.185 = (bf16[256,768]{1,0:T(8,128)(2,1)}, bf16[256,768]{1,0:T(8,128)(2,1)}, bf16[256,768]{1,0:T(8,128)(2,1)}, bf16[256,768]{1,0:T(8,128)(2,1)}, bf16[6...) custom-call(bf16[1024,768]{1,0:T(8,128)(2,1)} %inputs_ref.1, ...), custom_call_target="tpu_custom_call" | custom-call | tf_op jit(solution)/shard_map/pallas_call | solution.py:969
  252.9 12.1 %shard_map.186 = (bf16[256,768]{1,0:T(8,128)(2,1)}, bf16[256,768]{1,0:T(8,128)(2,1)}, bf16[256,768]{1,0:T(8,128)(2,1)}, bf16[256,768]{1,0:T(8,128)(2,1)}, f32[38...) custom-call(bf16[32,384,384]{2,1,0:T(8,128)(2,1)} %get-tuple-element, ...), custom_call_target="tpu_custom_call" | custom-call | tf_op jit(solution)/shard_map/pallas_call | solution.py:1052

commit v6 on v5

--- a/solution.py
+++ b/solution.py
@@ -23,8 +23,8 @@
 SMALL = 16
 PIECES = 32
 PIECE = 384
-SIDE = 128
-RAIL = 128
+SIDE = 112
+RAIL = 160
 WIDTH = 384
 AHEAD = 3
 LAG = 2
@@ -620,7 +620,7 @@
 
     def root_of(b):
         odd = lax.rem(b, 2)
-        return jnp.where(b < PIECES // 2, odd * (lines - 1), mid + odd)
+        return jnp.where(lax.rem(b, 4) < 2, odd * (lines - 1), mid + odd)
 
     def release_grown(b):
         root = root_of(b)

time: 265 us -> 265 us (level)
  no operation moved by 1% of the time
where the time goes in v6:
time: 265 us; the launch traced here: 264 us
  Pallas kernels  263 us (99%)
    pallas_call x1, Pallas kernels, run_layer(): pl.pallas_call(functools.partial(layer_kernel, lines), out_shape=[rows_ou...  251 us
    pallas_call x1, Pallas kernels, place_results(): pl.pallas_call(place_kernel, out_shape=[jax.ShapeDtypeStruct(r.shape, BF)...  12.1 us

profile of v6, /device:TPU:0, one launch (start us, length us, event | category | flops | bytes accessed | tf_op | source)
XLA Modules:
  0.0 264.2 jit_solution(13503375163261805366)
XLA Ops:
  0.6 251.3 %shard_map.185 = (bf16[256,768]{1,0:T(8,128)(2,1)}, bf16[256,768]{1,0:T(8,128)(2,1)}, bf16[256,768]{1,0:T(8,128)(2,1)}, bf16[256,768]{1,0:T(8,128)(2,1)}, bf16[6...) custom-call(bf16[1024,768]{1,0:T(8,128)(2,1)} %inputs_ref.1, ...), custom_call_target="tpu_custom_call" | custom-call | tf_op jit(solution)/shard_map/pallas_call | solution.py:969
  251.9 12.1 %shard_map.186 = (bf16[256,768]{1,0:T(8,128)(2,1)}, bf16[256,768]{1,0:T(8,128)(2,1)}, bf16[256,768]{1,0:T(8,128)(2,1)}, bf16[256,768]{1,0:T(8,128)(2,1)}, f32[38...) custom-call(bf16[32,384,384]{2,1,0:T(8,128)(2,1)} %get-tuple-element, ...), custom_call_target="tpu_custom_call" | custom-call | tf_op jit(solution)/shard_map/pallas_call | solution.py:1052
